TPU v7x, 1024 devices: a whole 4x8x16 slice. The times are simulated.
1024 devices in a mesh: dp: 64 (over z_lo, y, core), mp: 16 (over z_hi, x).
Axes of the slice: x: 4, y: 8, z: 16 (z_hi: 4, z_lo: 4; z = z_hi * 4 + z_lo), core: 2. Of those that a mesh axis runs over, the one named last changes fastest.
Arguments:
- tokens: bfloat16 [16384, 3072], P(('dp', 'mp')), parts along dimension 0, may hold values from -6 to 6
- ln_gain: float32 [3072], replicated, may hold values from 0.1 to 1.9
- w_in: bfloat16 [3072, 12288], P(None, 'mp'), may hold values from -0.109375 to 0.109375
- w_out: bfloat16 [12288, 3072], P('mp'), may hold values from -0.0546875 to 0.0546875
Outputs:
- mixed: bfloat16 [16384, 3072], P(('dp', 'mp')), parts along dimension 0
There are 64 independent parts, one for each index of `dp`. A program takes and returns all parts, laid end to end along the dimension named above; an argument that names none is the same for every part. Nothing has to cross between parts.
All inputs are finite; a program needn't handle non-finite values.
Results may differ from a plain program's by a relative error of at most 0.014.
Values may be sent and summed in bfloat16 or wider, within the bound.
No kernel may reach another device: no remote copies, remote signals or barrier semaphores. Data moves between devices by JAX's collectives and lax.ppermute only.
A program may use at most 32 MiB of HBM per device.

v0:
```python
import jax
import jax.numpy as jnp
from jax import lax
from jax.sharding import PartitionSpec as P


def normalize(tokens, ln_gain):
    values = tokens.astype(jnp.float32)
    center = jnp.mean(values, axis=1, keepdims=True)
    spread = jnp.mean((values - center) ** 2, axis=1, keepdims=True)
    return ((values - center) * lax.rsqrt(spread + 1e-06) * ln_gain).astype(jnp.bfloat16)


def activate(normed, w_in):
    linear = jnp.dot(normed, w_in, preferred_element_type=jnp.float32)
    return jax.nn.gelu(linear, approximate=False).astype(jnp.bfloat16)


def on_device(tokens, ln_gain, w_in, w_out):
    normed = normalize(tokens, ln_gain)
    gathered = lax.all_gather(normed, "mp", axis=0, tiled=True)
    hidden = activate(gathered, w_in)
    terms = jnp.dot(hidden, w_out, preferred_element_type=jnp.float32)
    summed = lax.psum_scatter(
        terms.astype(jnp.bfloat16), "mp", scatter_dimension=0, tiled=True
    ).astype(jnp.float32)
    return (tokens.astype(jnp.float32) + summed).astype(jnp.bfloat16)


def solution(mesh):
    placed = (P(("dp", "mp"), None), P(), P(None, "mp"), P("mp", None))
    return jax.shard_map(
        on_device, mesh=mesh, in_specs=placed, out_specs=P(("dp", "mp"), None), check_vma=False
    )
```

profile of v0, /device:TPU:1, one launch (start us, length us, event | category | flops | bytes accessed | tf_op | source)
XLA Modules:
  0.0 249.3 jit_solution(2562982342419656175)
XLA Ops:
  6.5 0.0 all-gather.2.cloned.1.call-start
  6.5 1.0 convert_reduce_fusion
  7.6 1.1 fusion.43
  8.7 1.6 fusion.45
  10.3 0.0 all-gather.2.cloned.1.call-update
  10.3 0.0 copy-start
  10.4 0.0 reduce-scatter.2.cloned.1.call-start
  10.4 101.2 %all-gather.2.cloned.1.call-done = bf16[256,3072]{1,0:T(8,128)(2,1)} async-done(((bf16[16,3072]{1,0:T(8,128)(2,1)}), bf16[256,3072]{1,0:T(8,128)(2,1)}) %all-gather.2.cloned.1.call-update) | async-done | bytes 1572880 | tf_op jit(solution)/shard_map/all_gather | solution.py:21
  111.6 10.3 %convolution_convert_fusion = bf16[256,3072]{1,0:T(8,128)(2,1)} fusion(bf16[768,3072]{1,0:T(8,128)(2,1)} %param.7, bf16[256,3072]{1,0:T(8,128)(2,1)} %all-gather.2.cloned.1.call-done, bf16[3072,768]{1,0:T(8,128)(2,1)} %param.6), kind=kOutput, calls=%fused_computation | convolution fusion | flops 2429485056 | bytes 12582912 | tf_op jit(solution)/shard_map/dot_general | solution.py:23
  121.9 0.0 reduce-scatter.2.cloned.1.call-update
  121.9 119.0 %reduce-scatter.2.cloned.1.call-done = bf16[16,3072]{1,0:T(8,128)(2,1)} async-done(((bf16[256,3072]{1,0:T(8,128)(2,1)}), bf16[16,3072]{1,0:T(8,128)(2,1)}) %reduce-scatter.2.cloned.1.call-update) | async-done | bytes 98320 | tf_op jit(solution)/shard_map/reduce_scatter | solution.py:24
  240.9 0.0 copy-done
  240.9 1.6 fusion.46
  (2 shorter events, 0.0 us)
Async XLA Ops:
  6.5 105.1 %all-gather.2.cloned.1.call-start = ((), (), s32[]{:S(2)}) async-start(), calls=%async_computation.1 | async-start | bytes 1671168 | tf_op jit(solution)/shard_map/all_gather | solution.py:21
  10.3 230.6 %copy-start = (bf16[16,3072]{1,0:T(8,128)(2,1)S(1)}, bf16[16,3072]{1,0:T(8,128)(2,1)}, u32[]{:S(2)}) copy-start(bf16[16,3072]{1,0:T(8,128)(2,1)} %param.4) | copy-start | bytes 294916
  10.4 230.5 %reduce-scatter.2.cloned.1.call-start = ((), (), s32[]{:S(2)}) async-start(), calls=%async_computation.2 | async-start | bytes 1671168 | tf_op jit(solution)/shard_map/reduce_scatter | solution.py:24
Sparse Core Ops, SparseCore 0:
  11.5 100.0 all-gather.1
  122.1 118.7 reduce-scatter.1
where the time goes:
time: 250 us; the launch traced here: 249 us
  waiting for transfers between devices  220 us (88%)
  between operations  13.4 us (5%)
  matrix products  10.3 us (4%)
  other arithmetic  5.34 us (2%)
    reduce_scatter x1, waiting for transfers between devices, on_device(): lax.psum_scatter(terms.astype(jnp.bfloat16), 'mp', scatter_dimension=0, t...  119 us
    all_gather x1, waiting for transfers between devices, on_device(): gathered = lax.all_gather(normed, 'mp', axis=0, tiled=True)  101 us
    dot_general x1, matrix products, on_device(): terms = jnp.dot(hidden, w_out, preferred_element_type=jnp.float32)  10.3 us
  transfers between devices with their start and end apart: 2, of which 2 were waited for; matrix products, arithmetic and copies ran while one was open for 0% of the time, Pallas kernels for 0%

commit v1 on v0

v1 whole, which is shorter than its diff:
```python
import functools

import jax
import jax.numpy as jnp
from jax import lax
from jax.experimental import pallas as pl
from jax.experimental.pallas import tpu as pltpu
from jax.sharding import PartitionSpec as P

SIDE = 4
GROUPS = ((0, 3, 1, 2),)
VMEM = pl.BlockSpec(memory_space=pltpu.VMEM)


def along_z(value, step):
    count = SIDE * SIDE
    return lax.ppermute(value, "mp", [(i, (i + SIDE * step) % count) for i in range(count)])


def along_x(value, step):
    pairs = [(i, i // SIDE * SIDE + (i + step) % SIDE) for i in range(SIDE * SIDE)]
    return lax.ppermute(value, "mp", pairs)


def call(body, outs, args, scratch=(), flops=0, limit=32):
    moved = sum(a.size * a.dtype.itemsize for a in args) + sum(
        o.size * jnp.dtype(o.dtype).itemsize for o in outs
    )
    return pl.pallas_call(
        body,
        out_shape=outs,
        in_specs=[VMEM] * len(args),
        out_specs=[VMEM] * len(outs),
        scratch_shapes=scratch,
        cost_estimate=pl.CostEstimate(flops=flops, bytes_accessed=moved, transcendentals=0),
        compiler_params=pltpu.CompilerParams(vmem_limit_bytes=limit * 2**20),
    )(*args)


def normalize_body(tokens, gain, out):
    values = tokens[...].astype(jnp.float32)
    center = jnp.mean(values, axis=1, keepdims=True)
    centered = values - center
    spread = jnp.mean(centered * centered, axis=1, keepdims=True)
    out[...] = (centered * lax.rsqrt(spread + 1e-06) * gain[...]).astype(jnp.bfloat16)


def feed_body(parts, *refs):
    rows, (w_in, w_out), outs, hidden = refs[:parts], refs[parts : parts + 2], refs[parts + 2 : -1], refs[-1]
    height = rows[0].shape[0]
    tile = 256

    @pl.loop(0, w_in.shape[1] // tile)
    def _(step):
        columns = pl.ds(pl.multiple_of(step * tile, tile), tile)
        block = jnp.concatenate([r[...] for r in rows], axis=0)
        linear = jnp.dot(block, w_in[:, columns], preferred_element_type=jnp.float32)
        active = linear * (0.5 * (1.0 + lax.erf(linear * (0.5**0.5))))
        hidden[:, columns] = active.astype(jnp.bfloat16)

    @pl.loop(0, w_out.shape[1] // tile)
    def _(step):
        columns = pl.ds(pl.multiple_of(step * tile, tile), tile)
        terms = jnp.dot(hidden[...], w_out[:, columns], preferred_element_type=jnp.float32)
        for index, out in enumerate(outs):
            out[:, columns] = terms[index * height : (index + 1) * height].astype(jnp.bfloat16)


def feed(rows, w_in, w_out):
    height, width = rows[0].shape
    total, units = height * len(rows), w_in.shape[1]
    return call(
        functools.partial(feed_body, len(rows)),
        [jax.ShapeDtypeStruct(r.shape, jnp.bfloat16) for r in rows],
        (*rows, w_in, w_out),
        scratch=[pltpu.VMEM((total, units), jnp.bfloat16)],
        flops=4 * total * units * width,
    )


def sum_body(count, *refs):
    total = refs[0][...].astype(jnp.float32)
    for ref in refs[1:count]:
        total = total + ref[...].astype(jnp.float32)
    height = refs[count].shape[0]
    for index, out in enumerate(refs[count:]):
        out[...] = total[index * height : (index + 1) * height].astype(jnp.bfloat16)


def add(terms, pieces):
    shape = (terms[0].shape[0] // pieces, terms[0].shape[1])
    outs = [jax.ShapeDtypeStruct(shape, jnp.bfloat16)] * pieces
    return call(functools.partial(sum_body, len(terms)), outs, terms)


def on_device(tokens, ln_gain, w_in, w_out):
    (normed,) = call(
        normalize_body, [jax.ShapeDtypeStruct(tokens.shape, jnp.bfloat16)], (tokens, ln_gain[None, :])
    )
    arrived = {step: along_z(normed, step) if step else normed for group in GROUPS for step in group}
    back = [tokens]
    for group in GROUPS:
        block = jnp.concatenate([arrived[step] for step in group], axis=0)
        rows = [block] + [along_x(block, step) for step in (1, 3, 2)]
        terms = feed(rows, w_in, w_out)
        summands = [terms[0]] + [along_x(term, -step) for term, step in zip(terms[1:], (1, 3, 2))]
        pieces = add(summands, len(group))
        back += [along_z(piece, -step) if step else piece for piece, step in zip(pieces, group)]
    return add(back, 1)[0]


def solution(mesh):
    placed = (P(("dp", "mp"), None), P(), P(None, "mp"), P("mp", None))
    return jax.shard_map(
        on_device, mesh=mesh, in_specs=placed, out_specs=P(("dp", "mp"), None), check_vma=False
    )
```

time: 250 us -> 128 us (0.51)
  the two profiles are of different devices: /device:TPU:1 before, /device:TPU:96 now
where the time goes in v1:
time: 128 us
  starting transfers between devices  70.3 us (55%)
  waiting for transfers between devices  44.6 us (35%)
  Pallas kernels  6.33 us (5%)
  local copies, waits for them, and re-layouts  6.28 us (5%)
    ppermute x6, starting transfers between devices, along_z(): lax.ppermute(value, 'mp', [(i, (i + SIDE * step) % count) for i in range(...  50.5 us
    ppermute x6, waiting for transfers between devices, along_z(): lax.ppermute(value, 'mp', [(i, (i + SIDE * step) % count) for i in range(...  23.8 us
    ppermute x6, waiting for transfers between devices, along_x(): return lax.ppermute(value, 'mp', pairs)  20.8 us
    ppermute x6, starting transfers between devices, along_x(): return lax.ppermute(value, 'mp', pairs)  19.8 us
    pallas_call x4, Pallas kernels, call(): pl.pallas_call(body, out_shape=outs, in_specs=[VMEM] * len(args), out_spe...  6.33 us
    unnamed x10, local copies, waits for them, and re-layouts  6.28 us
  transfers between devices with their start and end apart: 12, of which 8 were waited for; matrix products, arithmetic and copies ran while one was open for 0% of the time, Pallas kernels for 0%

profile of v1, /device:TPU:96, one launch (start us, length us, event | category | flops | bytes accessed | tf_op | source)
XLA Modules:
  0.0 127.7 jit_solution(17923282653430810796)
XLA Ops:
  0.0 0.0 copy-start.2
  0.0 0.9 copy-done.2
  0.9 0.0 copy-start.4
  0.9 0.7 copy-done.4
  1.6 0.2 shard_map.46
  1.8 18.5 %collective-permute-start.2 = (bf16[16,3072]{1,0:T(8,128)(2,1)S(1)}, bf16[16,3072]{1,0:T(8,128)(2,1)S(1)}, u32[]{:S(2)}, u32[]{:S(2)}) collective-permute-start(bf16[16,3072]{1,0:T(8,128)(2,1)S(1)} %shard_map.46), channel_id=1, source_target_pairs={{0,8},{1,9},{2,10},{3,11},{4,12},{5,13},{6,14},{7,15},{8,0},{9,1},... | collective-permute-start | bytes 294920 | tf_op jit(solution)/shard_map/ppermute | solution.py:17
  20.3 6.1 %collective-permute-start.1 = (bf16[16,3072]{1,0:T(8,128)(2,1)S(1)}, bf16[16,3072]{1,0:T(8,128)(2,1)S(1)}, u32[]{:S(2)}, u32[]{:S(2)}) collective-permute-start(bf16[16,3072]{1,0:T(8,128)(2,1)S(1)} %shard_map.46), channel_id=1, source_target_pairs={{0,4},{1,5},{2,6},{3,7},{4,8},{5,9},{6,10},{7,11},{8,12},{9,13},{1... | collective-permute-start | bytes 294920 | tf_op jit(solution)/shard_map/ppermute | solution.py:17
  26.4 3.6 %collective-permute-start = (bf16[16,3072]{1,0:T(8,128)(2,1)S(1)}, bf16[16,3072]{1,0:T(8,128)(2,1)S(1)}, u32[]{:S(2)}, u32[]{:S(2)}) collective-permute-start(bf16[16,3072]{1,0:T(8,128)(2,1)S(1)} %shard_map.46), channel_id=1, source_target_pairs={{0,12},{1,13},{2,14},{3,15},{4,0},{5,1},{6,2},{7,3},{8,4},{9,5},{1... | collective-permute-start | bytes 294920 | tf_op jit(solution)/shard_map/ppermute | solution.py:17
  30.1 0.0 collective-permute-done.2
  30.1 2.6 %collective-permute-done.1 = bf16[16,3072]{1,0:T(8,128)(2,1)S(1)} collective-permute-done((bf16[16,3072]{1,0:T(8,128)(2,1)S(1)}, bf16[16,3072]{1,0:T(8,128)(2,1)S(1)}, u32[]{:S(2)}, u32[]{:S(2)}) %collective-permute-start.1) | collective-permute-done | bytes 98336 | tf_op jit(solution)/shard_map/ppermute | solution.py:17
  32.7 9.1 %collective-permute-done = bf16[16,3072]{1,0:T(8,128)(2,1)S(1)} collective-permute-done((bf16[16,3072]{1,0:T(8,128)(2,1)S(1)}, bf16[16,3072]{1,0:T(8,128)(2,1)S(1)}, u32[]{:S(2)}, u32[]{:S(2)}) %collective-permute-start) | collective-permute-done | bytes 98336 | tf_op jit(solution)/shard_map/ppermute | solution.py:17
  41.8 0.0 copy-start.3
  41.8 5.1 %collective-permute-start.5 = (bf16[64,3072]{1,0:T(8,128)(2,1)S(1)}, bf16[64,3072]{1,0:T(8,128)(2,1)S(1)}, u32[]{:S(2)}, u32[]{:S(2)}) collective-permute-start(bf16[64,3072]{1,0:T(8,128)(2,1)S(1)} %pad_maximum_fusion.refs_0_), channel_id=1, source_target_pairs={{0,2},{1,3},{2,0},{3,1},{4,6},{5,7},{6,4},{7,5},{8,10},{9,11},{10,... | collective-permute-start | bytes 1179656 | tf_op jit(solution)/shard_map/ppermute | solution.py:22
  46.9 3.0 %collective-permute-start.4 = (bf16[64,3072]{1,0:T(8,128)(2,1)S(1)}, bf16[64,3072]{1,0:T(8,128)(2,1)S(1)}, u32[]{:S(2)}, u32[]{:S(2)}) collective-permute-start(bf16[64,3072]{1,0:T(8,128)(2,1)S(1)} %pad_maximum_fusion.refs_0_), channel_id=1, source_target_pairs={{0,3},{1,0},{2,1},{3,2},{4,7},{5,4},{6,5},{7,6},{8,11},{9,8},{10,9... | collective-permute-start | bytes 1179656 | tf_op jit(solution)/shard_map/ppermute | solution.py:22
  49.9 2.8 %collective-permute-start.3 = (bf16[64,3072]{1,0:T(8,128)(2,1)S(1)}, bf16[64,3072]{1,0:T(8,128)(2,1)S(1)}, u32[]{:S(2)}, u32[]{:S(2)}) collective-permute-start(bf16[64,3072]{1,0:T(8,128)(2,1)S(1)} %pad_maximum_fusion.refs_0_), channel_id=1, source_target_pairs={{0,1},{1,2},{2,3},{3,0},{4,5},{5,6},{6,7},{7,4},{8,9},{9,10},{10,1... | collective-permute-start | bytes 1179656 | tf_op jit(solution)/shard_map/ppermute | solution.py:22
  52.7 3.2 %collective-permute-done.5.refs_3_ = bf16[64,3072]{1,0:T(8,128)(2,1)S(1)} collective-permute-done((bf16[64,3072]{1,0:T(8,128)(2,1)S(1)}, bf16[64,3072]{1,0:T(8,128)(2,1)S(1)}, u32[]{:S(2)}, u32[]{:S(2)}) %collective-permute-start.5) | collective-permute-done | bytes 393248 | tf_op jit(solution)/shard_map/ppermute | solution.py:22
  56.0 2.7 %collective-permute-done.4.refs_2_ = bf16[64,3072]{1,0:T(8,128)(2,1)S(1)} collective-permute-done((bf16[64,3072]{1,0:T(8,128)(2,1)S(1)}, bf16[64,3072]{1,0:T(8,128)(2,1)S(1)}, u32[]{:S(2)}, u32[]{:S(2)}) %collective-permute-start.4) | collective-permute-done | bytes 393248 | tf_op jit(solution)/shard_map/ppermute | solution.py:22
  58.7 2.8 %collective-permute-done.3.refs_1_ = bf16[64,3072]{1,0:T(8,128)(2,1)S(1)} collective-permute-done((bf16[64,3072]{1,0:T(8,128)(2,1)S(1)}, bf16[64,3072]{1,0:T(8,128)(2,1)S(1)}, u32[]{:S(2)}, u32[]{:S(2)}) %collective-permute-start.3) | collective-permute-done | bytes 393248 | tf_op jit(solution)/shard_map/ppermute | solution.py:22
  61.5 0.0 copy-start
  61.5 2.3 %copy-done = bf16[3072,768]{1,0:T(8,128)(2,1)S(1)} copy-done((bf16[3072,768]{1,0:T(8,128)(2,1)S(1)}, bf16[3072,768]{1,0:T(8,128)(2,1)}, u32[]{:S(2)}) %copy-start) | copy-done | bytes 4718616
  63.8 0.0 copy-start.1
  63.8 2.3 %copy-done.1 = bf16[768,3072]{1,0:T(8,128)(2,1)S(1)} copy-done((bf16[768,3072]{1,0:T(8,128)(2,1)S(1)}, bf16[768,3072]{1,0:T(8,128)(2,1)}, u32[]{:S(2)}) %copy-start.1) | copy-done | bytes 4718616
  66.2 5.2 %shard_map.47 = (bf16[64,3072]{1,0:T(8,128)(2,1)S(1)}, bf16[64,3072]{1,0:T(8,128)(2,1)S(1)}, bf16[64,3072]{1,0:T(8,128)(2,1)S(1)}, bf16[64,3072]{1,0:T(8,128)(2,1)S(1)}) custom-call(bf16[64,3072]{1,0:T(8,128)(2,1)S(1)} %pad_maximum_fusion.refs_0_, bf16[64,3072]{1,0:T(8,128)(2,1)S(1)} %collective-permute-done.3.refs_1_, ...), custom_call_target="tpu_custom_call" | custom-call | flops 2415919104 | bytes 12582912 | tf_op jit(solution)/shard_map/pallas_call | solution.py:29
  71.4 1.9 %collective-permute-start.6 = (bf16[64,3072]{1,0:T(8,128)(2,1)S(1)}, bf16[64,3072]{1,0:T(8,128)(2,1)S(1)}, u32[]{:S(2)}, u32[]{:S(2)}) collective-permute-start(bf16[64,3072]{1,0:T(8,128)(2,1)S(1)} %get-tuple-element.14), channel_id=1, source_target_pairs={{0,3},{1,0},{2,1},{3,2},{4,7},{5,4},{6,5},{7,6},{8,11},{9,8},{10,9... | collective-permute-start | bytes 1179656 | tf_op jit(solution)/shard_map/ppermute | solution.py:22
  73.3 3.9 %collective-permute-start.7 = (bf16[64,3072]{1,0:T(8,128)(2,1)S(1)}, bf16[64,3072]{1,0:T(8,128)(2,1)S(1)}, u32[]{:S(2)}, u32[]{:S(2)}) collective-permute-start(bf16[64,3072]{1,0:T(8,128)(2,1)S(1)} %get-tuple-element.15), channel_id=1, source_target_pairs={{0,1},{1,2},{2,3},{3,0},{4,5},{5,6},{6,7},{7,4},{8,9},{9,10},{10,1... | collective-permute-start | bytes 1179656 | tf_op jit(solution)/shard_map/ppermute | solution.py:22
  77.2 3.1 %collective-permute-start.8 = (bf16[64,3072]{1,0:T(8,128)(2,1)S(1)}, bf16[64,3072]{1,0:T(8,128)(2,1)S(1)}, u32[]{:S(2)}, u32[]{:S(2)}) collective-permute-start(bf16[64,3072]{1,0:T(8,128)(2,1)S(1)} %get-tuple-element.16), channel_id=1, source_target_pairs={{0,2},{1,3},{2,0},{3,1},{4,6},{5,7},{6,4},{7,5},{8,10},{9,11},{10,... | collective-permute-start | bytes 1179656 | tf_op jit(solution)/shard_map/ppermute | solution.py:22
  80.3 3.8 %collective-permute-done.6.refs_1_ = bf16[64,3072]{1,0:T(8,128)(2,1)S(1)} collective-permute-done((bf16[64,3072]{1,0:T(8,128)(2,1)S(1)}, bf16[64,3072]{1,0:T(8,128)(2,1)S(1)}, u32[]{:S(2)}, u32[]{:S(2)}) %collective-permute-start.6) | collective-permute-done | bytes 393248 | tf_op jit(solution)/shard_map/ppermute | solution.py:22
  84.1 8.3 %collective-permute-done.7.refs_2_ = bf16[64,3072]{1,0:T(8,128)(2,1)S(1)} collective-permute-done((bf16[64,3072]{1,0:T(8,128)(2,1)S(1)}, bf16[64,3072]{1,0:T(8,128)(2,1)S(1)}, u32[]{:S(2)}, u32[]{:S(2)}) %collective-permute-start.7) | collective-permute-done | bytes 393248 | tf_op jit(solution)/shard_map/ppermute | solution.py:22
  92.3 0.0 collective-permute-done.8.refs_3_
  92.3 0.2 shard_map.48
  92.5 5.2 %collective-permute-start.9 = (bf16[16,3072]{1,0:T(8,128)(2,1)S(1)}, bf16[16,3072]{1,0:T(8,128)(2,1)S(1)}, u32[]{:S(2)}, u32[]{:S(2)}) collective-permute-start(bf16[16,3072]{1,0:T(8,128)(2,1)S(1)} %get-tuple-element.18), channel_id=1, source_target_pairs={{0,4},{1,5},{2,6},{3,7},{4,8},{5,9},{6,10},{7,11},{8,12},{9,13},{1... | collective-permute-start | bytes 294920 | tf_op jit(solution)/shard_map/ppermute | solution.py:17
  97.7 6.0 %collective-permute-start.10 = (bf16[16,3072]{1,0:T(8,128)(2,1)S(1)}, bf16[16,3072]{1,0:T(8,128)(2,1)S(1)}, u32[]{:S(2)}, u32[]{:S(2)}) collective-permute-start(bf16[16,3072]{1,0:T(8,128)(2,1)S(1)} %get-tuple-element.19), channel_id=1, source_target_pairs={{0,12},{1,13},{2,14},{3,15},{4,0},{5,1},{6,2},{7,3},{8,4},{9,5},{1... | collective-permute-start | bytes 294920 | tf_op jit(solution)/shard_map/ppermute | solution.py:17
  103.7 11.1 %collective-permute-start.11 = (bf16[16,3072]{1,0:T(8,128)(2,1)S(1)}, bf16[16,3072]{1,0:T(8,128)(2,1)S(1)}, u32[]{:S(2)}, u32[]{:S(2)}) collective-permute-start(bf16[16,3072]{1,0:T(8,128)(2,1)S(1)} %get-tuple-element.20), channel_id=1, source_target_pairs={{0,8},{1,9},{2,10},{3,11},{4,12},{5,13},{6,14},{7,15},{8,0},{9,1},... | collective-permute-start | bytes 294920 | tf_op jit(solution)/shard_map/ppermute | solution.py:17
  114.8 0.0 collective-permute-done.9.refs_2_
  114.8 0.0 collective-permute-done.10.refs_3_
  114.8 12.1 %collective-permute-done.11.refs_4_ = bf16[16,3072]{1,0:T(8,128)(2,1)S(1)} collective-permute-done((bf16[16,3072]{1,0:T(8,128)(2,1)S(1)}, bf16[16,3072]{1,0:T(8,128)(2,1)S(1)}, u32[]{:S(2)}, u32[]{:S(2)}) %collective-permute-start.11) | collective-permute-done | bytes 98336 | tf_op jit(solution)/shard_map/ppermute | solution.py:17
  127.0 0.0 copy-done.3
  127.0 0.7 shard_map.49
  (1 shorter events, 0.0 us)
Async XLA Ops:
  0.0 0.9 copy-start.2
  0.9 0.7 copy-start.4
  1.8 28.2 %collective-permute-start.2 = (bf16[16,3072]{1,0:T(8,128)(2,1)S(1)}, bf16[16,3072]{1,0:T(8,128)(2,1)S(1)}, u32[]{:S(2)}, u32[]{:S(2)}) collective-permute-start(bf16[16,3072]{1,0:T(8,128)(2,1)S(1)} %shard_map.46), channel_id=1, source_target_pairs={{0,8},{1,9},{2,10},{3,11},{4,12},{5,13},{6,14},{7,15},{8,0},{9,1},... | collective-permute-start | bytes 294920 | tf_op jit(solution)/shard_map/ppermute | solution.py:17
  20.3 12.4 %collective-permute-start.1 = (bf16[16,3072]{1,0:T(8,128)(2,1)S(1)}, bf16[16,3072]{1,0:T(8,128)(2,1)S(1)}, u32[]{:S(2)}, u32[]{:S(2)}) collective-permute-start(bf16[16,3072]{1,0:T(8,128)(2,1)S(1)} %shard_map.46), channel_id=1, source_target_pairs={{0,4},{1,5},{2,6},{3,7},{4,8},{5,9},{6,10},{7,11},{8,12},{9,13},{1... | collective-permute-start | bytes 294920 | tf_op jit(solution)/shard_map/ppermute | solution.py:17
  26.4 15.3 %collective-permute-start = (bf16[16,3072]{1,0:T(8,128)(2,1)S(1)}, bf16[16,3072]{1,0:T(8,128)(2,1)S(1)}, u32[]{:S(2)}, u32[]{:S(2)}) collective-permute-start(bf16[16,3072]{1,0:T(8,128)(2,1)S(1)} %shard_map.46), channel_id=1, source_target_pairs={{0,12},{1,13},{2,14},{3,15},{4,0},{5,1},{6,2},{7,3},{8,4},{9,5},{1... | collective-permute-start | bytes 294920 | tf_op jit(solution)/shard_map/ppermute | solution.py:17
  41.8 85.2 %copy-start.3 = (bf16[16,3072]{1,0:T(8,128)(2,1)S(1)}, bf16[16,3072]{1,0:T(8,128)(2,1)}, u32[]{:S(2)}) copy-start(bf16[16,3072]{1,0:T(8,128)(2,1)} %refs_0_.1) | copy-start | bytes 294916
  41.8 14.1 %collective-permute-start.5 = (bf16[64,3072]{1,0:T(8,128)(2,1)S(1)}, bf16[64,3072]{1,0:T(8,128)(2,1)S(1)}, u32[]{:S(2)}, u32[]{:S(2)}) collective-permute-start(bf16[64,3072]{1,0:T(8,128)(2,1)S(1)} %pad_maximum_fusion.refs_0_), channel_id=1, source_target_pairs={{0,2},{1,3},{2,0},{3,1},{4,6},{5,7},{6,4},{7,5},{8,10},{9,11},{10,... | collective-permute-start | bytes 1179656 | tf_op jit(solution)/shard_map/ppermute | solution.py:22
  46.9 11.8 %collective-permute-start.4 = (bf16[64,3072]{1,0:T(8,128)(2,1)S(1)}, bf16[64,3072]{1,0:T(8,128)(2,1)S(1)}, u32[]{:S(2)}, u32[]{:S(2)}) collective-permute-start(bf16[64,3072]{1,0:T(8,128)(2,1)S(1)} %pad_maximum_fusion.refs_0_), channel_id=1, source_target_pairs={{0,3},{1,0},{2,1},{3,2},{4,7},{5,4},{6,5},{7,6},{8,11},{9,8},{10,9... | collective-permute-start | bytes 1179656 | tf_op jit(solution)/shard_map/ppermute | solution.py:22
  49.9 11.5 %collective-permute-start.3 = (bf16[64,3072]{1,0:T(8,128)(2,1)S(1)}, bf16[64,3072]{1,0:T(8,128)(2,1)S(1)}, u32[]{:S(2)}, u32[]{:S(2)}) collective-permute-start(bf16[64,3072]{1,0:T(8,128)(2,1)S(1)} %pad_maximum_fusion.refs_0_), channel_id=1, source_target_pairs={{0,1},{1,2},{2,3},{3,0},{4,5},{5,6},{6,7},{7,4},{8,9},{9,10},{10,1... | collective-permute-start | bytes 1179656 | tf_op jit(solution)/shard_map/ppermute | solution.py:22
  61.5 2.3 %copy-start = (bf16[3072,768]{1,0:T(8,128)(2,1)S(1)}, bf16[3072,768]{1,0:T(8,128)(2,1)}, u32[]{:S(2)}) copy-start(bf16[3072,768]{1,0:T(8,128)(2,1)} %refs_4_.1) | copy-start | bytes 14155780
  63.8 2.3 %copy-start.1 = (bf16[768,3072]{1,0:T(8,128)(2,1)S(1)}, bf16[768,3072]{1,0:T(8,128)(2,1)}, u32[]{:S(2)}) copy-start(bf16[768,3072]{1,0:T(8,128)(2,1)} %refs_5_.1) | copy-start | bytes 14155780
  71.4 12.7 %collective-permute-start.6 = (bf16[64,3072]{1,0:T(8,128)(2,1)S(1)}, bf16[64,3072]{1,0:T(8,128)(2,1)S(1)}, u32[]{:S(2)}, u32[]{:S(2)}) collective-permute-start(bf16[64,3072]{1,0:T(8,128)(2,1)S(1)} %get-tuple-element.14), channel_id=1, source_target_pairs={{0,3},{1,0},{2,1},{3,2},{4,7},{5,4},{6,5},{7,6},{8,11},{9,8},{10,9... | collective-permute-start | bytes 1179656 | tf_op jit(solution)/shard_map/ppermute | solution.py:22
  73.3 19.0 %collective-permute-start.7 = (bf16[64,3072]{1,0:T(8,128)(2,1)S(1)}, bf16[64,3072]{1,0:T(8,128)(2,1)S(1)}, u32[]{:S(2)}, u32[]{:S(2)}) collective-permute-start(bf16[64,3072]{1,0:T(8,128)(2,1)S(1)} %get-tuple-element.15), channel_id=1, source_target_pairs={{0,1},{1,2},{2,3},{3,0},{4,5},{5,6},{6,7},{7,4},{8,9},{9,10},{10,1... | collective-permute-start | bytes 1179656 | tf_op jit(solution)/shard_map/ppermute | solution.py:22
  77.2 15.1 %collective-permute-start.8 = (bf16[64,3072]{1,0:T(8,128)(2,1)S(1)}, bf16[64,3072]{1,0:T(8,128)(2,1)S(1)}, u32[]{:S(2)}, u32[]{:S(2)}) collective-permute-start(bf16[64,3072]{1,0:T(8,128)(2,1)S(1)} %get-tuple-element.16), channel_id=1, source_target_pairs={{0,2},{1,3},{2,0},{3,1},{4,6},{5,7},{6,4},{7,5},{8,10},{9,11},{10,... | collective-permute-start | bytes 1179656 | tf_op jit(solution)/shard_map/ppermute | solution.py:22
  92.5 22.3 %collective-permute-start.9 = (bf16[16,3072]{1,0:T(8,128)(2,1)S(1)}, bf16[16,3072]{1,0:T(8,128)(2,1)S(1)}, u32[]{:S(2)}, u32[]{:S(2)}) collective-permute-start(bf16[16,3072]{1,0:T(8,128)(2,1)S(1)} %get-tuple-element.18), channel_id=1, source_target_pairs={{0,4},{1,5},{2,6},{3,7},{4,8},{5,9},{6,10},{7,11},{8,12},{9,13},{1... | collective-permute-start | bytes 294920 | tf_op jit(solution)/shard_map/ppermute | solution.py:17
  97.7 17.1 %collective-permute-start.10 = (bf16[16,3072]{1,0:T(8,128)(2,1)S(1)}, bf16[16,3072]{1,0:T(8,128)(2,1)S(1)}, u32[]{:S(2)}, u32[]{:S(2)}) collective-permute-start(bf16[16,3072]{1,0:T(8,128)(2,1)S(1)} %get-tuple-element.19), channel_id=1, source_target_pairs={{0,12},{1,13},{2,14},{3,15},{4,0},{5,1},{6,2},{7,3},{8,4},{9,5},{1... | collective-permute-start | bytes 294920 | tf_op jit(solution)/shard_map/ppermute | solution.py:17
  103.7 23.2 %collective-permute-start.11 = (bf16[16,3072]{1,0:T(8,128)(2,1)S(1)}, bf16[16,3072]{1,0:T(8,128)(2,1)S(1)}, u32[]{:S(2)}, u32[]{:S(2)}) collective-permute-start(bf16[16,3072]{1,0:T(8,128)(2,1)S(1)} %get-tuple-element.20), channel_id=1, source_target_pairs={{0,8},{1,9},{2,10},{3,11},{4,12},{5,13},{6,14},{7,15},{8,0},{9,1},... | collective-permute-start | bytes 294920 | tf_op jit(solution)/shard_map/ppermute | solution.py:17

commit v2 on v1

v2 whole, which is shorter than its diff:
```python
import functools

import jax
import jax.numpy as jnp
from jax import lax
from jax.experimental import pallas as pl
from jax.experimental.pallas import tpu as pltpu
from jax.sharding import PartitionSpec as P

SIDE = 4
VMEM = pl.BlockSpec(memory_space=pltpu.VMEM)
AFTER = pl.BlockSpec(memory_space=pl.ANY)


def trade(value, shape, axis, turn):
    dp, mp = shape
    pairs = []
    for batch in range(dp):
        flip = 1 if batch % 2 == turn else SIDE - 1
        for spot in range(mp):
            z, x = divmod(spot, SIDE)
            z, x = (z ^ flip, x) if axis == 0 else (z, x ^ flip)
            pairs.append((batch * mp + spot, batch * mp + z * SIDE + x))
    return lax.ppermute(value, ("dp", "mp"), pairs)


def call(body, outs, args, specs=None, scratch=(), flops=0, limit=16):
    moved = sum(a.size * a.dtype.itemsize for a in args) + sum(
        o.size * jnp.dtype(o.dtype).itemsize for o in outs
    )
    return pl.pallas_call(
        body,
        out_shape=outs,
        in_specs=specs or [VMEM] * len(args),
        out_specs=[VMEM] * len(outs),
        scratch_shapes=scratch,
        cost_estimate=pl.CostEstimate(flops=flops, bytes_accessed=moved, transcendentals=0),
        compiler_params=pltpu.CompilerParams(vmem_limit_bytes=limit * 2**20),
    )(*args)


def normalize_body(tokens, gain, out):
    values = tokens[...].astype(jnp.float32)
    center = jnp.mean(values, axis=1, keepdims=True)
    centered = values - center
    spread = jnp.mean(centered * centered, axis=1, keepdims=True)
    out[...] = (centered * lax.rsqrt(spread + 1e-06) * gain[...]).astype(jnp.bfloat16)


def ready_body(w_in, w_out, after, out):
    out[...] = w_in[:8, :128] + w_out[:8, :128]


def ready(w_in, w_out, after):
    outs = [jax.ShapeDtypeStruct((8, 128), jnp.bfloat16)]
    return call(ready_body, outs, (w_in, w_out, after), specs=[VMEM, VMEM, AFTER])[0]


def feed_body(parts, *refs):
    rows, (w_in, w_out), outs, hidden = refs[:parts], refs[parts : parts + 2], refs[parts + 3 : -1], refs[-1]
    height = rows[0].shape[0]
    tile = 256

    @pl.loop(0, w_in.shape[1] // tile)
    def _(step):
        columns = pl.ds(pl.multiple_of(step * tile, tile), tile)
        block = jnp.concatenate([r[...] for r in rows], axis=0)
        linear = jnp.dot(block, w_in[:, columns], preferred_element_type=jnp.float32)
        active = linear * (0.5 * (1.0 + lax.erf(linear * (0.5**0.5))))
        hidden[:, columns] = active.astype(jnp.bfloat16)

    @pl.loop(0, w_out.shape[1] // tile)
    def _(step):
        columns = pl.ds(pl.multiple_of(step * tile, tile), tile)
        terms = jnp.dot(hidden[...], w_out[:, columns], preferred_element_type=jnp.float32)
        for index, out in enumerate(outs):
            out[:, columns] = terms[index * height : (index + 1) * height].astype(jnp.bfloat16)


def feed(rows, w_in, w_out, after):
    height, width = rows[0].shape
    total, units = height * len(rows), w_in.shape[1]
    return call(
        functools.partial(feed_body, len(rows)),
        [jax.ShapeDtypeStruct(r.shape, jnp.bfloat16) for r in rows],
        (*rows, w_in, w_out, after),
        specs=[VMEM] * (len(rows) + 2) + [AFTER],
        scratch=[pltpu.VMEM((total, units), jnp.bfloat16)],
        flops=4 * total * units * width,
    )


def sum_body(count, *refs):
    total = refs[0][...].astype(jnp.float32)
    for ref in refs[1:count]:
        total = total + ref[...].astype(jnp.float32)
    height = refs[count].shape[0]
    for index, out in enumerate(refs[count:]):
        out[...] = total[index * height : (index + 1) * height].astype(jnp.bfloat16)


def add(terms, pieces=1):
    shape = (terms[0].shape[0] // pieces, terms[0].shape[1])
    outs = [jax.ShapeDtypeStruct(shape, jnp.bfloat16)] * pieces
    return call(functools.partial(sum_body, len(terms)), outs, terms)


def stack_body(*refs):
    height = refs[0].shape[0]
    for index, ref in enumerate(refs[:-2]):
        refs[-1][pl.ds(index * height, height), :] = ref[...]


def stack(parts, after):
    shape = (sum(p.shape[0] for p in parts), parts[0].shape[1])
    outs = [jax.ShapeDtypeStruct(shape, jnp.bfloat16)]
    return call(stack_body, outs, (*parts, after), specs=[VMEM] * len(parts) + [AFTER])[0]


def on_device(shape, tokens, ln_gain, w_in, w_out):
    along_z = functools.partial(trade, shape=shape, axis=0)
    along_x = functools.partial(trade, shape=shape, axis=1)
    (own,) = call(
        normalize_body, [jax.ShapeDtypeStruct(tokens.shape, jnp.bfloat16)], (tokens, ln_gain[None, :])
    )
    held = ready(w_in, w_out, own)
    pair = stack([own, along_z(own, turn=0)], held)
    four = stack([pair, along_z(pair, turn=1)], held)
    kept = stack([four, along_x(four, turn=0)], held)
    sent = along_x(kept, turn=1)
    (kept,) = feed([kept], w_in, w_out, kept)
    (sent,) = feed([sent], w_in, w_out, kept)
    kept, sent = add([kept, along_x(sent, turn=1)], 2)
    kept, sent = add([kept, along_x(sent, turn=0)], 2)
    kept, sent = add([kept, along_z(sent, turn=1)], 2)
    return add([tokens, kept, along_z(sent, turn=0)])[0]


def solution(mesh):
    placed = (P(("dp", "mp"), None), P(), P(None, "mp"), P("mp", None))
    body = functools.partial(on_device, (mesh.shape["dp"], mesh.shape["mp"]))
    return jax.shard_map(
        body, mesh=mesh, in_specs=placed, out_specs=P(("dp", "mp"), None), check_vma=False
    )
```

time: 128 us -> 131 us (1.023)
  the two profiles are of different devices: /device:TPU:96 before, /device:TPU:6 now
where the time goes in v2:
time: 131 us; the launch traced here: 130 us
  waiting for transfers between devices  62.7 us (48%)
  starting transfers between devices  51.9 us (40%)
  Pallas kernels  9.17 us (7%)
  local copies, waits for them, and re-layouts  6.28 us (5%)
    ppermute x8, waiting for transfers between devices, trade(): return lax.ppermute(value, ('dp', 'mp'), pairs)  62.7 us
    ppermute x8, starting transfers between devices, trade(): return lax.ppermute(value, ('dp', 'mp'), pairs)  51.9 us
    pallas_call x11, Pallas kernels, call(): pl.pallas_call(body, out_shape=outs, in_specs=specs or [VMEM] * len(args)...  9.17 us
    unnamed x14, local copies, waits for them, and re-layouts  6.28 us
  transfers between devices with their start and end apart: 8, of which 7 were waited for; matrix products, arithmetic and copies ran while one was open for 0% of the time, Pallas kernels for 3%

profile of v2, /device:TPU:6, one launch (start us, length us, event | category | flops | bytes accessed | tf_op | source)
XLA Modules:
  0.0 130.2 jit_solution(8743592640932539787)
XLA Ops:
  0.0 0.0 copy-start.4
  0.0 0.9 copy-done.4
  0.9 0.0 copy-start.6
  0.9 0.7 copy-done.6
  1.6 0.2 shard_map.46.after.refs_0_
  1.8 10.9 %collective-permute-start = (bf16[16,3072]{1,0:T(8,128)(2,1)S(1)}, bf16[16,3072]{1,0:T(8,128)(2,1)S(1)}, u32[]{:S(2)}, u32[]{:S(2)}) collective-permute-start(bf16[16,3072]{1,0:T(8,128)(2,1)S(1)} %shard_map.46.after.refs_0_), channel_id=1, source_target_pairs={{0,4},{1,5},{2,6},{3,7},{4,0},{5,1},{6,2},{7,3},{8,12},{9,13},{10,... | collective-permute-start | bytes 294920 | tf_op jit(solution)/shard_map/ppermute | solution.py:24
  12.8 0.0 copy-start
  12.8 2.3 %copy-done = bf16[3072,768]{1,0:T(8,128)(2,1)S(1)} copy-done((bf16[3072,768]{1,0:T(8,128)(2,1)S(1)}, bf16[3072,768]{1,0:T(8,128)(2,1)}, u32[]{:S(2)}) %copy-start) | copy-done | bytes 4718616
  15.1 0.0 copy-start.2
  15.1 2.3 %copy-done.2 = bf16[768,3072]{1,0:T(8,128)(2,1)S(1)} copy-done((bf16[768,3072]{1,0:T(8,128)(2,1)S(1)}, bf16[768,3072]{1,0:T(8,128)(2,1)}, u32[]{:S(2)}) %copy-start.2) | copy-done | bytes 4718616
  17.4 0.0 copy-start.1
  17.4 0.0 copy-start.3
  17.5 0.0 collective-permute-done.refs_1_
  17.5 14.8 %collective-permute-start.1 = (bf16[32,3072]{1,0:T(8,128)(2,1)S(1)}, bf16[32,3072]{1,0:T(8,128)(2,1)S(1)}, u32[]{:S(2)}, u32[]{:S(2)}) collective-permute-start(bf16[32,3072]{1,0:T(8,128)(2,1)S(1)} %shard_map.48.refs_0_), channel_id=1, source_target_pairs={{0,12},{1,13},{2,14},{3,15},{4,8},{5,9},{6,10},{7,11},{8,4},{9,5},... | collective-permute-start | bytes 589832 | tf_op jit(solution)/shard_map/ppermute | solution.py:24
  32.3 7.1 %collective-permute-done.1.refs_1_ = bf16[32,3072]{1,0:T(8,128)(2,1)S(1)} collective-permute-done((bf16[32,3072]{1,0:T(8,128)(2,1)S(1)}, bf16[32,3072]{1,0:T(8,128)(2,1)S(1)}, u32[]{:S(2)}, u32[]{:S(2)}) %collective-permute-start.1) | collective-permute-done | bytes 196640 | tf_op jit(solution)/shard_map/ppermute | solution.py:24
  39.4 2.7 %collective-permute-start.2 = (bf16[64,3072]{1,0:T(8,128)(2,1)S(1)}, bf16[64,3072]{1,0:T(8,128)(2,1)S(1)}, u32[]{:S(2)}, u32[]{:S(2)}) collective-permute-start(bf16[64,3072]{1,0:T(8,128)(2,1)S(1)} %shard_map.49.refs_0_), channel_id=1, source_target_pairs={{0,1},{1,0},{2,3},{3,2},{4,5},{5,4},{6,7},{7,6},{8,9},{9,8},{10,11... | collective-permute-start | bytes 1179656 | tf_op jit(solution)/shard_map/ppermute | solution.py:24
  42.2 6.9 %collective-permute-done.2.refs_1_ = bf16[64,3072]{1,0:T(8,128)(2,1)S(1)} collective-permute-done((bf16[64,3072]{1,0:T(8,128)(2,1)S(1)}, bf16[64,3072]{1,0:T(8,128)(2,1)S(1)}, u32[]{:S(2)}, u32[]{:S(2)}) %collective-permute-start.2) | collective-permute-done | bytes 393248 | tf_op jit(solution)/shard_map/ppermute | solution.py:24
  49.1 0.1 shard_map.50.refs_0_.refs_3_
  49.2 1.9 %collective-permute-start.3 = (bf16[128,3072]{1,0:T(8,128)(2,1)S(1)}, bf16[128,3072]{1,0:T(8,128)(2,1)S(1)}, u32[]{:S(2)}, u32[]{:S(2)}) collective-permute-start(bf16[128,3072]{1,0:T(8,128)(2,1)S(1)} %shard_map.50.refs_0_.refs_3_), channel_id=1, source_target_pairs={{0,3},{1,2},{2,1},{3,0},{4,7},{5,6},{6,5},{7,4},{8,11},{9,10},{10,... | collective-permute-start | bytes 2359304 | tf_op jit(solution)/shard_map/ppermute | solution.py:24
  51.1 0.0 copy-done.1
  51.1 0.0 copy-done.3
  51.1 3.9 %shard_map.51.refs_3_.refs_0_ = bf16[128,3072]{1,0:T(8,128)(2,1)S(1)} custom-call(bf16[128,3072]{1,0:T(8,128)(2,1)S(1)} %shard_map.50.refs_0_.refs_3_, bf16[3072,768]{1,0:T(8,128)(2,1)S(1)} %copy-done.1, bf16[768,3072]{1,0:T(8,128)(2,1)S(1)} %copy-done.3, bf16[128,3072]{1,0:T(8,128)(2,1)S(1)} %shard_map.50.refs_0_.refs_3_), custom_call_target="tpu_custom_call" | custom-call | flops 1207959552 | bytes 11796480 | tf_op jit(solution)/shard_map/pallas_call | solution.py:31
  55.0 0.0 copy-start.5
  55.0 9.2 %collective-permute-done.3.refs_0_ = bf16[128,3072]{1,0:T(8,128)(2,1)S(1)} collective-permute-done((bf16[128,3072]{1,0:T(8,128)(2,1)S(1)}, bf16[128,3072]{1,0:T(8,128)(2,1)S(1)}, u32[]{:S(2)}, u32[]{:S(2)}) %collective-permute-start.3) | collective-permute-done | bytes 786464 | tf_op jit(solution)/shard_map/ppermute | solution.py:24
  64.3 3.9 %shard_map.52 = bf16[128,3072]{1,0:T(8,128)(2,1)S(1)} custom-call(bf16[128,3072]{1,0:T(8,128)(2,1)S(1)} %collective-permute-done.3.refs_0_, bf16[3072,768]{1,0:T(8,128)(2,1)S(1)} %copy-done.1, bf16[768,3072]{1,0:T(8,128)(2,1)S(1)} %copy-done.3, bf16[128,3072]{1,0:T(8,128)(2,1)S(1)} %shard_map.51.refs_3_.refs_0_), custom_call_target="tpu_custom_call" | custom-call | flops 1207959552 | bytes 11796480 | tf_op jit(solution)/shard_map/pallas_call | solution.py:31
  68.2 1.9 %collective-permute-start.4 = (bf16[128,3072]{1,0:T(8,128)(2,1)S(1)}, bf16[128,3072]{1,0:T(8,128)(2,1)S(1)}, u32[]{:S(2)}, u32[]{:S(2)}) collective-permute-start(bf16[128,3072]{1,0:T(8,128)(2,1)S(1)} %shard_map.52), channel_id=1, source_target_pairs={{0,3},{1,2},{2,1},{3,0},{4,7},{5,6},{6,5},{7,4},{8,11},{9,10},{10,... | collective-permute-start | bytes 2359304 | tf_op jit(solution)/shard_map/ppermute | solution.py:24
  70.1 13.2 %collective-permute-done.4.refs_1_ = bf16[128,3072]{1,0:T(8,128)(2,1)S(1)} collective-permute-done((bf16[128,3072]{1,0:T(8,128)(2,1)S(1)}, bf16[128,3072]{1,0:T(8,128)(2,1)S(1)}, u32[]{:S(2)}, u32[]{:S(2)}) %collective-permute-start.4) | collective-permute-done | bytes 786464 | tf_op jit(solution)/shard_map/ppermute | solution.py:24
  83.3 0.2 shard_map.53
  83.5 1.9 %collective-permute-start.5 = (bf16[64,3072]{1,0:T(8,128)(2,1)S(1)}, bf16[64,3072]{1,0:T(8,128)(2,1)S(1)}, u32[]{:S(2)}, u32[]{:S(2)}) collective-permute-start(bf16[64,3072]{1,0:T(8,128)(2,1)S(1)} %get-tuple-element.12), channel_id=1, source_target_pairs={{0,1},{1,0},{2,3},{3,2},{4,5},{5,4},{6,7},{7,6},{8,9},{9,8},{10,11... | collective-permute-start | bytes 1179656 | tf_op jit(solution)/shard_map/ppermute | solution.py:24
  85.4 7.7 %collective-permute-done.5.refs_1_ = bf16[64,3072]{1,0:T(8,128)(2,1)S(1)} collective-permute-done((bf16[64,3072]{1,0:T(8,128)(2,1)S(1)}, bf16[64,3072]{1,0:T(8,128)(2,1)S(1)}, u32[]{:S(2)}, u32[]{:S(2)}) %collective-permute-start.5) | collective-permute-done | bytes 393248 | tf_op jit(solution)/shard_map/ppermute | solution.py:24
  93.1 0.1 shard_map.54
  93.2 4.5 %collective-permute-start.6 = (bf16[32,3072]{1,0:T(8,128)(2,1)S(1)}, bf16[32,3072]{1,0:T(8,128)(2,1)S(1)}, u32[]{:S(2)}, u32[]{:S(2)}) collective-permute-start(bf16[32,3072]{1,0:T(8,128)(2,1)S(1)} %get-tuple-element.14), channel_id=1, source_target_pairs={{0,12},{1,13},{2,14},{3,15},{4,8},{5,9},{6,10},{7,11},{8,4},{9,5},... | collective-permute-start | bytes 589832 | tf_op jit(solution)/shard_map/ppermute | solution.py:24
  97.7 13.8 %collective-permute-done.6.refs_1_ = bf16[32,3072]{1,0:T(8,128)(2,1)S(1)} collective-permute-done((bf16[32,3072]{1,0:T(8,128)(2,1)S(1)}, bf16[32,3072]{1,0:T(8,128)(2,1)S(1)}, u32[]{:S(2)}, u32[]{:S(2)}) %collective-permute-start.6) | collective-permute-done | bytes 196640 | tf_op jit(solution)/shard_map/ppermute | solution.py:24
  111.6 13.2 %collective-permute-start.7 = (bf16[16,3072]{1,0:T(8,128)(2,1)S(1)}, bf16[16,3072]{1,0:T(8,128)(2,1)S(1)}, u32[]{:S(2)}, u32[]{:S(2)}) collective-permute-start(bf16[16,3072]{1,0:T(8,128)(2,1)S(1)} %get-tuple-element.16), channel_id=1, source_target_pairs={{0,4},{1,5},{2,6},{3,7},{4,0},{5,1},{6,2},{7,3},{8,12},{9,13},{10,... | collective-permute-start | bytes 294920 | tf_op jit(solution)/shard_map/ppermute | solution.py:24
  124.8 4.7 %collective-permute-done.7.refs_2_ = bf16[16,3072]{1,0:T(8,128)(2,1)S(1)} collective-permute-done((bf16[16,3072]{1,0:T(8,128)(2,1)S(1)}, bf16[16,3072]{1,0:T(8,128)(2,1)S(1)}, u32[]{:S(2)}, u32[]{:S(2)}) %collective-permute-start.7) | collective-permute-done | bytes 98336 | tf_op jit(solution)/shard_map/ppermute | solution.py:24
  129.5 0.0 copy-done.5
  129.5 0.7 shard_map.56
  (4 shorter events, 0.1 us)
Async XLA Ops:
  0.0 0.9 copy-start.4
  0.9 0.7 copy-start.6
  1.8 15.6 %collective-permute-start = (bf16[16,3072]{1,0:T(8,128)(2,1)S(1)}, bf16[16,3072]{1,0:T(8,128)(2,1)S(1)}, u32[]{:S(2)}, u32[]{:S(2)}) collective-permute-start(bf16[16,3072]{1,0:T(8,128)(2,1)S(1)} %shard_map.46.after.refs_0_), channel_id=1, source_target_pairs={{0,4},{1,5},{2,6},{3,7},{4,0},{5,1},{6,2},{7,3},{8,12},{9,13},{10,... | collective-permute-start | bytes 294920 | tf_op jit(solution)/shard_map/ppermute | solution.py:24
  12.8 2.3 %copy-start = (bf16[3072,768]{1,0:T(8,128)(2,1)S(1)}, bf16[3072,768]{1,0:T(8,128)(2,1)}, u32[]{:S(2)}) copy-start(bf16[3072,768]{1,0:T(8,128)(2,1)} %refs_1_.3) | copy-start | bytes 14155780
  15.1 2.3 %copy-start.2 = (bf16[768,3072]{1,0:T(8,128)(2,1)S(1)}, bf16[768,3072]{1,0:T(8,128)(2,1)}, u32[]{:S(2)}) copy-start(bf16[768,3072]{1,0:T(8,128)(2,1)} %refs_2_.3) | copy-start | bytes 14155780
  17.4 33.6 %copy-start.1 = (bf16[3072,768]{1,0:T(8,128)(2,1)S(1)}, bf16[3072,768]{1,0:T(8,128)(2,1)}, u32[]{:S(2)}) copy-start(bf16[3072,768]{1,0:T(8,128)(2,1)} %refs_1_.3) | copy-start | bytes 14155780
  17.4 33.7 %copy-start.3 = (bf16[768,3072]{1,0:T(8,128)(2,1)S(1)}, bf16[768,3072]{1,0:T(8,128)(2,1)}, u32[]{:S(2)}) copy-start(bf16[768,3072]{1,0:T(8,128)(2,1)} %refs_2_.3) | copy-start | bytes 14155780
  17.5 21.9 %collective-permute-start.1 = (bf16[32,3072]{1,0:T(8,128)(2,1)S(1)}, bf16[32,3072]{1,0:T(8,128)(2,1)S(1)}, u32[]{:S(2)}, u32[]{:S(2)}) collective-permute-start(bf16[32,3072]{1,0:T(8,128)(2,1)S(1)} %shard_map.48.refs_0_), channel_id=1, source_target_pairs={{0,12},{1,13},{2,14},{3,15},{4,8},{5,9},{6,10},{7,11},{8,4},{9,5},... | collective-permute-start | bytes 589832 | tf_op jit(solution)/shard_map/ppermute | solution.py:24
  39.4 9.7 %collective-permute-start.2 = (bf16[64,3072]{1,0:T(8,128)(2,1)S(1)}, bf16[64,3072]{1,0:T(8,128)(2,1)S(1)}, u32[]{:S(2)}, u32[]{:S(2)}) collective-permute-start(bf16[64,3072]{1,0:T(8,128)(2,1)S(1)} %shard_map.49.refs_0_), channel_id=1, source_target_pairs={{0,1},{1,0},{2,3},{3,2},{4,5},{5,4},{6,7},{7,6},{8,9},{9,8},{10,11... | collective-permute-start | bytes 1179656 | tf_op jit(solution)/shard_map/ppermute | solution.py:24
  49.2 15.1 %collective-permute-start.3 = (bf16[128,3072]{1,0:T(8,128)(2,1)S(1)}, bf16[128,3072]{1,0:T(8,128)(2,1)S(1)}, u32[]{:S(2)}, u32[]{:S(2)}) collective-permute-start(bf16[128,3072]{1,0:T(8,128)(2,1)S(1)} %shard_map.50.refs_0_.refs_3_), channel_id=1, source_target_pairs={{0,3},{1,2},{2,1},{3,0},{4,7},{5,6},{6,5},{7,4},{8,11},{9,10},{10,... | collective-permute-start | bytes 2359304 | tf_op jit(solution)/shard_map/ppermute | solution.py:24
  55.0 74.4 %copy-start.5 = (bf16[16,3072]{1,0:T(8,128)(2,1)S(1)}, bf16[16,3072]{1,0:T(8,128)(2,1)}, u32[]{:S(2)}) copy-start(bf16[16,3072]{1,0:T(8,128)(2,1)} %refs_0_.1) | copy-start | bytes 294916
  68.2 15.1 %collective-permute-start.4 = (bf16[128,3072]{1,0:T(8,128)(2,1)S(1)}, bf16[128,3072]{1,0:T(8,128)(2,1)S(1)}, u32[]{:S(2)}, u32[]{:S(2)}) collective-permute-start(bf16[128,3072]{1,0:T(8,128)(2,1)S(1)} %shard_map.52), channel_id=1, source_target_pairs={{0,3},{1,2},{2,1},{3,0},{4,7},{5,6},{6,5},{7,4},{8,11},{9,10},{10,... | collective-permute-start | bytes 2359304 | tf_op jit(solution)/shard_map/ppermute | solution.py:24
  83.5 9.7 %collective-permute-start.5 = (bf16[64,3072]{1,0:T(8,128)(2,1)S(1)}, bf16[64,3072]{1,0:T(8,128)(2,1)S(1)}, u32[]{:S(2)}, u32[]{:S(2)}) collective-permute-start(bf16[64,3072]{1,0:T(8,128)(2,1)S(1)} %get-tuple-element.12), channel_id=1, source_target_pairs={{0,1},{1,0},{2,3},{3,2},{4,5},{5,4},{6,7},{7,6},{8,9},{9,8},{10,11... | collective-permute-start | bytes 1179656 | tf_op jit(solution)/shard_map/ppermute | solution.py:24
  93.2 18.3 %collective-permute-start.6 = (bf16[32,3072]{1,0:T(8,128)(2,1)S(1)}, bf16[32,3072]{1,0:T(8,128)(2,1)S(1)}, u32[]{:S(2)}, u32[]{:S(2)}) collective-permute-start(bf16[32,3072]{1,0:T(8,128)(2,1)S(1)} %get-tuple-element.14), channel_id=1, source_target_pairs={{0,12},{1,13},{2,14},{3,15},{4,8},{5,9},{6,10},{7,11},{8,4},{9,5},... | collective-permute-start | bytes 589832 | tf_op jit(solution)/shard_map/ppermute | solution.py:24
  111.6 17.9 %collective-permute-start.7 = (bf16[16,3072]{1,0:T(8,128)(2,1)S(1)}, bf16[16,3072]{1,0:T(8,128)(2,1)S(1)}, u32[]{:S(2)}, u32[]{:S(2)}) collective-permute-start(bf16[16,3072]{1,0:T(8,128)(2,1)S(1)} %get-tuple-element.16), channel_id=1, source_target_pairs={{0,4},{1,5},{2,6},{3,7},{4,0},{5,1},{6,2},{7,3},{8,12},{9,13},{10,... | collective-permute-start | bytes 294920 | tf_op jit(solution)/shard_map/ppermute | solution.py:24

commit v3 on v2

--- a/solution.py
+++ b/solution.py
@@ -124,15 +124,24 @@
         normalize_body, [jax.ShapeDtypeStruct(tokens.shape, jnp.bfloat16)], (tokens, ln_gain[None, :])
     )
     held = ready(w_in, w_out, own)
+    def forth(block):
+        kept = stack([block, along_x(block, turn=0)], held)
+        return kept, along_x(kept, turn=1)
+
+    def back(kept, sent):
+        kept, sent = add([kept, along_x(sent, turn=1)], 2)
+        return kept, along_x(sent, turn=0)
+
     pair = stack([own, along_z(own, turn=0)], held)
-    four = stack([pair, along_z(pair, turn=1)], held)
-    kept = stack([four, along_x(four, turn=0)], held)
-    sent = along_x(kept, turn=1)
-    (kept,) = feed([kept], w_in, w_out, kept)
-    (sent,) = feed([sent], w_in, w_out, kept)
-    kept, sent = add([kept, along_x(sent, turn=1)], 2)
-    kept, sent = add([kept, along_x(sent, turn=0)], 2)
-    kept, sent = add([kept, along_z(sent, turn=1)], 2)
+    other = along_z(pair, turn=1)
+    pair_rows = forth(pair)
+    pair_terms = feed(pair_rows, w_in, w_out, held)
+    other_rows = forth(other)
+    other_terms = feed(other_rows, w_in, w_out, pair_terms[0])
+    (other,) = add(back(*other_terms))
+    arrived = along_z(other, turn=1)
+    pair_terms, _ = lax.optimization_barrier((pair_terms, other))
+    kept, sent = add([*back(*pair_terms), arrived], 2)
     return add([tokens, kept, along_z(sent, turn=0)])[0]
 
 

time: 131 us -> 125 us (0.954)
  the two profiles are of different devices: /device:TPU:6 before, /device:TPU:32 now
where the time goes in v3:
time: 125 us; the launch traced here: 124 us
  starting transfers between devices  72.9 us (58%)
  waiting for transfers between devices  35.7 us (29%)
  Pallas kernels  9.14 us (7%)
  local copies, waits for them, and re-layouts  6.28 us (5%)
    ppermute x12, starting transfers between devices, trade(): return lax.ppermute(value, ('dp', 'mp'), pairs)  72.9 us
    ppermute x12, waiting for transfers between devices, trade(): return lax.ppermute(value, ('dp', 'mp'), pairs)  35.7 us
    pallas_call x12, Pallas kernels, call(): pl.pallas_call(body, out_shape=outs, in_specs=specs or [VMEM] * len(args)...  9.14 us
    unnamed x14, local copies, waits for them, and re-layouts  6.28 us
  transfers between devices with their start and end apart: 12, of which 9 were waited for; matrix products, arithmetic and copies ran while one was open for 0% of the time, Pallas kernels for 3%

profile of v3, /device:TPU:32, one launch (start us, length us, event | category | flops | bytes accessed | tf_op | source)
XLA Modules:
  0.0 124.3 jit_solution(690062437897977216)
XLA Ops:
  0.0 0.0 copy-start.4
  0.0 0.9 copy-done.4
  0.9 0.0 copy-start.6
  0.9 0.7 copy-done.6
  1.6 0.2 shard_map.46.after.refs_0_
  1.8 10.9 %collective-permute-start = (bf16[16,3072]{1,0:T(8,128)(2,1)S(1)}, bf16[16,3072]{1,0:T(8,128)(2,1)S(1)}, u32[]{:S(2)}, u32[]{:S(2)}) collective-permute-start(bf16[16,3072]{1,0:T(8,128)(2,1)S(1)} %shard_map.46.after.refs_0_), channel_id=1, source_target_pairs={{0,4},{1,5},{2,6},{3,7},{4,0},{5,1},{6,2},{7,3},{8,12},{9,13},{10,... | collective-permute-start | bytes 294920 | tf_op jit(solution)/shard_map/ppermute | solution.py:24
  12.8 0.0 copy-start
  12.8 2.3 %copy-done = bf16[3072,768]{1,0:T(8,128)(2,1)S(1)} copy-done((bf16[3072,768]{1,0:T(8,128)(2,1)S(1)}, bf16[3072,768]{1,0:T(8,128)(2,1)}, u32[]{:S(2)}) %copy-start) | copy-done | bytes 4718616
  15.1 0.0 copy-start.2
  15.1 2.3 %copy-done.2 = bf16[768,3072]{1,0:T(8,128)(2,1)S(1)} copy-done((bf16[768,3072]{1,0:T(8,128)(2,1)S(1)}, bf16[768,3072]{1,0:T(8,128)(2,1)}, u32[]{:S(2)}) %copy-start.2) | copy-done | bytes 4718616
  17.4 0.0 copy-start.1
  17.4 0.0 copy-start.3
  17.5 0.0 collective-permute-done.refs_1_
  17.5 14.8 %collective-permute-start.3 = (bf16[32,3072]{1,0:T(8,128)(2,1)S(1)}, bf16[32,3072]{1,0:T(8,128)(2,1)S(1)}, u32[]{:S(2)}, u32[]{:S(2)}) collective-permute-start(bf16[32,3072]{1,0:T(8,128)(2,1)S(1)} %shard_map.48.refs_0_), channel_id=1, source_target_pairs={{0,12},{1,13},{2,14},{3,15},{4,8},{5,9},{6,10},{7,11},{8,4},{9,5},... | collective-permute-start | bytes 589832 | tf_op jit(solution)/shard_map/ppermute | solution.py:24
  32.3 3.4 %collective-permute-start.1 = (bf16[32,3072]{1,0:T(8,128)(2,1)S(1)}, bf16[32,3072]{1,0:T(8,128)(2,1)S(1)}, u32[]{:S(2)}, u32[]{:S(2)}) collective-permute-start(bf16[32,3072]{1,0:T(8,128)(2,1)S(1)} %shard_map.48.refs_0_), channel_id=1, source_target_pairs={{0,1},{1,0},{2,3},{3,2},{4,5},{5,4},{6,7},{7,6},{8,9},{9,8},{10,11... | collective-permute-start | bytes 589832 | tf_op jit(solution)/shard_map/ppermute | solution.py:24
  35.7 3.7 %collective-permute-done.3.refs_0_ = bf16[32,3072]{1,0:T(8,128)(2,1)S(1)} collective-permute-done((bf16[32,3072]{1,0:T(8,128)(2,1)S(1)}, bf16[32,3072]{1,0:T(8,128)(2,1)S(1)}, u32[]{:S(2)}, u32[]{:S(2)}) %collective-permute-start.3) | collective-permute-done | bytes 196640 | tf_op jit(solution)/shard_map/ppermute | solution.py:24
  39.4 3.4 %collective-permute-start.4 = (bf16[32,3072]{1,0:T(8,128)(2,1)S(1)}, bf16[32,3072]{1,0:T(8,128)(2,1)S(1)}, u32[]{:S(2)}, u32[]{:S(2)}) collective-permute-start(bf16[32,3072]{1,0:T(8,128)(2,1)S(1)} %collective-permute-done.3.refs_0_), channel_id=1, source_target_pairs={{0,1},{1,0},{2,3},{3,2},{4,5},{5,4},{6,7},{7,6},{8,9},{9,8},{10,11... | collective-permute-start | bytes 589832 | tf_op jit(solution)/shard_map/ppermute | solution.py:24
  42.8 0.0 collective-permute-done.1.refs_1_
  42.8 4.0 %collective-permute-start.2 = (bf16[64,3072]{1,0:T(8,128)(2,1)S(1)}, bf16[64,3072]{1,0:T(8,128)(2,1)S(1)}, u32[]{:S(2)}, u32[]{:S(2)}) collective-permute-start(bf16[64,3072]{1,0:T(8,128)(2,1)S(1)} %shard_map.49.refs_0_), channel_id=1, source_target_pairs={{0,3},{1,2},{2,1},{3,0},{4,7},{5,6},{6,5},{7,4},{8,11},{9,10},{10,... | collective-permute-start | bytes 1179656 | tf_op jit(solution)/shard_map/ppermute | solution.py:24
  46.9 0.4 collective-permute-done.4.refs_1_
  47.3 6.5 %collective-permute-start.5 = (bf16[64,3072]{1,0:T(8,128)(2,1)S(1)}, bf16[64,3072]{1,0:T(8,128)(2,1)S(1)}, u32[]{:S(2)}, u32[]{:S(2)}) collective-permute-start(bf16[64,3072]{1,0:T(8,128)(2,1)S(1)} %shard_map.51.refs_0_), channel_id=1, source_target_pairs={{0,3},{1,2},{2,1},{3,0},{4,7},{5,6},{6,5},{7,4},{8,11},{9,10},{10,... | collective-permute-start | bytes 1179656 | tf_op jit(solution)/shard_map/ppermute | solution.py:24
  53.8 0.0 collective-permute-done.2.refs_1_
  53.8 0.0 copy-done.1
  53.8 0.0 copy-done.3
  53.8 3.9 %shard_map.50 = (bf16[64,3072]{1,0:T(8,128)(2,1)S(1)}, bf16[64,3072]{1,0:T(8,128)(2,1)S(1)}) custom-call(bf16[64,3072]{1,0:T(8,128)(2,1)S(1)} %shard_map.49.refs_0_, bf16[64,3072]{1,0:T(8,128)(2,1)S(1)} %collective-permute-done.2.refs_1_, bf16[3072,768]{1,0:T(8,128)(2,1)S(1)} %copy-done.1, bf16[768,3072]{1,0:T(8,128)(2,1)S(1)} %copy-done.3, ...), custom_call_target="tpu_custom_call" | custom-call | flops 1207959552 | bytes 11012096 | tf_op jit(solution)/shard_map/pallas_call | solution.py:31
  57.7 1.8 %collective-permute-done.5.refs_1_ = bf16[64,3072]{1,0:T(8,128)(2,1)S(1)} collective-permute-done((bf16[64,3072]{1,0:T(8,128)(2,1)S(1)}, bf16[64,3072]{1,0:T(8,128)(2,1)S(1)}, u32[]{:S(2)}, u32[]{:S(2)}) %collective-permute-start.5) | collective-permute-done | bytes 393248 | tf_op jit(solution)/shard_map/ppermute | solution.py:24
  59.5 0.0 copy-start.5
  59.5 3.9 %shard_map.52 = (bf16[64,3072]{1,0:T(8,128)(2,1)S(1)}, bf16[64,3072]{1,0:T(8,128)(2,1)S(1)}) custom-call(bf16[64,3072]{1,0:T(8,128)(2,1)S(1)} %shard_map.51.refs_0_, bf16[64,3072]{1,0:T(8,128)(2,1)S(1)} %collective-permute-done.5.refs_1_, bf16[3072,768]{1,0:T(8,128)(2,1)S(1)} %copy-done.1, bf16[768,3072]{1,0:T(8,128)(2,1)S(1)} %copy-done.3, ...), custom_call_target="tpu_custom_call" | custom-call | flops 1207959552 | bytes 11403264 | tf_op jit(solution)/shard_map/pallas_call | solution.py:31
  63.4 5.1 %collective-permute-start.6 = (bf16[64,3072]{1,0:T(8,128)(2,1)S(1)}, bf16[64,3072]{1,0:T(8,128)(2,1)S(1)}, u32[]{:S(2)}, u32[]{:S(2)}) collective-permute-start(bf16[64,3072]{1,0:T(8,128)(2,1)S(1)} %get-tuple-element.20), channel_id=1, source_target_pairs={{0,3},{1,2},{2,1},{3,0},{4,7},{5,6},{6,5},{7,4},{8,11},{9,10},{10,... | collective-permute-start | bytes 1179656 | tf_op jit(solution)/shard_map/ppermute | solution.py:24
  68.6 6.8 %collective-permute-done.6.refs_1_ = bf16[64,3072]{1,0:T(8,128)(2,1)S(1)} collective-permute-done((bf16[64,3072]{1,0:T(8,128)(2,1)S(1)}, bf16[64,3072]{1,0:T(8,128)(2,1)S(1)}, u32[]{:S(2)}, u32[]{:S(2)}) %collective-permute-start.6) | collective-permute-done | bytes 393248 | tf_op jit(solution)/shard_map/ppermute | solution.py:24
  75.3 0.1 shard_map.53
  75.4 1.9 %collective-permute-start.7 = (bf16[32,3072]{1,0:T(8,128)(2,1)S(1)}, bf16[32,3072]{1,0:T(8,128)(2,1)S(1)}, u32[]{:S(2)}, u32[]{:S(2)}) collective-permute-start(bf16[32,3072]{1,0:T(8,128)(2,1)S(1)} %get-tuple-element.22), channel_id=1, source_target_pairs={{0,1},{1,0},{2,3},{3,2},{4,5},{5,4},{6,7},{7,6},{8,9},{9,8},{10,11... | collective-permute-start | bytes 589832 | tf_op jit(solution)/shard_map/ppermute | solution.py:24
  77.4 7.7 %collective-permute-done.7.refs_1_ = bf16[32,3072]{1,0:T(8,128)(2,1)S(1)} collective-permute-done((bf16[32,3072]{1,0:T(8,128)(2,1)S(1)}, bf16[32,3072]{1,0:T(8,128)(2,1)S(1)}, u32[]{:S(2)}, u32[]{:S(2)}) %collective-permute-start.7) | collective-permute-done | bytes 196640 | tf_op jit(solution)/shard_map/ppermute | solution.py:24
  85.2 5.6 %collective-permute-start.8 = (bf16[64,3072]{1,0:T(8,128)(2,1)S(1)}, bf16[64,3072]{1,0:T(8,128)(2,1)S(1)}, u32[]{:S(2)}, u32[]{:S(2)}) collective-permute-start(bf16[64,3072]{1,0:T(8,128)(2,1)S(1)} %get-tuple-element.24), channel_id=1, source_target_pairs={{0,3},{1,2},{2,1},{3,0},{4,7},{5,6},{6,5},{7,4},{8,11},{9,10},{10,... | collective-permute-start | bytes 1179656 | tf_op jit(solution)/shard_map/ppermute | solution.py:24
  90.7 2.8 %collective-permute-start.10 = (bf16[32,3072]{1,0:T(8,128)(2,1)S(1)}, bf16[32,3072]{1,0:T(8,128)(2,1)S(1)}, u32[]{:S(2)}, u32[]{:S(2)}) collective-permute-start(bf16[32,3072]{1,0:T(8,128)(2,1)S(1)} %shard_map.54), channel_id=1, source_target_pairs={{0,12},{1,13},{2,14},{3,15},{4,8},{5,9},{6,10},{7,11},{8,4},{9,5},... | collective-permute-start | bytes 589832 | tf_op jit(solution)/shard_map/ppermute | solution.py:24
  93.6 5.0 %collective-permute-done.8.refs_1_ = bf16[64,3072]{1,0:T(8,128)(2,1)S(1)} collective-permute-done((bf16[64,3072]{1,0:T(8,128)(2,1)S(1)}, bf16[64,3072]{1,0:T(8,128)(2,1)S(1)}, u32[]{:S(2)}, u32[]{:S(2)}) %collective-permute-start.8) | collective-permute-done | bytes 393248 | tf_op jit(solution)/shard_map/ppermute | solution.py:24
  98.6 0.1 shard_map.55
  98.7 1.9 %collective-permute-start.9 = (bf16[32,3072]{1,0:T(8,128)(2,1)S(1)}, bf16[32,3072]{1,0:T(8,128)(2,1)S(1)}, u32[]{:S(2)}, u32[]{:S(2)}) collective-permute-start(bf16[32,3072]{1,0:T(8,128)(2,1)S(1)} %get-tuple-element.26), channel_id=1, source_target_pairs={{0,1},{1,0},{2,3},{3,2},{4,5},{5,4},{6,7},{7,6},{8,9},{9,8},{10,11... | collective-permute-start | bytes 589832 | tf_op jit(solution)/shard_map/ppermute | solution.py:24
  100.6 1.7 %collective-permute-done.10.refs_2_ = bf16[32,3072]{1,0:T(8,128)(2,1)S(1)} collective-permute-done((bf16[32,3072]{1,0:T(8,128)(2,1)S(1)}, bf16[32,3072]{1,0:T(8,128)(2,1)S(1)}, u32[]{:S(2)}, u32[]{:S(2)}) %collective-permute-start.10) | collective-permute-done | bytes 196640 | tf_op jit(solution)/shard_map/ppermute | solution.py:24
  102.3 3.9 %collective-permute-done.9.refs_1_ = bf16[32,3072]{1,0:T(8,128)(2,1)S(1)} collective-permute-done((bf16[32,3072]{1,0:T(8,128)(2,1)S(1)}, bf16[32,3072]{1,0:T(8,128)(2,1)S(1)}, u32[]{:S(2)}, u32[]{:S(2)}) %collective-permute-start.9) | collective-permute-done | bytes 196640 | tf_op jit(solution)/shard_map/ppermute | solution.py:24
  106.2 0.1 shard_map.56
  106.3 12.6 %collective-permute-start.11 = (bf16[16,3072]{1,0:T(8,128)(2,1)S(1)}, bf16[16,3072]{1,0:T(8,128)(2,1)S(1)}, u32[]{:S(2)}, u32[]{:S(2)}) collective-permute-start(bf16[16,3072]{1,0:T(8,128)(2,1)S(1)} %get-tuple-element.28), channel_id=1, source_target_pairs={{0,4},{1,5},{2,6},{3,7},{4,0},{5,1},{6,2},{7,3},{8,12},{9,13},{10,... | collective-permute-start | bytes 294920 | tf_op jit(solution)/shard_map/ppermute | solution.py:24
  118.9 4.7 %collective-permute-done.11.refs_2_ = bf16[16,3072]{1,0:T(8,128)(2,1)S(1)} collective-permute-done((bf16[16,3072]{1,0:T(8,128)(2,1)S(1)}, bf16[16,3072]{1,0:T(8,128)(2,1)S(1)}, u32[]{:S(2)}, u32[]{:S(2)}) %collective-permute-start.11) | collective-permute-done | bytes 98336 | tf_op jit(solution)/shard_map/ppermute | solution.py:24
  123.6 0.0 copy-done.5
  123.6 0.7 shard_map.57
  (5 shorter events, 0.1 us)
Async XLA Ops:
  0.0 0.9 copy-start.4
  0.9 0.7 copy-start.6
  1.8 15.6 %collective-permute-start = (bf16[16,3072]{1,0:T(8,128)(2,1)S(1)}, bf16[16,3072]{1,0:T(8,128)(2,1)S(1)}, u32[]{:S(2)}, u32[]{:S(2)}) collective-permute-start(bf16[16,3072]{1,0:T(8,128)(2,1)S(1)} %shard_map.46.after.refs_0_), channel_id=1, source_target_pairs={{0,4},{1,5},{2,6},{3,7},{4,0},{5,1},{6,2},{7,3},{8,12},{9,13},{10,... | collective-permute-start | bytes 294920 | tf_op jit(solution)/shard_map/ppermute | solution.py:24
  12.8 2.3 %copy-start = (bf16[3072,768]{1,0:T(8,128)(2,1)S(1)}, bf16[3072,768]{1,0:T(8,128)(2,1)}, u32[]{:S(2)}) copy-start(bf16[3072,768]{1,0:T(8,128)(2,1)} %refs_2_.3) | copy-start | bytes 14155780
  15.1 2.3 %copy-start.2 = (bf16[768,3072]{1,0:T(8,128)(2,1)S(1)}, bf16[768,3072]{1,0:T(8,128)(2,1)}, u32[]{:S(2)}) copy-start(bf16[768,3072]{1,0:T(8,128)(2,1)} %refs_3_.3) | copy-start | bytes 14155780
  17.4 36.3 %copy-start.1 = (bf16[3072,768]{1,0:T(8,128)(2,1)S(1)}, bf16[3072,768]{1,0:T(8,128)(2,1)}, u32[]{:S(2)}) copy-start(bf16[3072,768]{1,0:T(8,128)(2,1)} %refs_2_.3) | copy-start | bytes 14155780
  17.4 36.3 %copy-start.3 = (bf16[768,3072]{1,0:T(8,128)(2,1)S(1)}, bf16[768,3072]{1,0:T(8,128)(2,1)}, u32[]{:S(2)}) copy-start(bf16[768,3072]{1,0:T(8,128)(2,1)} %refs_3_.3) | copy-start | bytes 14155780
  17.5 21.9 %collective-permute-start.3 = (bf16[32,3072]{1,0:T(8,128)(2,1)S(1)}, bf16[32,3072]{1,0:T(8,128)(2,1)S(1)}, u32[]{:S(2)}, u32[]{:S(2)}) collective-permute-start(bf16[32,3072]{1,0:T(8,128)(2,1)S(1)} %shard_map.48.refs_0_), channel_id=1, source_target_pairs={{0,12},{1,13},{2,14},{3,15},{4,8},{5,9},{6,10},{7,11},{8,4},{9,5},... | collective-permute-start | bytes 589832 | tf_op jit(solution)/shard_map/ppermute | solution.py:24
  32.3 10.5 %collective-permute-start.1 = (bf16[32,3072]{1,0:T(8,128)(2,1)S(1)}, bf16[32,3072]{1,0:T(8,128)(2,1)S(1)}, u32[]{:S(2)}, u32[]{:S(2)}) collective-permute-start(bf16[32,3072]{1,0:T(8,128)(2,1)S(1)} %shard_map.48.refs_0_), channel_id=1, source_target_pairs={{0,1},{1,0},{2,3},{3,2},{4,5},{5,4},{6,7},{7,6},{8,9},{9,8},{10,11... | collective-permute-start | bytes 589832 | tf_op jit(solution)/shard_map/ppermute | solution.py:24
  39.4 7.9 %collective-permute-start.4 = (bf16[32,3072]{1,0:T(8,128)(2,1)S(1)}, bf16[32,3072]{1,0:T(8,128)(2,1)S(1)}, u32[]{:S(2)}, u32[]{:S(2)}) collective-permute-start(bf16[32,3072]{1,0:T(8,128)(2,1)S(1)} %collective-permute-done.3.refs_0_), channel_id=1, source_target_pairs={{0,1},{1,0},{2,3},{3,2},{4,5},{5,4},{6,7},{7,6},{8,9},{9,8},{10,11... | collective-permute-start | bytes 589832 | tf_op jit(solution)/shard_map/ppermute | solution.py:24
  42.8 10.9 %collective-permute-start.2 = (bf16[64,3072]{1,0:T(8,128)(2,1)S(1)}, bf16[64,3072]{1,0:T(8,128)(2,1)S(1)}, u32[]{:S(2)}, u32[]{:S(2)}) collective-permute-start(bf16[64,3072]{1,0:T(8,128)(2,1)S(1)} %shard_map.49.refs_0_), channel_id=1, source_target_pairs={{0,3},{1,2},{2,1},{3,0},{4,7},{5,6},{6,5},{7,4},{8,11},{9,10},{10,... | collective-permute-start | bytes 1179656 | tf_op jit(solution)/shard_map/ppermute | solution.py:24
  47.3 12.2 %collective-permute-start.5 = (bf16[64,3072]{1,0:T(8,128)(2,1)S(1)}, bf16[64,3072]{1,0:T(8,128)(2,1)S(1)}, u32[]{:S(2)}, u32[]{:S(2)}) collective-permute-start(bf16[64,3072]{1,0:T(8,128)(2,1)S(1)} %shard_map.51.refs_0_), channel_id=1, source_target_pairs={{0,3},{1,2},{2,1},{3,0},{4,7},{5,6},{6,5},{7,4},{8,11},{9,10},{10,... | collective-permute-start | bytes 1179656 | tf_op jit(solution)/shard_map/ppermute | solution.py:24
  59.5 64.1 %copy-start.5 = (bf16[16,3072]{1,0:T(8,128)(2,1)S(1)}, bf16[16,3072]{1,0:T(8,128)(2,1)}, u32[]{:S(2)}) copy-start(bf16[16,3072]{1,0:T(8,128)(2,1)} %refs_0_.1) | copy-start | bytes 294916
  63.4 11.9 %collective-permute-start.6 = (bf16[64,3072]{1,0:T(8,128)(2,1)S(1)}, bf16[64,3072]{1,0:T(8,128)(2,1)S(1)}, u32[]{:S(2)}, u32[]{:S(2)}) collective-permute-start(bf16[64,3072]{1,0:T(8,128)(2,1)S(1)} %get-tuple-element.20), channel_id=1, source_target_pairs={{0,3},{1,2},{2,1},{3,0},{4,7},{5,6},{6,5},{7,4},{8,11},{9,10},{10,... | collective-permute-start | bytes 1179656 | tf_op jit(solution)/shard_map/ppermute | solution.py:24
  75.4 9.7 %collective-permute-start.7 = (bf16[32,3072]{1,0:T(8,128)(2,1)S(1)}, bf16[32,3072]{1,0:T(8,128)(2,1)S(1)}, u32[]{:S(2)}, u32[]{:S(2)}) collective-permute-start(bf16[32,3072]{1,0:T(8,128)(2,1)S(1)} %get-tuple-element.22), channel_id=1, source_target_pairs={{0,1},{1,0},{2,3},{3,2},{4,5},{5,4},{6,7},{7,6},{8,9},{9,8},{10,11... | collective-permute-start | bytes 589832 | tf_op jit(solution)/shard_map/ppermute | solution.py:24
  85.2 13.4 %collective-permute-start.8 = (bf16[64,3072]{1,0:T(8,128)(2,1)S(1)}, bf16[64,3072]{1,0:T(8,128)(2,1)S(1)}, u32[]{:S(2)}, u32[]{:S(2)}) collective-permute-start(bf16[64,3072]{1,0:T(8,128)(2,1)S(1)} %get-tuple-element.24), channel_id=1, source_target_pairs={{0,3},{1,2},{2,1},{3,0},{4,7},{5,6},{6,5},{7,4},{8,11},{9,10},{10,... | collective-permute-start | bytes 1179656 | tf_op jit(solution)/shard_map/ppermute | solution.py:24
  90.7 11.6 %collective-permute-start.10 = (bf16[32,3072]{1,0:T(8,128)(2,1)S(1)}, bf16[32,3072]{1,0:T(8,128)(2,1)S(1)}, u32[]{:S(2)}, u32[]{:S(2)}) collective-permute-start(bf16[32,3072]{1,0:T(8,128)(2,1)S(1)} %shard_map.54), channel_id=1, source_target_pairs={{0,12},{1,13},{2,14},{3,15},{4,8},{5,9},{6,10},{7,11},{8,4},{9,5},... | collective-permute-start | bytes 589832 | tf_op jit(solution)/shard_map/ppermute | solution.py:24
  98.7 7.6 %collective-permute-start.9 = (bf16[32,3072]{1,0:T(8,128)(2,1)S(1)}, bf16[32,3072]{1,0:T(8,128)(2,1)S(1)}, u32[]{:S(2)}, u32[]{:S(2)}) collective-permute-start(bf16[32,3072]{1,0:T(8,128)(2,1)S(1)} %get-tuple-element.26), channel_id=1, source_target_pairs={{0,1},{1,0},{2,3},{3,2},{4,5},{5,4},{6,7},{7,6},{8,9},{9,8},{10,11... | collective-permute-start | bytes 589832 | tf_op jit(solution)/shard_map/ppermute | solution.py:24
  106.3 17.2 %collective-permute-start.11 = (bf16[16,3072]{1,0:T(8,128)(2,1)S(1)}, bf16[16,3072]{1,0:T(8,128)(2,1)S(1)}, u32[]{:S(2)}, u32[]{:S(2)}) collective-permute-start(bf16[16,3072]{1,0:T(8,128)(2,1)S(1)} %get-tuple-element.28), channel_id=1, source_target_pairs={{0,4},{1,5},{2,6},{3,7},{4,0},{5,1},{6,2},{7,3},{8,12},{9,13},{10,... | collective-permute-start | bytes 294920 | tf_op jit(solution)/shard_map/ppermute | solution.py:24

commit v4 on v2

--- a/solution.py
+++ b/solution.py
@@ -12,14 +12,14 @@
 AFTER = pl.BlockSpec(memory_space=pl.ANY)
 
 
-def trade(value, shape, axis, turn):
+def shift(value, shape, axis, step):
     dp, mp = shape
     pairs = []
     for batch in range(dp):
-        flip = 1 if batch % 2 == turn else SIDE - 1
+        move = step if batch % 2 == 0 else -step
         for spot in range(mp):
             z, x = divmod(spot, SIDE)
-            z, x = (z ^ flip, x) if axis == 0 else (z, x ^ flip)
+            z, x = ((z + move) % SIDE, x) if axis == 0 else (z, (x + move) % SIDE)
             pairs.append((batch * mp + spot, batch * mp + z * SIDE + x))
     return lax.ppermute(value, ("dp", "mp"), pairs)
 
@@ -118,22 +118,25 @@
 
 
 def on_device(shape, tokens, ln_gain, w_in, w_out):
-    along_z = functools.partial(trade, shape=shape, axis=0)
-    along_x = functools.partial(trade, shape=shape, axis=1)
+    along_z = functools.partial(shift, shape=shape, axis=0)
+    along_x = functools.partial(shift, shape=shape, axis=1)
     (own,) = call(
         normalize_body, [jax.ShapeDtypeStruct(tokens.shape, jnp.bfloat16)], (tokens, ln_gain[None, :])
     )
+    near, far = along_z(own, step=1), along_z(own, step=-1)
+    opposite = along_z(near, step=1)
     held = ready(w_in, w_out, own)
-    pair = stack([own, along_z(own, turn=0)], held)
-    four = stack([pair, along_z(pair, turn=1)], held)
-    kept = stack([four, along_x(four, turn=0)], held)
-    sent = along_x(kept, turn=1)
-    (kept,) = feed([kept], w_in, w_out, kept)
-    (sent,) = feed([sent], w_in, w_out, kept)
-    kept, sent = add([kept, along_x(sent, turn=1)], 2)
-    kept, sent = add([kept, along_x(sent, turn=0)], 2)
-    kept, sent = add([kept, along_z(sent, turn=1)], 2)
-    return add([tokens, kept, along_z(sent, turn=0)])[0]
+    own = stack([own, near, far, opposite], held)
+    near, far = along_x(own, step=1), along_x(own, step=-1)
+    opposite = along_x(near, step=1)
+    own, near, far = feed([own, near, far], w_in, w_out, held)
+    near, far = along_x(near, step=-1), along_x(far, step=1)
+    (opposite,) = feed([opposite], w_in, w_out, own)
+    opposite = along_x(opposite, step=2)
+    own, near, far, opposite = add([own, near, far, opposite], 4)
+    opposite = along_z(opposite, step=2)
+    near, far = along_z(near, step=-1), along_z(far, step=1)
+    return add([tokens, own, near, far, opposite])[0]
 
 
 def solution(mesh):

time: 131 us -> 113 us (0.86)
  the two profiles are of different devices: /device:TPU:6 before, /device:TPU:34 now
where the time goes in v4:
time: 113 us; the launch traced here: 112 us
  starting transfers between devices  62.4 us (55%)
  waiting for transfers between devices  33.9 us (30%)
  Pallas kernels  9.48 us (8%)
  local copies, waits for them, and re-layouts  6.27 us (6%)
    ppermute x12, starting transfers between devices, shift(): return lax.ppermute(value, ('dp', 'mp'), pairs)  62.4 us
    ppermute x12, waiting for transfers between devices, shift(): return lax.ppermute(value, ('dp', 'mp'), pairs)  33.9 us
    pallas_call x7, Pallas kernels, call(): pl.pallas_call(body, out_shape=outs, in_specs=specs or [VMEM] * len(args)...  9.48 us
    unnamed x12, local copies, waits for them, and re-layouts  6.27 us
  transfers between devices with their start and end apart: 12, of which 6 were waited for; matrix products, arithmetic and copies ran while one was open for 0% of the time, Pallas kernels for 7%

profile of v4, /device:TPU:34, one launch (start us, length us, event | category | flops | bytes accessed | tf_op | source)
XLA Modules:
  0.0 112.2 jit_solution(1175708473640023973)
XLA Ops:
  0.0 0.0 copy-start.4
  0.0 0.9 copy-done.4
  0.9 0.0 copy-start.5
  0.9 0.7 copy-done.5
  1.6 0.2 shard_map.46.after.refs_0_
  1.8 10.9 %collective-permute-start = (bf16[16,3072]{1,0:T(8,128)(2,1)S(1)}, bf16[16,3072]{1,0:T(8,128)(2,1)S(1)}, u32[]{:S(2)}, u32[]{:S(2)}) collective-permute-start(bf16[16,3072]{1,0:T(8,128)(2,1)S(1)} %shard_map.46.after.refs_0_), channel_id=1, source_target_pairs={{0,4},{1,5},{2,6},{3,7},{4,8},{5,9},{6,10},{7,11},{8,12},{9,13},{1... | collective-permute-start | bytes 294920 | tf_op jit(solution)/shard_map/ppermute | solution.py:24
  12.8 9.2 %collective-permute-start.1 = (bf16[16,3072]{1,0:T(8,128)(2,1)S(1)}, bf16[16,3072]{1,0:T(8,128)(2,1)S(1)}, u32[]{:S(2)}, u32[]{:S(2)}) collective-permute-start(bf16[16,3072]{1,0:T(8,128)(2,1)S(1)} %shard_map.46.after.refs_0_), channel_id=1, source_target_pairs={{0,12},{1,13},{2,14},{3,15},{4,0},{5,1},{6,2},{7,3},{8,4},{9,5},{1... | collective-permute-start | bytes 294920 | tf_op jit(solution)/shard_map/ppermute | solution.py:24
  22.0 0.9 collective-permute-done.refs_1_
  22.9 4.3 %collective-permute-start.2 = (bf16[16,3072]{1,0:T(8,128)(2,1)S(1)}, bf16[16,3072]{1,0:T(8,128)(2,1)S(1)}, u32[]{:S(2)}, u32[]{:S(2)}) collective-permute-start(bf16[16,3072]{1,0:T(8,128)(2,1)S(1)} %collective-permute-done.refs_1_), channel_id=1, source_target_pairs={{0,4},{1,5},{2,6},{3,7},{4,8},{5,9},{6,10},{7,11},{8,12},{9,13},{1... | collective-permute-start | bytes 294920 | tf_op jit(solution)/shard_map/ppermute | solution.py:24
  27.3 0.0 copy-start
  27.3 2.3 %copy-done = bf16[3072,768]{1,0:T(8,128)(2,1)S(1)} copy-done((bf16[3072,768]{1,0:T(8,128)(2,1)S(1)}, bf16[3072,768]{1,0:T(8,128)(2,1)}, u32[]{:S(2)}) %copy-start) | copy-done | bytes 4718616
  29.6 0.0 copy-start.2
  29.6 2.3 %copy-done.2 = bf16[768,3072]{1,0:T(8,128)(2,1)S(1)} copy-done((bf16[768,3072]{1,0:T(8,128)(2,1)S(1)}, bf16[768,3072]{1,0:T(8,128)(2,1)}, u32[]{:S(2)}) %copy-start.2) | copy-done | bytes 4718616
  31.9 0.0 copy-start.1
  31.9 0.0 copy-start.3
  31.9 0.0 collective-permute-done.1.refs_2_
  31.9 4.6 %collective-permute-done.2.refs_3_ = bf16[16,3072]{1,0:T(8,128)(2,1)S(1)} collective-permute-done((bf16[16,3072]{1,0:T(8,128)(2,1)S(1)}, bf16[16,3072]{1,0:T(8,128)(2,1)S(1)}, u32[]{:S(2)}, u32[]{:S(2)}) %collective-permute-start.2) | collective-permute-done | bytes 98336 | tf_op jit(solution)/shard_map/ppermute | solution.py:24
  36.5 3.4 %collective-permute-start.3 = (bf16[64,3072]{1,0:T(8,128)(2,1)S(1)}, bf16[64,3072]{1,0:T(8,128)(2,1)S(1)}, u32[]{:S(2)}, u32[]{:S(2)}) collective-permute-start(bf16[64,3072]{1,0:T(8,128)(2,1)S(1)} %shard_map.48.refs_0_), channel_id=1, source_target_pairs={{0,1},{1,2},{2,3},{3,0},{4,5},{5,6},{6,7},{7,4},{8,9},{9,10},{10,1... | collective-permute-start | bytes 1179656 | tf_op jit(solution)/shard_map/ppermute | solution.py:24
  39.9 2.4 %collective-permute-start.4 = (bf16[64,3072]{1,0:T(8,128)(2,1)S(1)}, bf16[64,3072]{1,0:T(8,128)(2,1)S(1)}, u32[]{:S(2)}, u32[]{:S(2)}) collective-permute-start(bf16[64,3072]{1,0:T(8,128)(2,1)S(1)} %shard_map.48.refs_0_), channel_id=1, source_target_pairs={{0,3},{1,0},{2,1},{3,2},{4,7},{5,4},{6,5},{7,6},{8,11},{9,8},{10,9... | collective-permute-start | bytes 1179656 | tf_op jit(solution)/shard_map/ppermute | solution.py:24
  42.4 5.1 %collective-permute-done.3.refs_1_ = bf16[64,3072]{1,0:T(8,128)(2,1)S(1)} collective-permute-done((bf16[64,3072]{1,0:T(8,128)(2,1)S(1)}, bf16[64,3072]{1,0:T(8,128)(2,1)S(1)}, u32[]{:S(2)}, u32[]{:S(2)}) %collective-permute-start.3) | collective-permute-done | bytes 393248 | tf_op jit(solution)/shard_map/ppermute | solution.py:24
  47.5 4.1 %collective-permute-start.7 = (bf16[64,3072]{1,0:T(8,128)(2,1)S(1)}, bf16[64,3072]{1,0:T(8,128)(2,1)S(1)}, u32[]{:S(2)}, u32[]{:S(2)}) collective-permute-start(bf16[64,3072]{1,0:T(8,128)(2,1)S(1)} %collective-permute-done.3.refs_1_), channel_id=1, source_target_pairs={{0,1},{1,2},{2,3},{3,0},{4,5},{5,6},{6,7},{7,4},{8,9},{9,10},{10,1... | collective-permute-start | bytes 1179656 | tf_op jit(solution)/shard_map/ppermute | solution.py:24
  51.7 0.0 collective-permute-done.4.refs_2_
  51.7 0.0 copy-done.1
  51.7 0.0 copy-done.3
  51.7 4.6 %shard_map.49 = (bf16[64,3072]{1,0:T(8,128)(2,1)S(1)}, bf16[64,3072]{1,0:T(8,128)(2,1)S(1)}, bf16[64,3072]{1,0:T(8,128)(2,1)S(1)}) custom-call(bf16[64,3072]{1,0:T(8,128)(2,1)S(1)} %shard_map.48.refs_0_, bf16[64,3072]{1,0:T(8,128)(2,1)S(1)} %collective-permute-done.3.refs_1_, bf16[64,3072]{1,0:T(8,128)(2,1)S(1)} %collective-permute-done.4.refs_2_, ...), custom_call_target="tpu_custom_call" | custom-call | flops 1811939328 | bytes 11798528 | tf_op jit(solution)/shard_map/pallas_call | solution.py:31
  56.3 1.9 %collective-permute-start.5 = (bf16[64,3072]{1,0:T(8,128)(2,1)S(1)}, bf16[64,3072]{1,0:T(8,128)(2,1)S(1)}, u32[]{:S(2)}, u32[]{:S(2)}) collective-permute-start(bf16[64,3072]{1,0:T(8,128)(2,1)S(1)} %get-tuple-element.13), channel_id=1, source_target_pairs={{0,3},{1,0},{2,1},{3,2},{4,7},{5,4},{6,5},{7,6},{8,11},{9,8},{10,9... | collective-permute-start | bytes 1179656 | tf_op jit(solution)/shard_map/ppermute | solution.py:24
  58.3 3.9 %collective-permute-start.6 = (bf16[64,3072]{1,0:T(8,128)(2,1)S(1)}, bf16[64,3072]{1,0:T(8,128)(2,1)S(1)}, u32[]{:S(2)}, u32[]{:S(2)}) collective-permute-start(bf16[64,3072]{1,0:T(8,128)(2,1)S(1)} %get-tuple-element.14), channel_id=1, source_target_pairs={{0,1},{1,2},{2,3},{3,0},{4,5},{5,6},{6,7},{7,4},{8,9},{9,10},{10,1... | collective-permute-start | bytes 1179656 | tf_op jit(solution)/shard_map/ppermute | solution.py:24
  62.2 0.0 collective-permute-done.7.refs_0_
  62.2 3.7 %shard_map.50 = bf16[64,3072]{1,0:T(8,128)(2,1)S(1)} custom-call(bf16[64,3072]{1,0:T(8,128)(2,1)S(1)} %collective-permute-done.7.refs_0_, bf16[3072,768]{1,0:T(8,128)(2,1)S(1)} %copy-done.1, bf16[768,3072]{1,0:T(8,128)(2,1)S(1)} %copy-done.3, bf16[64,3072]{1,0:T(8,128)(2,1)S(1)} %get-tuple-element.12.refs_3_.refs_0_), custom_call_target="tpu_custom_call" | custom-call | flops 603979776 | bytes 10616832 | tf_op jit(solution)/shard_map/pallas_call | solution.py:31
  65.9 4.8 %collective-permute-start.8 = (bf16[64,3072]{1,0:T(8,128)(2,1)S(1)}, bf16[64,3072]{1,0:T(8,128)(2,1)S(1)}, u32[]{:S(2)}, u32[]{:S(2)}) collective-permute-start(bf16[64,3072]{1,0:T(8,128)(2,1)S(1)} %shard_map.50), channel_id=1, source_target_pairs={{0,2},{1,3},{2,0},{3,1},{4,6},{5,7},{6,4},{7,5},{8,10},{9,11},{10,... | collective-permute-start | bytes 1179656 | tf_op jit(solution)/shard_map/ppermute | solution.py:24
  70.7 0.0 collective-permute-done.5.refs_1_
  70.7 0.0 collective-permute-done.6.refs_2_
  70.8 9.1 %collective-permute-done.8.refs_3_ = bf16[64,3072]{1,0:T(8,128)(2,1)S(1)} collective-permute-done((bf16[64,3072]{1,0:T(8,128)(2,1)S(1)}, bf16[64,3072]{1,0:T(8,128)(2,1)S(1)}, u32[]{:S(2)}, u32[]{:S(2)}) %collective-permute-start.8) | collective-permute-done | bytes 393248 | tf_op jit(solution)/shard_map/ppermute | solution.py:24
  79.8 0.2 shard_map.51
  80.0 7.0 %collective-permute-start.9 = (bf16[16,3072]{1,0:T(8,128)(2,1)S(1)}, bf16[16,3072]{1,0:T(8,128)(2,1)S(1)}, u32[]{:S(2)}, u32[]{:S(2)}) collective-permute-start(bf16[16,3072]{1,0:T(8,128)(2,1)S(1)} %get-tuple-element.16), channel_id=1, source_target_pairs={{0,12},{1,13},{2,14},{3,15},{4,0},{5,1},{6,2},{7,3},{8,4},{9,5},{1... | collective-permute-start | bytes 294920 | tf_op jit(solution)/shard_map/ppermute | solution.py:24
  87.0 2.8 %collective-permute-start.10 = (bf16[16,3072]{1,0:T(8,128)(2,1)S(1)}, bf16[16,3072]{1,0:T(8,128)(2,1)S(1)}, u32[]{:S(2)}, u32[]{:S(2)}) collective-permute-start(bf16[16,3072]{1,0:T(8,128)(2,1)S(1)} %get-tuple-element.17), channel_id=1, source_target_pairs={{0,4},{1,5},{2,6},{3,7},{4,8},{5,9},{6,10},{7,11},{8,12},{9,13},{1... | collective-permute-start | bytes 294920 | tf_op jit(solution)/shard_map/ppermute | solution.py:24
  89.8 7.5 %collective-permute-start.11 = (bf16[16,3072]{1,0:T(8,128)(2,1)S(1)}, bf16[16,3072]{1,0:T(8,128)(2,1)S(1)}, u32[]{:S(2)}, u32[]{:S(2)}) collective-permute-start(bf16[16,3072]{1,0:T(8,128)(2,1)S(1)} %get-tuple-element.18), channel_id=1, source_target_pairs={{0,8},{1,9},{2,10},{3,11},{4,12},{5,13},{6,14},{7,15},{8,0},{9,1},... | collective-permute-start | bytes 294920 | tf_op jit(solution)/shard_map/ppermute | solution.py:24
  97.3 0.0 collective-permute-done.9.refs_2_
  97.4 0.2 collective-permute-done.10.refs_3_
  97.6 13.9 %collective-permute-done.11.refs_4_ = bf16[16,3072]{1,0:T(8,128)(2,1)S(1)} collective-permute-done((bf16[16,3072]{1,0:T(8,128)(2,1)S(1)}, bf16[16,3072]{1,0:T(8,128)(2,1)S(1)}, u32[]{:S(2)}, u32[]{:S(2)}) %collective-permute-start.11) | collective-permute-done | bytes 98336 | tf_op jit(solution)/shard_map/ppermute | solution.py:24
  111.5 0.7 shard_map.52
  (2 shorter events, 0.0 us)
Async XLA Ops:
  0.0 0.9 copy-start.4
  0.9 0.7 copy-start.5
  1.8 21.1 %collective-permute-start = (bf16[16,3072]{1,0:T(8,128)(2,1)S(1)}, bf16[16,3072]{1,0:T(8,128)(2,1)S(1)}, u32[]{:S(2)}, u32[]{:S(2)}) collective-permute-start(bf16[16,3072]{1,0:T(8,128)(2,1)S(1)} %shard_map.46.after.refs_0_), channel_id=1, source_target_pairs={{0,4},{1,5},{2,6},{3,7},{4,8},{5,9},{6,10},{7,11},{8,12},{9,13},{1... | collective-permute-start | bytes 294920 | tf_op jit(solution)/shard_map/ppermute | solution.py:24
  12.8 19.2 %collective-permute-start.1 = (bf16[16,3072]{1,0:T(8,128)(2,1)S(1)}, bf16[16,3072]{1,0:T(8,128)(2,1)S(1)}, u32[]{:S(2)}, u32[]{:S(2)}) collective-permute-start(bf16[16,3072]{1,0:T(8,128)(2,1)S(1)} %shard_map.46.after.refs_0_), channel_id=1, source_target_pairs={{0,12},{1,13},{2,14},{3,15},{4,0},{5,1},{6,2},{7,3},{8,4},{9,5},{1... | collective-permute-start | bytes 294920 | tf_op jit(solution)/shard_map/ppermute | solution.py:24
  22.9 13.6 %collective-permute-start.2 = (bf16[16,3072]{1,0:T(8,128)(2,1)S(1)}, bf16[16,3072]{1,0:T(8,128)(2,1)S(1)}, u32[]{:S(2)}, u32[]{:S(2)}) collective-permute-start(bf16[16,3072]{1,0:T(8,128)(2,1)S(1)} %collective-permute-done.refs_1_), channel_id=1, source_target_pairs={{0,4},{1,5},{2,6},{3,7},{4,8},{5,9},{6,10},{7,11},{8,12},{9,13},{1... | collective-permute-start | bytes 294920 | tf_op jit(solution)/shard_map/ppermute | solution.py:24
  27.3 2.3 %copy-start = (bf16[3072,768]{1,0:T(8,128)(2,1)S(1)}, bf16[3072,768]{1,0:T(8,128)(2,1)}, u32[]{:S(2)}) copy-start(bf16[3072,768]{1,0:T(8,128)(2,1)} %refs_1_.1) | copy-start | bytes 14155780
  29.6 2.3 %copy-start.2 = (bf16[768,3072]{1,0:T(8,128)(2,1)S(1)}, bf16[768,3072]{1,0:T(8,128)(2,1)}, u32[]{:S(2)}) copy-start(bf16[768,3072]{1,0:T(8,128)(2,1)} %refs_2_.1) | copy-start | bytes 14155780
  31.9 19.7 %copy-start.1 = (bf16[3072,768]{1,0:T(8,128)(2,1)S(1)}, bf16[3072,768]{1,0:T(8,128)(2,1)}, u32[]{:S(2)}) copy-start(bf16[3072,768]{1,0:T(8,128)(2,1)} %refs_1_.1) | copy-start | bytes 14155780
  31.9 19.8 %copy-start.3 = (bf16[768,3072]{1,0:T(8,128)(2,1)S(1)}, bf16[768,3072]{1,0:T(8,128)(2,1)}, u32[]{:S(2)}) copy-start(bf16[768,3072]{1,0:T(8,128)(2,1)} %refs_2_.1) | copy-start | bytes 14155780
  36.5 11.0 %collective-permute-start.3 = (bf16[64,3072]{1,0:T(8,128)(2,1)S(1)}, bf16[64,3072]{1,0:T(8,128)(2,1)S(1)}, u32[]{:S(2)}, u32[]{:S(2)}) collective-permute-start(bf16[64,3072]{1,0:T(8,128)(2,1)S(1)} %shard_map.48.refs_0_), channel_id=1, source_target_pairs={{0,1},{1,2},{2,3},{3,0},{4,5},{5,6},{6,7},{7,4},{8,9},{9,10},{10,1... | collective-permute-start | bytes 1179656 | tf_op jit(solution)/shard_map/ppermute | solution.py:24
  39.9 11.7 %collective-permute-start.4 = (bf16[64,3072]{1,0:T(8,128)(2,1)S(1)}, bf16[64,3072]{1,0:T(8,128)(2,1)S(1)}, u32[]{:S(2)}, u32[]{:S(2)}) collective-permute-start(bf16[64,3072]{1,0:T(8,128)(2,1)S(1)} %shard_map.48.refs_0_), channel_id=1, source_target_pairs={{0,3},{1,0},{2,1},{3,2},{4,7},{5,4},{6,5},{7,6},{8,11},{9,8},{10,9... | collective-permute-start | bytes 1179656 | tf_op jit(solution)/shard_map/ppermute | solution.py:24
  47.5 14.7 %collective-permute-start.7 = (bf16[64,3072]{1,0:T(8,128)(2,1)S(1)}, bf16[64,3072]{1,0:T(8,128)(2,1)S(1)}, u32[]{:S(2)}, u32[]{:S(2)}) collective-permute-start(bf16[64,3072]{1,0:T(8,128)(2,1)S(1)} %collective-permute-done.3.refs_1_), channel_id=1, source_target_pairs={{0,1},{1,2},{2,3},{3,0},{4,5},{5,6},{6,7},{7,4},{8,9},{9,10},{10,1... | collective-permute-start | bytes 1179656 | tf_op jit(solution)/shard_map/ppermute | solution.py:24
  56.3 14.4 %collective-permute-start.5 = (bf16[64,3072]{1,0:T(8,128)(2,1)S(1)}, bf16[64,3072]{1,0:T(8,128)(2,1)S(1)}, u32[]{:S(2)}, u32[]{:S(2)}) collective-permute-start(bf16[64,3072]{1,0:T(8,128)(2,1)S(1)} %get-tuple-element.13), channel_id=1, source_target_pairs={{0,3},{1,0},{2,1},{3,2},{4,7},{5,4},{6,5},{7,6},{8,11},{9,8},{10,9... | collective-permute-start | bytes 1179656 | tf_op jit(solution)/shard_map/ppermute | solution.py:24
  58.3 12.5 %collective-permute-start.6 = (bf16[64,3072]{1,0:T(8,128)(2,1)S(1)}, bf16[64,3072]{1,0:T(8,128)(2,1)S(1)}, u32[]{:S(2)}, u32[]{:S(2)}) collective-permute-start(bf16[64,3072]{1,0:T(8,128)(2,1)S(1)} %get-tuple-element.14), channel_id=1, source_target_pairs={{0,1},{1,2},{2,3},{3,0},{4,5},{5,6},{6,7},{7,4},{8,9},{9,10},{10,1... | collective-permute-start | bytes 1179656 | tf_op jit(solution)/shard_map/ppermute | solution.py:24
  65.9 13.9 %collective-permute-start.8 = (bf16[64,3072]{1,0:T(8,128)(2,1)S(1)}, bf16[64,3072]{1,0:T(8,128)(2,1)S(1)}, u32[]{:S(2)}, u32[]{:S(2)}) collective-permute-start(bf16[64,3072]{1,0:T(8,128)(2,1)S(1)} %shard_map.50), channel_id=1, source_target_pairs={{0,2},{1,3},{2,0},{3,1},{4,6},{5,7},{6,4},{7,5},{8,10},{9,11},{10,... | collective-permute-start | bytes 1179656 | tf_op jit(solution)/shard_map/ppermute | solution.py:24
  80.0 17.3 %collective-permute-start.9 = (bf16[16,3072]{1,0:T(8,128)(2,1)S(1)}, bf16[16,3072]{1,0:T(8,128)(2,1)S(1)}, u32[]{:S(2)}, u32[]{:S(2)}) collective-permute-start(bf16[16,3072]{1,0:T(8,128)(2,1)S(1)} %get-tuple-element.16), channel_id=1, source_target_pairs={{0,12},{1,13},{2,14},{3,15},{4,0},{5,1},{6,2},{7,3},{8,4},{9,5},{1... | collective-permute-start | bytes 294920 | tf_op jit(solution)/shard_map/ppermute | solution.py:24
  87.0 10.5 %collective-permute-start.10 = (bf16[16,3072]{1,0:T(8,128)(2,1)S(1)}, bf16[16,3072]{1,0:T(8,128)(2,1)S(1)}, u32[]{:S(2)}, u32[]{:S(2)}) collective-permute-start(bf16[16,3072]{1,0:T(8,128)(2,1)S(1)} %get-tuple-element.17), channel_id=1, source_target_pairs={{0,4},{1,5},{2,6},{3,7},{4,8},{5,9},{6,10},{7,11},{8,12},{9,13},{1... | collective-permute-start | bytes 294920 | tf_op jit(solution)/shard_map/ppermute | solution.py:24
  89.8 21.7 %collective-permute-start.11 = (bf16[16,3072]{1,0:T(8,128)(2,1)S(1)}, bf16[16,3072]{1,0:T(8,128)(2,1)S(1)}, u32[]{:S(2)}, u32[]{:S(2)}) collective-permute-start(bf16[16,3072]{1,0:T(8,128)(2,1)S(1)} %get-tuple-element.18), channel_id=1, source_target_pairs={{0,8},{1,9},{2,10},{3,11},{4,12},{5,13},{6,14},{7,15},{8,0},{9,1},... | collective-permute-start | bytes 294920 | tf_op jit(solution)/shard_map/ppermute | solution.py:24

commit v5 on v4

--- a/solution.py
+++ b/solution.py
@@ -59,17 +59,13 @@
 def feed_body(parts, *refs):
     rows, (w_in, w_out), outs, hidden = refs[:parts], refs[parts : parts + 2], refs[parts + 3 : -1], refs[-1]
     height = rows[0].shape[0]
-    tile = 256
+    block = jnp.concatenate([r[...] for r in rows], axis=0)
+    linear = jnp.dot(block, w_in[...], preferred_element_type=jnp.float32)
+    active = linear * (0.5 * (1.0 + lax.erf(linear * (0.5**0.5))))
+    hidden[...] = active.astype(jnp.bfloat16)
+    tile = w_out.shape[1] // 2
 
-    @pl.loop(0, w_in.shape[1] // tile)
-    def _(step):
-        columns = pl.ds(pl.multiple_of(step * tile, tile), tile)
-        block = jnp.concatenate([r[...] for r in rows], axis=0)
-        linear = jnp.dot(block, w_in[:, columns], preferred_element_type=jnp.float32)
-        active = linear * (0.5 * (1.0 + lax.erf(linear * (0.5**0.5))))
-        hidden[:, columns] = active.astype(jnp.bfloat16)
-
-    @pl.loop(0, w_out.shape[1] // tile)
+    @pl.loop(0, 2)
     def _(step):
         columns = pl.ds(pl.multiple_of(step * tile, tile), tile)
         terms = jnp.dot(hidden[...], w_out[:, columns], preferred_element_type=jnp.float32)

time: 113 us -> 110 us (0.973)
  the two profiles are of different devices: /device:TPU:34 before, /device:TPU:1 now
where the time goes in v5:
time: 110 us; the launch traced here: 108 us
  starting transfers between devices  69.4 us (63%)
  waiting for transfers between devices  26.3 us (24%)
  local copies, waits for them, and re-layouts  6.27 us (6%)
  Pallas kernels  5.62 us (5%)
    ppermute x12, starting transfers between devices, shift(): return lax.ppermute(value, ('dp', 'mp'), pairs)  69.4 us
    ppermute x12, waiting for transfers between devices, shift(): return lax.ppermute(value, ('dp', 'mp'), pairs)  26.3 us
    unnamed x12, local copies, waits for them, and re-layouts  6.27 us
    pallas_call x7, Pallas kernels, call(): pl.pallas_call(body, out_shape=outs, in_specs=specs or [VMEM] * len(args)...  5.62 us
  transfers between devices with their start and end apart: 12, of which 5 were waited for; matrix products, arithmetic and copies ran while one was open for 0% of the time, Pallas kernels for 4%

profile of v5, /device:TPU:1, one launch (start us, length us, event | category | flops | bytes accessed | tf_op | source)
XLA Modules:
  0.0 107.9 jit_solution(2916826470415084330)
XLA Ops:
  0.0 0.0 copy-start.4
  0.0 0.9 copy-done.4
  0.9 0.0 copy-start.5
  0.9 0.7 copy-done.5
  1.6 0.2 shard_map.46.after.refs_0_
  1.8 18.7 %collective-permute-start = (bf16[16,3072]{1,0:T(8,128)(2,1)S(1)}, bf16[16,3072]{1,0:T(8,128)(2,1)S(1)}, u32[]{:S(2)}, u32[]{:S(2)}) collective-permute-start(bf16[16,3072]{1,0:T(8,128)(2,1)S(1)} %shard_map.46.after.refs_0_), channel_id=1, source_target_pairs={{0,4},{1,5},{2,6},{3,7},{4,8},{5,9},{6,10},{7,11},{8,12},{9,13},{1... | collective-permute-start | bytes 294920 | tf_op jit(solution)/shard_map/ppermute | solution.py:24
  20.6 1.9 %collective-permute-start.1 = (bf16[16,3072]{1,0:T(8,128)(2,1)S(1)}, bf16[16,3072]{1,0:T(8,128)(2,1)S(1)}, u32[]{:S(2)}, u32[]{:S(2)}) collective-permute-start(bf16[16,3072]{1,0:T(8,128)(2,1)S(1)} %shard_map.46.after.refs_0_), channel_id=1, source_target_pairs={{0,12},{1,13},{2,14},{3,15},{4,0},{5,1},{6,2},{7,3},{8,4},{9,5},{1... | collective-permute-start | bytes 294920 | tf_op jit(solution)/shard_map/ppermute | solution.py:24
  22.5 0.0 collective-permute-done.refs_1_
  22.5 11.4 %collective-permute-start.2 = (bf16[16,3072]{1,0:T(8,128)(2,1)S(1)}, bf16[16,3072]{1,0:T(8,128)(2,1)S(1)}, u32[]{:S(2)}, u32[]{:S(2)}) collective-permute-start(bf16[16,3072]{1,0:T(8,128)(2,1)S(1)} %collective-permute-done.refs_1_), channel_id=1, source_target_pairs={{0,4},{1,5},{2,6},{3,7},{4,8},{5,9},{6,10},{7,11},{8,12},{9,13},{1... | collective-permute-start | bytes 294920 | tf_op jit(solution)/shard_map/ppermute | solution.py:24
  33.9 0.0 copy-start
  33.9 2.3 %copy-done = bf16[3072,768]{1,0:T(8,128)(2,1)S(1)} copy-done((bf16[3072,768]{1,0:T(8,128)(2,1)S(1)}, bf16[3072,768]{1,0:T(8,128)(2,1)}, u32[]{:S(2)}) %copy-start) | copy-done | bytes 4718616
  36.2 0.0 copy-start.2
  36.2 2.3 %copy-done.2 = bf16[768,3072]{1,0:T(8,128)(2,1)S(1)} copy-done((bf16[768,3072]{1,0:T(8,128)(2,1)S(1)}, bf16[768,3072]{1,0:T(8,128)(2,1)}, u32[]{:S(2)}) %copy-start.2) | copy-done | bytes 4718616
  38.6 0.0 copy-start.1
  38.6 0.0 copy-start.3
  38.6 0.0 collective-permute-done.1.refs_2_
  38.6 0.0 collective-permute-done.2.refs_3_
  38.6 3.9 %collective-permute-start.3 = (bf16[64,3072]{1,0:T(8,128)(2,1)S(1)}, bf16[64,3072]{1,0:T(8,128)(2,1)S(1)}, u32[]{:S(2)}, u32[]{:S(2)}) collective-permute-start(bf16[64,3072]{1,0:T(8,128)(2,1)S(1)} %shard_map.48.refs_0_), channel_id=1, source_target_pairs={{0,1},{1,2},{2,3},{3,0},{4,5},{5,6},{6,7},{7,4},{8,9},{9,10},{10,1... | collective-permute-start | bytes 1179656 | tf_op jit(solution)/shard_map/ppermute | solution.py:24
  42.5 1.9 %collective-permute-start.4 = (bf16[64,3072]{1,0:T(8,128)(2,1)S(1)}, bf16[64,3072]{1,0:T(8,128)(2,1)S(1)}, u32[]{:S(2)}, u32[]{:S(2)}) collective-permute-start(bf16[64,3072]{1,0:T(8,128)(2,1)S(1)} %shard_map.48.refs_0_), channel_id=1, source_target_pairs={{0,3},{1,0},{2,1},{3,2},{4,7},{5,4},{6,5},{7,6},{8,11},{9,8},{10,9... | collective-permute-start | bytes 1179656 | tf_op jit(solution)/shard_map/ppermute | solution.py:24
  44.5 4.7 %collective-permute-done.3.refs_1_ = bf16[64,3072]{1,0:T(8,128)(2,1)S(1)} collective-permute-done((bf16[64,3072]{1,0:T(8,128)(2,1)S(1)}, bf16[64,3072]{1,0:T(8,128)(2,1)S(1)}, u32[]{:S(2)}, u32[]{:S(2)}) %collective-permute-start.3) | collective-permute-done | bytes 393248 | tf_op jit(solution)/shard_map/ppermute | solution.py:24
  49.1 4.8 %collective-permute-start.7 = (bf16[64,3072]{1,0:T(8,128)(2,1)S(1)}, bf16[64,3072]{1,0:T(8,128)(2,1)S(1)}, u32[]{:S(2)}, u32[]{:S(2)}) collective-permute-start(bf16[64,3072]{1,0:T(8,128)(2,1)S(1)} %collective-permute-done.3.refs_1_), channel_id=1, source_target_pairs={{0,1},{1,2},{2,3},{3,0},{4,5},{5,6},{6,7},{7,4},{8,9},{9,10},{10,1... | collective-permute-start | bytes 1179656 | tf_op jit(solution)/shard_map/ppermute | solution.py:24
  53.9 0.0 collective-permute-done.4.refs_2_
  53.9 0.0 copy-done.1
  54.0 0.0 copy-done.3
  54.0 2.4 %shard_map.49 = (bf16[64,3072]{1,0:T(8,128)(2,1)S(1)}, bf16[64,3072]{1,0:T(8,128)(2,1)S(1)}, bf16[64,3072]{1,0:T(8,128)(2,1)S(1)}) custom-call(bf16[64,3072]{1,0:T(8,128)(2,1)S(1)} %shard_map.48.refs_0_, bf16[64,3072]{1,0:T(8,128)(2,1)S(1)} %collective-permute-done.3.refs_1_, bf16[64,3072]{1,0:T(8,128)(2,1)S(1)} %collective-permute-done.4.refs_2_, ...), custom_call_target="tpu_custom_call" | custom-call | flops 1811939328 | bytes 11798528 | tf_op jit(solution)/shard_map/pallas_call | solution.py:31
  56.4 1.9 %collective-permute-start.5 = (bf16[64,3072]{1,0:T(8,128)(2,1)S(1)}, bf16[64,3072]{1,0:T(8,128)(2,1)S(1)}, u32[]{:S(2)}, u32[]{:S(2)}) collective-permute-start(bf16[64,3072]{1,0:T(8,128)(2,1)S(1)} %get-tuple-element.13), channel_id=1, source_target_pairs={{0,3},{1,0},{2,1},{3,2},{4,7},{5,4},{6,5},{7,6},{8,11},{9,8},{10,9... | collective-permute-start | bytes 1179656 | tf_op jit(solution)/shard_map/ppermute | solution.py:24
  58.3 4.6 %collective-permute-start.6 = (bf16[64,3072]{1,0:T(8,128)(2,1)S(1)}, bf16[64,3072]{1,0:T(8,128)(2,1)S(1)}, u32[]{:S(2)}, u32[]{:S(2)}) collective-permute-start(bf16[64,3072]{1,0:T(8,128)(2,1)S(1)} %get-tuple-element.14), channel_id=1, source_target_pairs={{0,1},{1,2},{2,3},{3,0},{4,5},{5,6},{6,7},{7,4},{8,9},{9,10},{10,1... | collective-permute-start | bytes 1179656 | tf_op jit(solution)/shard_map/ppermute | solution.py:24
  62.9 0.0 collective-permute-done.7.refs_0_
  62.9 2.0 %shard_map.50 = bf16[64,3072]{1,0:T(8,128)(2,1)S(1)} custom-call(bf16[64,3072]{1,0:T(8,128)(2,1)S(1)} %collective-permute-done.7.refs_0_, bf16[3072,768]{1,0:T(8,128)(2,1)S(1)} %copy-done.1, bf16[768,3072]{1,0:T(8,128)(2,1)S(1)} %copy-done.3, bf16[64,3072]{1,0:T(8,128)(2,1)S(1)} %get-tuple-element.12.refs_3_.refs_0_), custom_call_target="tpu_custom_call" | custom-call | flops 603979776 | bytes 10616832 | tf_op jit(solution)/shard_map/pallas_call | solution.py:31
  65.0 1.9 %collective-permute-start.8 = (bf16[64,3072]{1,0:T(8,128)(2,1)S(1)}, bf16[64,3072]{1,0:T(8,128)(2,1)S(1)}, u32[]{:S(2)}, u32[]{:S(2)}) collective-permute-start(bf16[64,3072]{1,0:T(8,128)(2,1)S(1)} %shard_map.50), channel_id=1, source_target_pairs={{0,2},{1,3},{2,0},{3,1},{4,6},{5,7},{6,4},{7,5},{8,10},{9,11},{10,... | collective-permute-start | bytes 1179656 | tf_op jit(solution)/shard_map/ppermute | solution.py:24
  66.9 0.0 collective-permute-done.5.refs_1_
  66.9 10.5 %collective-permute-done.6.refs_2_ = bf16[64,3072]{1,0:T(8,128)(2,1)S(1)} collective-permute-done((bf16[64,3072]{1,0:T(8,128)(2,1)S(1)}, bf16[64,3072]{1,0:T(8,128)(2,1)S(1)}, u32[]{:S(2)}, u32[]{:S(2)}) %collective-permute-start.6) | collective-permute-done | bytes 393248 | tf_op jit(solution)/shard_map/ppermute | solution.py:24
  77.4 1.3 %collective-permute-done.8.refs_3_ = bf16[64,3072]{1,0:T(8,128)(2,1)S(1)} collective-permute-done((bf16[64,3072]{1,0:T(8,128)(2,1)S(1)}, bf16[64,3072]{1,0:T(8,128)(2,1)S(1)}, u32[]{:S(2)}, u32[]{:S(2)}) %collective-permute-start.8) | collective-permute-done | bytes 393248 | tf_op jit(solution)/shard_map/ppermute | solution.py:24
  78.7 0.2 shard_map.51
  78.9 2.9 %collective-permute-start.9 = (bf16[16,3072]{1,0:T(8,128)(2,1)S(1)}, bf16[16,3072]{1,0:T(8,128)(2,1)S(1)}, u32[]{:S(2)}, u32[]{:S(2)}) collective-permute-start(bf16[16,3072]{1,0:T(8,128)(2,1)S(1)} %get-tuple-element.16), channel_id=1, source_target_pairs={{0,12},{1,13},{2,14},{3,15},{4,0},{5,1},{6,2},{7,3},{8,4},{9,5},{1... | collective-permute-start | bytes 294920 | tf_op jit(solution)/shard_map/ppermute | solution.py:24
  81.8 8.4 %collective-permute-start.10 = (bf16[16,3072]{1,0:T(8,128)(2,1)S(1)}, bf16[16,3072]{1,0:T(8,128)(2,1)S(1)}, u32[]{:S(2)}, u32[]{:S(2)}) collective-permute-start(bf16[16,3072]{1,0:T(8,128)(2,1)S(1)} %get-tuple-element.17), channel_id=1, source_target_pairs={{0,4},{1,5},{2,6},{3,7},{4,8},{5,9},{6,10},{7,11},{8,12},{9,13},{1... | collective-permute-start | bytes 294920 | tf_op jit(solution)/shard_map/ppermute | solution.py:24
  90.2 7.0 %collective-permute-start.11 = (bf16[16,3072]{1,0:T(8,128)(2,1)S(1)}, bf16[16,3072]{1,0:T(8,128)(2,1)S(1)}, u32[]{:S(2)}, u32[]{:S(2)}) collective-permute-start(bf16[16,3072]{1,0:T(8,128)(2,1)S(1)} %get-tuple-element.18), channel_id=1, source_target_pairs={{0,8},{1,9},{2,10},{3,11},{4,12},{5,13},{6,14},{7,15},{8,0},{9,1},... | collective-permute-start | bytes 294920 | tf_op jit(solution)/shard_map/ppermute | solution.py:24
  97.2 0.0 collective-permute-done.9.refs_2_
  97.2 3.5 %collective-permute-done.10.refs_3_ = bf16[16,3072]{1,0:T(8,128)(2,1)S(1)} collective-permute-done((bf16[16,3072]{1,0:T(8,128)(2,1)S(1)}, bf16[16,3072]{1,0:T(8,128)(2,1)S(1)}, u32[]{:S(2)}, u32[]{:S(2)}) %collective-permute-start.10) | collective-permute-done | bytes 98336 | tf_op jit(solution)/shard_map/ppermute | solution.py:24
  100.7 6.4 %collective-permute-done.11.refs_4_ = bf16[16,3072]{1,0:T(8,128)(2,1)S(1)} collective-permute-done((bf16[16,3072]{1,0:T(8,128)(2,1)S(1)}, bf16[16,3072]{1,0:T(8,128)(2,1)S(1)}, u32[]{:S(2)}, u32[]{:S(2)}) %collective-permute-start.11) | collective-permute-done | bytes 98336 | tf_op jit(solution)/shard_map/ppermute | solution.py:24
  107.1 0.7 shard_map.52
  (2 shorter events, 0.0 us)
Async XLA Ops:
  0.0 0.9 copy-start.4
  0.9 0.7 copy-start.5
  1.8 20.7 %collective-permute-start = (bf16[16,3072]{1,0:T(8,128)(2,1)S(1)}, bf16[16,3072]{1,0:T(8,128)(2,1)S(1)}, u32[]{:S(2)}, u32[]{:S(2)}) collective-permute-start(bf16[16,3072]{1,0:T(8,128)(2,1)S(1)} %shard_map.46.after.refs_0_), channel_id=1, source_target_pairs={{0,4},{1,5},{2,6},{3,7},{4,8},{5,9},{6,10},{7,11},{8,12},{9,13},{1... | collective-permute-start | bytes 294920 | tf_op jit(solution)/shard_map/ppermute | solution.py:24
  20.6 18.0 %collective-permute-start.1 = (bf16[16,3072]{1,0:T(8,128)(2,1)S(1)}, bf16[16,3072]{1,0:T(8,128)(2,1)S(1)}, u32[]{:S(2)}, u32[]{:S(2)}) collective-permute-start(bf16[16,3072]{1,0:T(8,128)(2,1)S(1)} %shard_map.46.after.refs_0_), channel_id=1, source_target_pairs={{0,12},{1,13},{2,14},{3,15},{4,0},{5,1},{6,2},{7,3},{8,4},{9,5},{1... | collective-permute-start | bytes 294920 | tf_op jit(solution)/shard_map/ppermute | solution.py:24
  22.5 16.1 %collective-permute-start.2 = (bf16[16,3072]{1,0:T(8,128)(2,1)S(1)}, bf16[16,3072]{1,0:T(8,128)(2,1)S(1)}, u32[]{:S(2)}, u32[]{:S(2)}) collective-permute-start(bf16[16,3072]{1,0:T(8,128)(2,1)S(1)} %collective-permute-done.refs_1_), channel_id=1, source_target_pairs={{0,4},{1,5},{2,6},{3,7},{4,8},{5,9},{6,10},{7,11},{8,12},{9,13},{1... | collective-permute-start | bytes 294920 | tf_op jit(solution)/shard_map/ppermute | solution.py:24
  33.9 2.3 %copy-start = (bf16[3072,768]{1,0:T(8,128)(2,1)S(1)}, bf16[3072,768]{1,0:T(8,128)(2,1)}, u32[]{:S(2)}) copy-start(bf16[3072,768]{1,0:T(8,128)(2,1)} %refs_1_.1) | copy-start | bytes 14155780
  36.2 2.3 %copy-start.2 = (bf16[768,3072]{1,0:T(8,128)(2,1)S(1)}, bf16[768,3072]{1,0:T(8,128)(2,1)}, u32[]{:S(2)}) copy-start(bf16[768,3072]{1,0:T(8,128)(2,1)} %refs_2_.1) | copy-start | bytes 14155780
  38.6 15.4 %copy-start.1 = (bf16[3072,768]{1,0:T(8,128)(2,1)S(1)}, bf16[3072,768]{1,0:T(8,128)(2,1)}, u32[]{:S(2)}) copy-start(bf16[3072,768]{1,0:T(8,128)(2,1)} %refs_1_.1) | copy-start | bytes 14155780
  38.6 15.4 %copy-start.3 = (bf16[768,3072]{1,0:T(8,128)(2,1)S(1)}, bf16[768,3072]{1,0:T(8,128)(2,1)}, u32[]{:S(2)}) copy-start(bf16[768,3072]{1,0:T(8,128)(2,1)} %refs_2_.1) | copy-start | bytes 14155780
  38.6 10.5 %collective-permute-start.3 = (bf16[64,3072]{1,0:T(8,128)(2,1)S(1)}, bf16[64,3072]{1,0:T(8,128)(2,1)S(1)}, u32[]{:S(2)}, u32[]{:S(2)}) collective-permute-start(bf16[64,3072]{1,0:T(8,128)(2,1)S(1)} %shard_map.48.refs_0_), channel_id=1, source_target_pairs={{0,1},{1,2},{2,3},{3,0},{4,5},{5,6},{6,7},{7,4},{8,9},{9,10},{10,1... | collective-permute-start | bytes 1179656 | tf_op jit(solution)/shard_map/ppermute | solution.py:24
  42.5 11.4 %collective-permute-start.4 = (bf16[64,3072]{1,0:T(8,128)(2,1)S(1)}, bf16[64,3072]{1,0:T(8,128)(2,1)S(1)}, u32[]{:S(2)}, u32[]{:S(2)}) collective-permute-start(bf16[64,3072]{1,0:T(8,128)(2,1)S(1)} %shard_map.48.refs_0_), channel_id=1, source_target_pairs={{0,3},{1,0},{2,1},{3,2},{4,7},{5,4},{6,5},{7,6},{8,11},{9,8},{10,9... | collective-permute-start | bytes 1179656 | tf_op jit(solution)/shard_map/ppermute | solution.py:24
  49.1 13.8 %collective-permute-start.7 = (bf16[64,3072]{1,0:T(8,128)(2,1)S(1)}, bf16[64,3072]{1,0:T(8,128)(2,1)S(1)}, u32[]{:S(2)}, u32[]{:S(2)}) collective-permute-start(bf16[64,3072]{1,0:T(8,128)(2,1)S(1)} %collective-permute-done.3.refs_1_), channel_id=1, source_target_pairs={{0,1},{1,2},{2,3},{3,0},{4,5},{5,6},{6,7},{7,4},{8,9},{9,10},{10,1... | collective-permute-start | bytes 1179656 | tf_op jit(solution)/shard_map/ppermute | solution.py:24
  56.4 10.5 %collective-permute-start.5 = (bf16[64,3072]{1,0:T(8,128)(2,1)S(1)}, bf16[64,3072]{1,0:T(8,128)(2,1)S(1)}, u32[]{:S(2)}, u32[]{:S(2)}) collective-permute-start(bf16[64,3072]{1,0:T(8,128)(2,1)S(1)} %get-tuple-element.13), channel_id=1, source_target_pairs={{0,3},{1,0},{2,1},{3,2},{4,7},{5,4},{6,5},{7,6},{8,11},{9,8},{10,9... | collective-permute-start | bytes 1179656 | tf_op jit(solution)/shard_map/ppermute | solution.py:24
  58.3 19.1 %collective-permute-start.6 = (bf16[64,3072]{1,0:T(8,128)(2,1)S(1)}, bf16[64,3072]{1,0:T(8,128)(2,1)S(1)}, u32[]{:S(2)}, u32[]{:S(2)}) collective-permute-start(bf16[64,3072]{1,0:T(8,128)(2,1)S(1)} %get-tuple-element.14), channel_id=1, source_target_pairs={{0,1},{1,2},{2,3},{3,0},{4,5},{5,6},{6,7},{7,4},{8,9},{9,10},{10,1... | collective-permute-start | bytes 1179656 | tf_op jit(solution)/shard_map/ppermute | solution.py:24
  65.0 13.7 %collective-permute-start.8 = (bf16[64,3072]{1,0:T(8,128)(2,1)S(1)}, bf16[64,3072]{1,0:T(8,128)(2,1)S(1)}, u32[]{:S(2)}, u32[]{:S(2)}) collective-permute-start(bf16[64,3072]{1,0:T(8,128)(2,1)S(1)} %shard_map.50), channel_id=1, source_target_pairs={{0,2},{1,3},{2,0},{3,1},{4,6},{5,7},{6,4},{7,5},{8,10},{9,11},{10,... | collective-permute-start | bytes 1179656 | tf_op jit(solution)/shard_map/ppermute | solution.py:24
  78.9 18.4 %collective-permute-start.9 = (bf16[16,3072]{1,0:T(8,128)(2,1)S(1)}, bf16[16,3072]{1,0:T(8,128)(2,1)S(1)}, u32[]{:S(2)}, u32[]{:S(2)}) collective-permute-start(bf16[16,3072]{1,0:T(8,128)(2,1)S(1)} %get-tuple-element.16), channel_id=1, source_target_pairs={{0,12},{1,13},{2,14},{3,15},{4,0},{5,1},{6,2},{7,3},{8,4},{9,5},{1... | collective-permute-start | bytes 294920 | tf_op jit(solution)/shard_map/ppermute | solution.py:24
  81.8 18.9 %collective-permute-start.10 = (bf16[16,3072]{1,0:T(8,128)(2,1)S(1)}, bf16[16,3072]{1,0:T(8,128)(2,1)S(1)}, u32[]{:S(2)}, u32[]{:S(2)}) collective-permute-start(bf16[16,3072]{1,0:T(8,128)(2,1)S(1)} %get-tuple-element.17), channel_id=1, source_target_pairs={{0,4},{1,5},{2,6},{3,7},{4,8},{5,9},{6,10},{7,11},{8,12},{9,13},{1... | collective-permute-start | bytes 294920 | tf_op jit(solution)/shard_map/ppermute | solution.py:24
  90.2 16.9 %collective-permute-start.11 = (bf16[16,3072]{1,0:T(8,128)(2,1)S(1)}, bf16[16,3072]{1,0:T(8,128)(2,1)S(1)}, u32[]{:S(2)}, u32[]{:S(2)}) collective-permute-start(bf16[16,3072]{1,0:T(8,128)(2,1)S(1)} %get-tuple-element.18), channel_id=1, source_target_pairs={{0,8},{1,9},{2,10},{3,11},{4,12},{5,13},{6,14},{7,15},{8,0},{9,1},... | collective-permute-start | bytes 294920 | tf_op jit(solution)/shard_map/ppermute | solution.py:24

commit v6 on v5

--- a/solution.py
+++ b/solution.py
@@ -132,7 +132,7 @@
     own, near, far, opposite = add([own, near, far, opposite], 4)
     opposite = along_z(opposite, step=2)
     near, far = along_z(near, step=-1), along_z(far, step=1)
-    return add([tokens, own, near, far, opposite])[0]
+    return add([tokens, own, opposite, near, far])[0]
 
 
 def solution(mesh):

time: 110 us -> 108 us (0.982)
  waiting for transfers between devices: 26.3 us -> 25 us
    ppermute x12, waiting for transfers between devices: 26.3 us -> 25 us  [shift(): return lax.ppermute(value, ('dp', 'mp'), pairs)]
where the time goes in v6:
time: 108 us; the launch traced here: 107 us
  starting transfers between devices  69.4 us (64%)
  waiting for transfers between devices  25 us (23%)
  local copies, waits for them, and re-layouts  6.27 us (6%)
  Pallas kernels  5.62 us (5%)
    ppermute x12, starting transfers between devices, shift(): return lax.ppermute(value, ('dp', 'mp'), pairs)  69.4 us
    ppermute x12, waiting for transfers between devices, shift(): return lax.ppermute(value, ('dp', 'mp'), pairs)  25 us
    unnamed x12, local copies, waits for them, and re-layouts  6.27 us
    pallas_call x7, Pallas kernels, call(): pl.pallas_call(body, out_shape=outs, in_specs=specs or [VMEM] * len(args)...  5.62 us
  transfers between devices with their start and end apart: 12, of which 5 were waited for; matrix products, arithmetic and copies ran while one was open for 0% of the time, Pallas kernels for 4%

profile of v6, /device:TPU:1, one launch (start us, length us, event | category | flops | bytes accessed | tf_op | source)
XLA Modules:
  0.0 106.5 jit_solution(16268419052045640863)
XLA Ops:
  0.0 0.0 copy-start.4
  0.0 0.9 copy-done.4
  0.9 0.0 copy-start.5
  0.9 0.7 copy-done.5
  1.6 0.2 shard_map.46.after.refs_0_
  1.8 18.7 %collective-permute-start = (bf16[16,3072]{1,0:T(8,128)(2,1)S(1)}, bf16[16,3072]{1,0:T(8,128)(2,1)S(1)}, u32[]{:S(2)}, u32[]{:S(2)}) collective-permute-start(bf16[16,3072]{1,0:T(8,128)(2,1)S(1)} %shard_map.46.after.refs_0_), channel_id=1, source_target_pairs={{0,4},{1,5},{2,6},{3,7},{4,8},{5,9},{6,10},{7,11},{8,12},{9,13},{1... | collective-permute-start | bytes 294920 | tf_op jit(solution)/shard_map/ppermute | solution.py:24
  20.6 1.9 %collective-permute-start.1 = (bf16[16,3072]{1,0:T(8,128)(2,1)S(1)}, bf16[16,3072]{1,0:T(8,128)(2,1)S(1)}, u32[]{:S(2)}, u32[]{:S(2)}) collective-permute-start(bf16[16,3072]{1,0:T(8,128)(2,1)S(1)} %shard_map.46.after.refs_0_), channel_id=1, source_target_pairs={{0,12},{1,13},{2,14},{3,15},{4,0},{5,1},{6,2},{7,3},{8,4},{9,5},{1... | collective-permute-start | bytes 294920 | tf_op jit(solution)/shard_map/ppermute | solution.py:24
  22.5 0.0 collective-permute-done.refs_1_
  22.5 11.4 %collective-permute-start.2 = (bf16[16,3072]{1,0:T(8,128)(2,1)S(1)}, bf16[16,3072]{1,0:T(8,128)(2,1)S(1)}, u32[]{:S(2)}, u32[]{:S(2)}) collective-permute-start(bf16[16,3072]{1,0:T(8,128)(2,1)S(1)} %collective-permute-done.refs_1_), channel_id=1, source_target_pairs={{0,4},{1,5},{2,6},{3,7},{4,8},{5,9},{6,10},{7,11},{8,12},{9,13},{1... | collective-permute-start | bytes 294920 | tf_op jit(solution)/shard_map/ppermute | solution.py:24
  33.9 0.0 copy-start
  33.9 2.3 %copy-done = bf16[3072,768]{1,0:T(8,128)(2,1)S(1)} copy-done((bf16[3072,768]{1,0:T(8,128)(2,1)S(1)}, bf16[3072,768]{1,0:T(8,128)(2,1)}, u32[]{:S(2)}) %copy-start) | copy-done | bytes 4718616
  36.2 0.0 copy-start.2
  36.2 2.3 %copy-done.2 = bf16[768,3072]{1,0:T(8,128)(2,1)S(1)} copy-done((bf16[768,3072]{1,0:T(8,128)(2,1)S(1)}, bf16[768,3072]{1,0:T(8,128)(2,1)}, u32[]{:S(2)}) %copy-start.2) | copy-done | bytes 4718616
  38.6 0.0 copy-start.1
  38.6 0.0 copy-start.3
  38.6 0.0 collective-permute-done.1.refs_2_
  38.6 0.0 collective-permute-done.2.refs_3_
  38.6 3.9 %collective-permute-start.3 = (bf16[64,3072]{1,0:T(8,128)(2,1)S(1)}, bf16[64,3072]{1,0:T(8,128)(2,1)S(1)}, u32[]{:S(2)}, u32[]{:S(2)}) collective-permute-start(bf16[64,3072]{1,0:T(8,128)(2,1)S(1)} %shard_map.48.refs_0_), channel_id=1, source_target_pairs={{0,1},{1,2},{2,3},{3,0},{4,5},{5,6},{6,7},{7,4},{8,9},{9,10},{10,1... | collective-permute-start | bytes 1179656 | tf_op jit(solution)/shard_map/ppermute | solution.py:24
  42.5 1.9 %collective-permute-start.4 = (bf16[64,3072]{1,0:T(8,128)(2,1)S(1)}, bf16[64,3072]{1,0:T(8,128)(2,1)S(1)}, u32[]{:S(2)}, u32[]{:S(2)}) collective-permute-start(bf16[64,3072]{1,0:T(8,128)(2,1)S(1)} %shard_map.48.refs_0_), channel_id=1, source_target_pairs={{0,3},{1,0},{2,1},{3,2},{4,7},{5,4},{6,5},{7,6},{8,11},{9,8},{10,9... | collective-permute-start | bytes 1179656 | tf_op jit(solution)/shard_map/ppermute | solution.py:24
  44.5 4.7 %collective-permute-done.3.refs_1_ = bf16[64,3072]{1,0:T(8,128)(2,1)S(1)} collective-permute-done((bf16[64,3072]{1,0:T(8,128)(2,1)S(1)}, bf16[64,3072]{1,0:T(8,128)(2,1)S(1)}, u32[]{:S(2)}, u32[]{:S(2)}) %collective-permute-start.3) | collective-permute-done | bytes 393248 | tf_op jit(solution)/shard_map/ppermute | solution.py:24
  49.1 4.8 %collective-permute-start.7 = (bf16[64,3072]{1,0:T(8,128)(2,1)S(1)}, bf16[64,3072]{1,0:T(8,128)(2,1)S(1)}, u32[]{:S(2)}, u32[]{:S(2)}) collective-permute-start(bf16[64,3072]{1,0:T(8,128)(2,1)S(1)} %collective-permute-done.3.refs_1_), channel_id=1, source_target_pairs={{0,1},{1,2},{2,3},{3,0},{4,5},{5,6},{6,7},{7,4},{8,9},{9,10},{10,1... | collective-permute-start | bytes 1179656 | tf_op jit(solution)/shard_map/ppermute | solution.py:24
  53.9 0.0 collective-permute-done.4.refs_2_
  53.9 0.0 copy-done.1
  54.0 0.0 copy-done.3
  54.0 2.4 %shard_map.49 = (bf16[64,3072]{1,0:T(8,128)(2,1)S(1)}, bf16[64,3072]{1,0:T(8,128)(2,1)S(1)}, bf16[64,3072]{1,0:T(8,128)(2,1)S(1)}) custom-call(bf16[64,3072]{1,0:T(8,128)(2,1)S(1)} %shard_map.48.refs_0_, bf16[64,3072]{1,0:T(8,128)(2,1)S(1)} %collective-permute-done.3.refs_1_, bf16[64,3072]{1,0:T(8,128)(2,1)S(1)} %collective-permute-done.4.refs_2_, ...), custom_call_target="tpu_custom_call" | custom-call | flops 1811939328 | bytes 11798528 | tf_op jit(solution)/shard_map/pallas_call | solution.py:31
  56.4 1.9 %collective-permute-start.5 = (bf16[64,3072]{1,0:T(8,128)(2,1)S(1)}, bf16[64,3072]{1,0:T(8,128)(2,1)S(1)}, u32[]{:S(2)}, u32[]{:S(2)}) collective-permute-start(bf16[64,3072]{1,0:T(8,128)(2,1)S(1)} %get-tuple-element.13), channel_id=1, source_target_pairs={{0,3},{1,0},{2,1},{3,2},{4,7},{5,4},{6,5},{7,6},{8,11},{9,8},{10,9... | collective-permute-start | bytes 1179656 | tf_op jit(solution)/shard_map/ppermute | solution.py:24
  58.3 4.6 %collective-permute-start.6 = (bf16[64,3072]{1,0:T(8,128)(2,1)S(1)}, bf16[64,3072]{1,0:T(8,128)(2,1)S(1)}, u32[]{:S(2)}, u32[]{:S(2)}) collective-permute-start(bf16[64,3072]{1,0:T(8,128)(2,1)S(1)} %get-tuple-element.14), channel_id=1, source_target_pairs={{0,1},{1,2},{2,3},{3,0},{4,5},{5,6},{6,7},{7,4},{8,9},{9,10},{10,1... | collective-permute-start | bytes 1179656 | tf_op jit(solution)/shard_map/ppermute | solution.py:24
  62.9 0.0 collective-permute-done.7.refs_0_
  62.9 2.0 %shard_map.50 = bf16[64,3072]{1,0:T(8,128)(2,1)S(1)} custom-call(bf16[64,3072]{1,0:T(8,128)(2,1)S(1)} %collective-permute-done.7.refs_0_, bf16[3072,768]{1,0:T(8,128)(2,1)S(1)} %copy-done.1, bf16[768,3072]{1,0:T(8,128)(2,1)S(1)} %copy-done.3, bf16[64,3072]{1,0:T(8,128)(2,1)S(1)} %get-tuple-element.12.refs_3_.refs_0_), custom_call_target="tpu_custom_call" | custom-call | flops 603979776 | bytes 10616832 | tf_op jit(solution)/shard_map/pallas_call | solution.py:31
  65.0 1.9 %collective-permute-start.8 = (bf16[64,3072]{1,0:T(8,128)(2,1)S(1)}, bf16[64,3072]{1,0:T(8,128)(2,1)S(1)}, u32[]{:S(2)}, u32[]{:S(2)}) collective-permute-start(bf16[64,3072]{1,0:T(8,128)(2,1)S(1)} %shard_map.50), channel_id=1, source_target_pairs={{0,2},{1,3},{2,0},{3,1},{4,6},{5,7},{6,4},{7,5},{8,10},{9,11},{10,... | collective-permute-start | bytes 1179656 | tf_op jit(solution)/shard_map/ppermute | solution.py:24
  66.9 0.0 collective-permute-done.5.refs_1_
  66.9 10.5 %collective-permute-done.6.refs_2_ = bf16[64,3072]{1,0:T(8,128)(2,1)S(1)} collective-permute-done((bf16[64,3072]{1,0:T(8,128)(2,1)S(1)}, bf16[64,3072]{1,0:T(8,128)(2,1)S(1)}, u32[]{:S(2)}, u32[]{:S(2)}) %collective-permute-start.6) | collective-permute-done | bytes 393248 | tf_op jit(solution)/shard_map/ppermute | solution.py:24
  77.4 1.3 %collective-permute-done.8.refs_3_ = bf16[64,3072]{1,0:T(8,128)(2,1)S(1)} collective-permute-done((bf16[64,3072]{1,0:T(8,128)(2,1)S(1)}, bf16[64,3072]{1,0:T(8,128)(2,1)S(1)}, u32[]{:S(2)}, u32[]{:S(2)}) %collective-permute-start.8) | collective-permute-done | bytes 393248 | tf_op jit(solution)/shard_map/ppermute | solution.py:24
  78.7 0.2 shard_map.51
  78.9 6.6 %collective-permute-start.9 = (bf16[16,3072]{1,0:T(8,128)(2,1)S(1)}, bf16[16,3072]{1,0:T(8,128)(2,1)S(1)}, u32[]{:S(2)}, u32[]{:S(2)}) collective-permute-start(bf16[16,3072]{1,0:T(8,128)(2,1)S(1)} %get-tuple-element.16), channel_id=1, source_target_pairs={{0,8},{1,9},{2,10},{3,11},{4,12},{5,13},{6,14},{7,15},{8,0},{9,1},... | collective-permute-start | bytes 294920 | tf_op jit(solution)/shard_map/ppermute | solution.py:24
  85.4 9.9 %collective-permute-start.10 = (bf16[16,3072]{1,0:T(8,128)(2,1)S(1)}, bf16[16,3072]{1,0:T(8,128)(2,1)S(1)}, u32[]{:S(2)}, u32[]{:S(2)}) collective-permute-start(bf16[16,3072]{1,0:T(8,128)(2,1)S(1)} %get-tuple-element.17), channel_id=1, source_target_pairs={{0,12},{1,13},{2,14},{3,15},{4,0},{5,1},{6,2},{7,3},{8,4},{9,5},{1... | collective-permute-start | bytes 294920 | tf_op jit(solution)/shard_map/ppermute | solution.py:24
  95.3 1.9 %collective-permute-start.11 = (bf16[16,3072]{1,0:T(8,128)(2,1)S(1)}, bf16[16,3072]{1,0:T(8,128)(2,1)S(1)}, u32[]{:S(2)}, u32[]{:S(2)}) collective-permute-start(bf16[16,3072]{1,0:T(8,128)(2,1)S(1)} %get-tuple-element.18), channel_id=1, source_target_pairs={{0,4},{1,5},{2,6},{3,7},{4,8},{5,9},{6,10},{7,11},{8,12},{9,13},{1... | collective-permute-start | bytes 294920 | tf_op jit(solution)/shard_map/ppermute | solution.py:24
  97.2 0.0 collective-permute-done.9.refs_2_
  97.2 0.4 collective-permute-done.10.refs_3_
  97.6 8.2 %collective-permute-done.11.refs_4_ = bf16[16,3072]{1,0:T(8,128)(2,1)S(1)} collective-permute-done((bf16[16,3072]{1,0:T(8,128)(2,1)S(1)}, bf16[16,3072]{1,0:T(8,128)(2,1)S(1)}, u32[]{:S(2)}, u32[]{:S(2)}) %collective-permute-start.11) | collective-permute-done | bytes 98336 | tf_op jit(solution)/shard_map/ppermute | solution.py:24
  105.8 0.7 shard_map.52
  (2 shorter events, 0.0 us)
Async XLA Ops:
  0.0 0.9 copy-start.4
  0.9 0.7 copy-start.5
  1.8 20.7 %collective-permute-start = (bf16[16,3072]{1,0:T(8,128)(2,1)S(1)}, bf16[16,3072]{1,0:T(8,128)(2,1)S(1)}, u32[]{:S(2)}, u32[]{:S(2)}) collective-permute-start(bf16[16,3072]{1,0:T(8,128)(2,1)S(1)} %shard_map.46.after.refs_0_), channel_id=1, source_target_pairs={{0,4},{1,5},{2,6},{3,7},{4,8},{5,9},{6,10},{7,11},{8,12},{9,13},{1... | collective-permute-start | bytes 294920 | tf_op jit(solution)/shard_map/ppermute | solution.py:24
  20.6 18.0 %collective-permute-start.1 = (bf16[16,3072]{1,0:T(8,128)(2,1)S(1)}, bf16[16,3072]{1,0:T(8,128)(2,1)S(1)}, u32[]{:S(2)}, u32[]{:S(2)}) collective-permute-start(bf16[16,3072]{1,0:T(8,128)(2,1)S(1)} %shard_map.46.after.refs_0_), channel_id=1, source_target_pairs={{0,12},{1,13},{2,14},{3,15},{4,0},{5,1},{6,2},{7,3},{8,4},{9,5},{1... | collective-permute-start | bytes 294920 | tf_op jit(solution)/shard_map/ppermute | solution.py:24
  22.5 16.1 %collective-permute-start.2 = (bf16[16,3072]{1,0:T(8,128)(2,1)S(1)}, bf16[16,3072]{1,0:T(8,128)(2,1)S(1)}, u32[]{:S(2)}, u32[]{:S(2)}) collective-permute-start(bf16[16,3072]{1,0:T(8,128)(2,1)S(1)} %collective-permute-done.refs_1_), channel_id=1, source_target_pairs={{0,4},{1,5},{2,6},{3,7},{4,8},{5,9},{6,10},{7,11},{8,12},{9,13},{1... | collective-permute-start | bytes 294920 | tf_op jit(solution)/shard_map/ppermute | solution.py:24
  33.9 2.3 %copy-start = (bf16[3072,768]{1,0:T(8,128)(2,1)S(1)}, bf16[3072,768]{1,0:T(8,128)(2,1)}, u32[]{:S(2)}) copy-start(bf16[3072,768]{1,0:T(8,128)(2,1)} %refs_1_.1) | copy-start | bytes 14155780
  36.2 2.3 %copy-start.2 = (bf16[768,3072]{1,0:T(8,128)(2,1)S(1)}, bf16[768,3072]{1,0:T(8,128)(2,1)}, u32[]{:S(2)}) copy-start(bf16[768,3072]{1,0:T(8,128)(2,1)} %refs_2_.1) | copy-start | bytes 14155780
  38.6 15.4 %copy-start.1 = (bf16[3072,768]{1,0:T(8,128)(2,1)S(1)}, bf16[3072,768]{1,0:T(8,128)(2,1)}, u32[]{:S(2)}) copy-start(bf16[3072,768]{1,0:T(8,128)(2,1)} %refs_1_.1) | copy-start | bytes 14155780
  38.6 15.4 %copy-start.3 = (bf16[768,3072]{1,0:T(8,128)(2,1)S(1)}, bf16[768,3072]{1,0:T(8,128)(2,1)}, u32[]{:S(2)}) copy-start(bf16[768,3072]{1,0:T(8,128)(2,1)} %refs_2_.1) | copy-start | bytes 14155780
  38.6 10.5 %collective-permute-start.3 = (bf16[64,3072]{1,0:T(8,128)(2,1)S(1)}, bf16[64,3072]{1,0:T(8,128)(2,1)S(1)}, u32[]{:S(2)}, u32[]{:S(2)}) collective-permute-start(bf16[64,3072]{1,0:T(8,128)(2,1)S(1)} %shard_map.48.refs_0_), channel_id=1, source_target_pairs={{0,1},{1,2},{2,3},{3,0},{4,5},{5,6},{6,7},{7,4},{8,9},{9,10},{10,1... | collective-permute-start | bytes 1179656 | tf_op jit(solution)/shard_map/ppermute | solution.py:24
  42.5 11.4 %collective-permute-start.4 = (bf16[64,3072]{1,0:T(8,128)(2,1)S(1)}, bf16[64,3072]{1,0:T(8,128)(2,1)S(1)}, u32[]{:S(2)}, u32[]{:S(2)}) collective-permute-start(bf16[64,3072]{1,0:T(8,128)(2,1)S(1)} %shard_map.48.refs_0_), channel_id=1, source_target_pairs={{0,3},{1,0},{2,1},{3,2},{4,7},{5,4},{6,5},{7,6},{8,11},{9,8},{10,9... | collective-permute-start | bytes 1179656 | tf_op jit(solution)/shard_map/ppermute | solution.py:24
  49.1 13.8 %collective-permute-start.7 = (bf16[64,3072]{1,0:T(8,128)(2,1)S(1)}, bf16[64,3072]{1,0:T(8,128)(2,1)S(1)}, u32[]{:S(2)}, u32[]{:S(2)}) collective-permute-start(bf16[64,3072]{1,0:T(8,128)(2,1)S(1)} %collective-permute-done.3.refs_1_), channel_id=1, source_target_pairs={{0,1},{1,2},{2,3},{3,0},{4,5},{5,6},{6,7},{7,4},{8,9},{9,10},{10,1... | collective-permute-start | bytes 1179656 | tf_op jit(solution)/shard_map/ppermute | solution.py:24
  56.4 10.5 %collective-permute-start.5 = (bf16[64,3072]{1,0:T(8,128)(2,1)S(1)}, bf16[64,3072]{1,0:T(8,128)(2,1)S(1)}, u32[]{:S(2)}, u32[]{:S(2)}) collective-permute-start(bf16[64,3072]{1,0:T(8,128)(2,1)S(1)} %get-tuple-element.13), channel_id=1, source_target_pairs={{0,3},{1,0},{2,1},{3,2},{4,7},{5,4},{6,5},{7,6},{8,11},{9,8},{10,9... | collective-permute-start | bytes 1179656 | tf_op jit(solution)/shard_map/ppermute | solution.py:24
  58.3 19.1 %collective-permute-start.6 = (bf16[64,3072]{1,0:T(8,128)(2,1)S(1)}, bf16[64,3072]{1,0:T(8,128)(2,1)S(1)}, u32[]{:S(2)}, u32[]{:S(2)}) collective-permute-start(bf16[64,3072]{1,0:T(8,128)(2,1)S(1)} %get-tuple-element.14), channel_id=1, source_target_pairs={{0,1},{1,2},{2,3},{3,0},{4,5},{5,6},{6,7},{7,4},{8,9},{9,10},{10,1... | collective-permute-start | bytes 1179656 | tf_op jit(solution)/shard_map/ppermute | solution.py:24
  65.0 13.7 %collective-permute-start.8 = (bf16[64,3072]{1,0:T(8,128)(2,1)S(1)}, bf16[64,3072]{1,0:T(8,128)(2,1)S(1)}, u32[]{:S(2)}, u32[]{:S(2)}) collective-permute-start(bf16[64,3072]{1,0:T(8,128)(2,1)S(1)} %shard_map.50), channel_id=1, source_target_pairs={{0,2},{1,3},{2,0},{3,1},{4,6},{5,7},{6,4},{7,5},{8,10},{9,11},{10,... | collective-permute-start | bytes 1179656 | tf_op jit(solution)/shard_map/ppermute | solution.py:24
  78.9 18.4 %collective-permute-start.9 = (bf16[16,3072]{1,0:T(8,128)(2,1)S(1)}, bf16[16,3072]{1,0:T(8,128)(2,1)S(1)}, u32[]{:S(2)}, u32[]{:S(2)}) collective-permute-start(bf16[16,3072]{1,0:T(8,128)(2,1)S(1)} %get-tuple-element.16), channel_id=1, source_target_pairs={{0,8},{1,9},{2,10},{3,11},{4,12},{5,13},{6,14},{7,15},{8,0},{9,1},... | collective-permute-start | bytes 294920 | tf_op jit(solution)/shard_map/ppermute | solution.py:24
  85.4 12.2 %collective-permute-start.10 = (bf16[16,3072]{1,0:T(8,128)(2,1)S(1)}, bf16[16,3072]{1,0:T(8,128)(2,1)S(1)}, u32[]{:S(2)}, u32[]{:S(2)}) collective-permute-start(bf16[16,3072]{1,0:T(8,128)(2,1)S(1)} %get-tuple-element.17), channel_id=1, source_target_pairs={{0,12},{1,13},{2,14},{3,15},{4,0},{5,1},{6,2},{7,3},{8,4},{9,5},{1... | collective-permute-start | bytes 294920 | tf_op jit(solution)/shard_map/ppermute | solution.py:24
  95.3 10.5 %collective-permute-start.11 = (bf16[16,3072]{1,0:T(8,128)(2,1)S(1)}, bf16[16,3072]{1,0:T(8,128)(2,1)S(1)}, u32[]{:S(2)}, u32[]{:S(2)}) collective-permute-start(bf16[16,3072]{1,0:T(8,128)(2,1)S(1)} %get-tuple-element.18), channel_id=1, source_target_pairs={{0,4},{1,5},{2,6},{3,7},{4,8},{5,9},{6,10},{7,11},{8,12},{9,13},{1... | collective-permute-start | bytes 294920 | tf_op jit(solution)/shard_map/ppermute | solution.py:24

commit v7 on v6

--- a/solution.py
+++ b/solution.py
@@ -120,7 +120,7 @@
         normalize_body, [jax.ShapeDtypeStruct(tokens.shape, jnp.bfloat16)], (tokens, ln_gain[None, :])
     )
     near, far = along_z(own, step=1), along_z(own, step=-1)
-    opposite = along_z(near, step=1)
+    opposite = along_z(own, step=2)
     held = ready(w_in, w_out, own)
     own = stack([own, near, far, opposite], held)
     near, far = along_x(own, step=1), along_x(own, step=-1)

time: 108 us -> 113 us (1.046)
  waiting for transfers between devices: 25 us -> 33 us
  starting transfers between devices: 69.4 us -> 67.4 us
    ppermute x12, waiting for transfers between devices: 25 us -> 33 us  [shift(): return lax.ppermute(value, ('dp', 'mp'), pairs)]
    ppermute x12, starting transfers between devices: 69.4 us -> 67.4 us  [shift(): return lax.ppermute(value, ('dp', 'mp'), pairs)]
  transfers between devices with their start and end apart: 12 -> 12, of which waited for: 5 -> 6; matrix products, arithmetic and copies ran while one was open for 0% -> 0% of each run, Pallas kernels for 4% -> 4%
where the time goes in v7:
time: 113 us; the launch traced here: 112 us
  starting transfers between devices  67.4 us (60%)
  waiting for transfers between devices  33 us (29%)
  local copies, waits for them, and re-layouts  6.27 us (6%)
  Pallas kernels  5.62 us (5%)
    ppermute x12, starting transfers between devices, shift(): return lax.ppermute(value, ('dp', 'mp'), pairs)  67.4 us
    ppermute x12, waiting for transfers between devices, shift(): return lax.ppermute(value, ('dp', 'mp'), pairs)  33 us
    unnamed x12, local copies, waits for them, and re-layouts  6.27 us
    pallas_call x7, Pallas kernels, call(): pl.pallas_call(body, out_shape=outs, in_specs=specs or [VMEM] * len(args)...  5.62 us
  transfers between devices with their start and end apart: 12, of which 6 were waited for; matrix products, arithmetic and copies ran while one was open for 0% of the time, Pallas kernels for 4%

profile of v7, /device:TPU:1, one launch (start us, length us, event | category | flops | bytes accessed | tf_op | source)
XLA Modules:
  0.0 112.5 jit_solution(9627240687306347002)
XLA Ops:
  0.0 0.0 copy-start.4
  0.0 0.9 copy-done.4
  0.9 0.0 copy-start.5
  0.9 0.7 copy-done.5
  1.6 0.2 shard_map.46.after.refs_0_
  1.8 19.9 %collective-permute-start.2 = (bf16[16,3072]{1,0:T(8,128)(2,1)S(1)}, bf16[16,3072]{1,0:T(8,128)(2,1)S(1)}, u32[]{:S(2)}, u32[]{:S(2)}) collective-permute-start(bf16[16,3072]{1,0:T(8,128)(2,1)S(1)} %shard_map.46.after.refs_0_), channel_id=1, source_target_pairs={{0,8},{1,9},{2,10},{3,11},{4,12},{5,13},{6,14},{7,15},{8,0},{9,1},... | collective-permute-start | bytes 294920 | tf_op jit(solution)/shard_map/ppermute | solution.py:24
  21.8 5.8 %collective-permute-start.1 = (bf16[16,3072]{1,0:T(8,128)(2,1)S(1)}, bf16[16,3072]{1,0:T(8,128)(2,1)S(1)}, u32[]{:S(2)}, u32[]{:S(2)}) collective-permute-start(bf16[16,3072]{1,0:T(8,128)(2,1)S(1)} %shard_map.46.after.refs_0_), channel_id=1, source_target_pairs={{0,12},{1,13},{2,14},{3,15},{4,0},{5,1},{6,2},{7,3},{8,4},{9,5},{1... | collective-permute-start | bytes 294920 | tf_op jit(solution)/shard_map/ppermute | solution.py:24
  27.6 3.4 %collective-permute-start = (bf16[16,3072]{1,0:T(8,128)(2,1)S(1)}, bf16[16,3072]{1,0:T(8,128)(2,1)S(1)}, u32[]{:S(2)}, u32[]{:S(2)}) collective-permute-start(bf16[16,3072]{1,0:T(8,128)(2,1)S(1)} %shard_map.46.after.refs_0_), channel_id=1, source_target_pairs={{0,4},{1,5},{2,6},{3,7},{4,8},{5,9},{6,10},{7,11},{8,12},{9,13},{1... | collective-permute-start | bytes 294920 | tf_op jit(solution)/shard_map/ppermute | solution.py:24
  31.0 0.0 copy-start
  31.0 2.3 %copy-done = bf16[3072,768]{1,0:T(8,128)(2,1)S(1)} copy-done((bf16[3072,768]{1,0:T(8,128)(2,1)S(1)}, bf16[3072,768]{1,0:T(8,128)(2,1)}, u32[]{:S(2)}) %copy-start) | copy-done | bytes 4718616
  33.3 0.0 copy-start.2
  33.3 2.3 %copy-done.2 = bf16[768,3072]{1,0:T(8,128)(2,1)S(1)} copy-done((bf16[768,3072]{1,0:T(8,128)(2,1)S(1)}, bf16[768,3072]{1,0:T(8,128)(2,1)}, u32[]{:S(2)}) %copy-start.2) | copy-done | bytes 4718616
  35.6 0.0 copy-start.1
  35.6 0.0 copy-start.3
  35.7 0.0 collective-permute-done.2.refs_3_
  35.7 0.0 collective-permute-done.1.refs_2_
  35.7 3.3 %collective-permute-done.refs_1_ = bf16[16,3072]{1,0:T(8,128)(2,1)S(1)} collective-permute-done((bf16[16,3072]{1,0:T(8,128)(2,1)S(1)}, bf16[16,3072]{1,0:T(8,128)(2,1)S(1)}, u32[]{:S(2)}, u32[]{:S(2)}) %collective-permute-start) | collective-permute-done | bytes 98336 | tf_op jit(solution)/shard_map/ppermute | solution.py:24
  39.0 4.4 %collective-permute-start.3 = (bf16[64,3072]{1,0:T(8,128)(2,1)S(1)}, bf16[64,3072]{1,0:T(8,128)(2,1)S(1)}, u32[]{:S(2)}, u32[]{:S(2)}) collective-permute-start(bf16[64,3072]{1,0:T(8,128)(2,1)S(1)} %shard_map.48.refs_0_), channel_id=1, source_target_pairs={{0,1},{1,2},{2,3},{3,0},{4,5},{5,6},{6,7},{7,4},{8,9},{9,10},{10,1... | collective-permute-start | bytes 1179656 | tf_op jit(solution)/shard_map/ppermute | solution.py:24
  43.4 1.9 %collective-permute-start.4 = (bf16[64,3072]{1,0:T(8,128)(2,1)S(1)}, bf16[64,3072]{1,0:T(8,128)(2,1)S(1)}, u32[]{:S(2)}, u32[]{:S(2)}) collective-permute-start(bf16[64,3072]{1,0:T(8,128)(2,1)S(1)} %shard_map.48.refs_0_), channel_id=1, source_target_pairs={{0,3},{1,0},{2,1},{3,2},{4,7},{5,4},{6,5},{7,6},{8,11},{9,8},{10,9... | collective-permute-start | bytes 1179656 | tf_op jit(solution)/shard_map/ppermute | solution.py:24
  45.3 4.4 %collective-permute-done.3.refs_1_ = bf16[64,3072]{1,0:T(8,128)(2,1)S(1)} collective-permute-done((bf16[64,3072]{1,0:T(8,128)(2,1)S(1)}, bf16[64,3072]{1,0:T(8,128)(2,1)S(1)}, u32[]{:S(2)}, u32[]{:S(2)}) %collective-permute-start.3) | collective-permute-done | bytes 393248 | tf_op jit(solution)/shard_map/ppermute | solution.py:24
  49.8 5.3 %collective-permute-start.7 = (bf16[64,3072]{1,0:T(8,128)(2,1)S(1)}, bf16[64,3072]{1,0:T(8,128)(2,1)S(1)}, u32[]{:S(2)}, u32[]{:S(2)}) collective-permute-start(bf16[64,3072]{1,0:T(8,128)(2,1)S(1)} %collective-permute-done.3.refs_1_), channel_id=1, source_target_pairs={{0,1},{1,2},{2,3},{3,0},{4,5},{5,6},{6,7},{7,4},{8,9},{9,10},{10,1... | collective-permute-start | bytes 1179656 | tf_op jit(solution)/shard_map/ppermute | solution.py:24
  55.1 0.0 collective-permute-done.4.refs_2_
  55.1 0.0 copy-done.1
  55.1 0.0 copy-done.3
  55.1 2.4 %shard_map.49 = (bf16[64,3072]{1,0:T(8,128)(2,1)S(1)}, bf16[64,3072]{1,0:T(8,128)(2,1)S(1)}, bf16[64,3072]{1,0:T(8,128)(2,1)S(1)}) custom-call(bf16[64,3072]{1,0:T(8,128)(2,1)S(1)} %shard_map.48.refs_0_, bf16[64,3072]{1,0:T(8,128)(2,1)S(1)} %collective-permute-done.3.refs_1_, bf16[64,3072]{1,0:T(8,128)(2,1)S(1)} %collective-permute-done.4.refs_2_, ...), custom_call_target="tpu_custom_call" | custom-call | flops 1811939328 | bytes 11798528 | tf_op jit(solution)/shard_map/pallas_call | solution.py:31
  57.5 1.9 %collective-permute-start.5 = (bf16[64,3072]{1,0:T(8,128)(2,1)S(1)}, bf16[64,3072]{1,0:T(8,128)(2,1)S(1)}, u32[]{:S(2)}, u32[]{:S(2)}) collective-permute-start(bf16[64,3072]{1,0:T(8,128)(2,1)S(1)} %get-tuple-element.13), channel_id=1, source_target_pairs={{0,3},{1,0},{2,1},{3,2},{4,7},{5,4},{6,5},{7,6},{8,11},{9,8},{10,9... | collective-permute-start | bytes 1179656 | tf_op jit(solution)/shard_map/ppermute | solution.py:24
  59.5 4.6 %collective-permute-start.6 = (bf16[64,3072]{1,0:T(8,128)(2,1)S(1)}, bf16[64,3072]{1,0:T(8,128)(2,1)S(1)}, u32[]{:S(2)}, u32[]{:S(2)}) collective-permute-start(bf16[64,3072]{1,0:T(8,128)(2,1)S(1)} %get-tuple-element.14), channel_id=1, source_target_pairs={{0,1},{1,2},{2,3},{3,0},{4,5},{5,6},{6,7},{7,4},{8,9},{9,10},{10,1... | collective-permute-start | bytes 1179656 | tf_op jit(solution)/shard_map/ppermute | solution.py:24
  64.0 0.0 collective-permute-done.7.refs_0_
  64.1 2.0 %shard_map.50 = bf16[64,3072]{1,0:T(8,128)(2,1)S(1)} custom-call(bf16[64,3072]{1,0:T(8,128)(2,1)S(1)} %collective-permute-done.7.refs_0_, bf16[3072,768]{1,0:T(8,128)(2,1)S(1)} %copy-done.1, bf16[768,3072]{1,0:T(8,128)(2,1)S(1)} %copy-done.3, bf16[64,3072]{1,0:T(8,128)(2,1)S(1)} %get-tuple-element.12.refs_3_.refs_0_), custom_call_target="tpu_custom_call" | custom-call | flops 603979776 | bytes 10616832 | tf_op jit(solution)/shard_map/pallas_call | solution.py:31
  66.1 1.9 %collective-permute-start.8 = (bf16[64,3072]{1,0:T(8,128)(2,1)S(1)}, bf16[64,3072]{1,0:T(8,128)(2,1)S(1)}, u32[]{:S(2)}, u32[]{:S(2)}) collective-permute-start(bf16[64,3072]{1,0:T(8,128)(2,1)S(1)} %shard_map.50), channel_id=1, source_target_pairs={{0,2},{1,3},{2,0},{3,1},{4,6},{5,7},{6,4},{7,5},{8,10},{9,11},{10,... | collective-permute-start | bytes 1179656 | tf_op jit(solution)/shard_map/ppermute | solution.py:24
  68.0 0.0 collective-permute-done.5.refs_1_
  68.0 10.2 %collective-permute-done.6.refs_2_ = bf16[64,3072]{1,0:T(8,128)(2,1)S(1)} collective-permute-done((bf16[64,3072]{1,0:T(8,128)(2,1)S(1)}, bf16[64,3072]{1,0:T(8,128)(2,1)S(1)}, u32[]{:S(2)}, u32[]{:S(2)}) %collective-permute-start.6) | collective-permute-done | bytes 393248 | tf_op jit(solution)/shard_map/ppermute | solution.py:24
  78.3 1.3 %collective-permute-done.8.refs_3_ = bf16[64,3072]{1,0:T(8,128)(2,1)S(1)} collective-permute-done((bf16[64,3072]{1,0:T(8,128)(2,1)S(1)}, bf16[64,3072]{1,0:T(8,128)(2,1)S(1)}, u32[]{:S(2)}, u32[]{:S(2)}) %collective-permute-start.8) | collective-permute-done | bytes 393248 | tf_op jit(solution)/shard_map/ppermute | solution.py:24
  79.5 0.2 shard_map.51
  79.7 9.1 %collective-permute-start.9 = (bf16[16,3072]{1,0:T(8,128)(2,1)S(1)}, bf16[16,3072]{1,0:T(8,128)(2,1)S(1)}, u32[]{:S(2)}, u32[]{:S(2)}) collective-permute-start(bf16[16,3072]{1,0:T(8,128)(2,1)S(1)} %get-tuple-element.16), channel_id=1, source_target_pairs={{0,8},{1,9},{2,10},{3,11},{4,12},{5,13},{6,14},{7,15},{8,0},{9,1},... | collective-permute-start | bytes 294920 | tf_op jit(solution)/shard_map/ppermute | solution.py:24
  88.8 5.2 %collective-permute-start.10 = (bf16[16,3072]{1,0:T(8,128)(2,1)S(1)}, bf16[16,3072]{1,0:T(8,128)(2,1)S(1)}, u32[]{:S(2)}, u32[]{:S(2)}) collective-permute-start(bf16[16,3072]{1,0:T(8,128)(2,1)S(1)} %get-tuple-element.17), channel_id=1, source_target_pairs={{0,12},{1,13},{2,14},{3,15},{4,0},{5,1},{6,2},{7,3},{8,4},{9,5},{1... | collective-permute-start | bytes 294920 | tf_op jit(solution)/shard_map/ppermute | solution.py:24
  94.1 4.0 %collective-permute-start.11 = (bf16[16,3072]{1,0:T(8,128)(2,1)S(1)}, bf16[16,3072]{1,0:T(8,128)(2,1)S(1)}, u32[]{:S(2)}, u32[]{:S(2)}) collective-permute-start(bf16[16,3072]{1,0:T(8,128)(2,1)S(1)} %get-tuple-element.18), channel_id=1, source_target_pairs={{0,4},{1,5},{2,6},{3,7},{4,8},{5,9},{6,10},{7,11},{8,12},{9,13},{1... | collective-permute-start | bytes 294920 | tf_op jit(solution)/shard_map/ppermute | solution.py:24
  98.0 0.0 collective-permute-done.9.refs_2_
  98.1 1.3 %collective-permute-done.10.refs_3_ = bf16[16,3072]{1,0:T(8,128)(2,1)S(1)} collective-permute-done((bf16[16,3072]{1,0:T(8,128)(2,1)S(1)}, bf16[16,3072]{1,0:T(8,128)(2,1)S(1)}, u32[]{:S(2)}, u32[]{:S(2)}) %collective-permute-start.10) | collective-permute-done | bytes 98336 | tf_op jit(solution)/shard_map/ppermute | solution.py:24
  99.4 12.4 %collective-permute-done.11.refs_4_ = bf16[16,3072]{1,0:T(8,128)(2,1)S(1)} collective-permute-done((bf16[16,3072]{1,0:T(8,128)(2,1)S(1)}, bf16[16,3072]{1,0:T(8,128)(2,1)S(1)}, u32[]{:S(2)}, u32[]{:S(2)}) %collective-permute-start.11) | collective-permute-done | bytes 98336 | tf_op jit(solution)/shard_map/ppermute | solution.py:24
  111.8 0.7 shard_map.52
  (2 shorter events, 0.0 us)
Async XLA Ops:
  0.0 0.9 copy-start.4
  0.9 0.7 copy-start.5
  1.8 33.8 %collective-permute-start.2 = (bf16[16,3072]{1,0:T(8,128)(2,1)S(1)}, bf16[16,3072]{1,0:T(8,128)(2,1)S(1)}, u32[]{:S(2)}, u32[]{:S(2)}) collective-permute-start(bf16[16,3072]{1,0:T(8,128)(2,1)S(1)} %shard_map.46.after.refs_0_), channel_id=1, source_target_pairs={{0,8},{1,9},{2,10},{3,11},{4,12},{5,13},{6,14},{7,15},{8,0},{9,1},... | collective-permute-start | bytes 294920 | tf_op jit(solution)/shard_map/ppermute | solution.py:24
  21.8 13.9 %collective-permute-start.1 = (bf16[16,3072]{1,0:T(8,128)(2,1)S(1)}, bf16[16,3072]{1,0:T(8,128)(2,1)S(1)}, u32[]{:S(2)}, u32[]{:S(2)}) collective-permute-start(bf16[16,3072]{1,0:T(8,128)(2,1)S(1)} %shard_map.46.after.refs_0_), channel_id=1, source_target_pairs={{0,12},{1,13},{2,14},{3,15},{4,0},{5,1},{6,2},{7,3},{8,4},{9,5},{1... | collective-permute-start | bytes 294920 | tf_op jit(solution)/shard_map/ppermute | solution.py:24
  27.6 11.4 %collective-permute-start = (bf16[16,3072]{1,0:T(8,128)(2,1)S(1)}, bf16[16,3072]{1,0:T(8,128)(2,1)S(1)}, u32[]{:S(2)}, u32[]{:S(2)}) collective-permute-start(bf16[16,3072]{1,0:T(8,128)(2,1)S(1)} %shard_map.46.after.refs_0_), channel_id=1, source_target_pairs={{0,4},{1,5},{2,6},{3,7},{4,8},{5,9},{6,10},{7,11},{8,12},{9,13},{1... | collective-permute-start | bytes 294920 | tf_op jit(solution)/shard_map/ppermute | solution.py:24
  31.0 2.3 %copy-start = (bf16[3072,768]{1,0:T(8,128)(2,1)S(1)}, bf16[3072,768]{1,0:T(8,128)(2,1)}, u32[]{:S(2)}) copy-start(bf16[3072,768]{1,0:T(8,128)(2,1)} %refs_1_.1) | copy-start | bytes 14155780
  33.3 2.3 %copy-start.2 = (bf16[768,3072]{1,0:T(8,128)(2,1)S(1)}, bf16[768,3072]{1,0:T(8,128)(2,1)}, u32[]{:S(2)}) copy-start(bf16[768,3072]{1,0:T(8,128)(2,1)} %refs_2_.1) | copy-start | bytes 14155780
  35.6 19.4 %copy-start.1 = (bf16[3072,768]{1,0:T(8,128)(2,1)S(1)}, bf16[3072,768]{1,0:T(8,128)(2,1)}, u32[]{:S(2)}) copy-start(bf16[3072,768]{1,0:T(8,128)(2,1)} %refs_1_.1) | copy-start | bytes 14155780
  35.6 19.4 %copy-start.3 = (bf16[768,3072]{1,0:T(8,128)(2,1)S(1)}, bf16[768,3072]{1,0:T(8,128)(2,1)}, u32[]{:S(2)}) copy-start(bf16[768,3072]{1,0:T(8,128)(2,1)} %refs_2_.1) | copy-start | bytes 14155780
  39.0 10.7 %collective-permute-start.3 = (bf16[64,3072]{1,0:T(8,128)(2,1)S(1)}, bf16[64,3072]{1,0:T(8,128)(2,1)S(1)}, u32[]{:S(2)}, u32[]{:S(2)}) collective-permute-start(bf16[64,3072]{1,0:T(8,128)(2,1)S(1)} %shard_map.48.refs_0_), channel_id=1, source_target_pairs={{0,1},{1,2},{2,3},{3,0},{4,5},{5,6},{6,7},{7,4},{8,9},{9,10},{10,1... | collective-permute-start | bytes 1179656 | tf_op jit(solution)/shard_map/ppermute | solution.py:24
  43.4 11.7 %collective-permute-start.4 = (bf16[64,3072]{1,0:T(8,128)(2,1)S(1)}, bf16[64,3072]{1,0:T(8,128)(2,1)S(1)}, u32[]{:S(2)}, u32[]{:S(2)}) collective-permute-start(bf16[64,3072]{1,0:T(8,128)(2,1)S(1)} %shard_map.48.refs_0_), channel_id=1, source_target_pairs={{0,3},{1,0},{2,1},{3,2},{4,7},{5,4},{6,5},{7,6},{8,11},{9,8},{10,9... | collective-permute-start | bytes 1179656 | tf_op jit(solution)/shard_map/ppermute | solution.py:24
  49.8 14.3 %collective-permute-start.7 = (bf16[64,3072]{1,0:T(8,128)(2,1)S(1)}, bf16[64,3072]{1,0:T(8,128)(2,1)S(1)}, u32[]{:S(2)}, u32[]{:S(2)}) collective-permute-start(bf16[64,3072]{1,0:T(8,128)(2,1)S(1)} %collective-permute-done.3.refs_1_), channel_id=1, source_target_pairs={{0,1},{1,2},{2,3},{3,0},{4,5},{5,6},{6,7},{7,4},{8,9},{9,10},{10,1... | collective-permute-start | bytes 1179656 | tf_op jit(solution)/shard_map/ppermute | solution.py:24
  57.5 10.5 %collective-permute-start.5 = (bf16[64,3072]{1,0:T(8,128)(2,1)S(1)}, bf16[64,3072]{1,0:T(8,128)(2,1)S(1)}, u32[]{:S(2)}, u32[]{:S(2)}) collective-permute-start(bf16[64,3072]{1,0:T(8,128)(2,1)S(1)} %get-tuple-element.13), channel_id=1, source_target_pairs={{0,3},{1,0},{2,1},{3,2},{4,7},{5,4},{6,5},{7,6},{8,11},{9,8},{10,9... | collective-permute-start | bytes 1179656 | tf_op jit(solution)/shard_map/ppermute | solution.py:24
  59.5 18.8 %collective-permute-start.6 = (bf16[64,3072]{1,0:T(8,128)(2,1)S(1)}, bf16[64,3072]{1,0:T(8,128)(2,1)S(1)}, u32[]{:S(2)}, u32[]{:S(2)}) collective-permute-start(bf16[64,3072]{1,0:T(8,128)(2,1)S(1)} %get-tuple-element.14), channel_id=1, source_target_pairs={{0,1},{1,2},{2,3},{3,0},{4,5},{5,6},{6,7},{7,4},{8,9},{9,10},{10,1... | collective-permute-start | bytes 1179656 | tf_op jit(solution)/shard_map/ppermute | solution.py:24
  66.1 13.4 %collective-permute-start.8 = (bf16[64,3072]{1,0:T(8,128)(2,1)S(1)}, bf16[64,3072]{1,0:T(8,128)(2,1)S(1)}, u32[]{:S(2)}, u32[]{:S(2)}) collective-permute-start(bf16[64,3072]{1,0:T(8,128)(2,1)S(1)} %shard_map.50), channel_id=1, source_target_pairs={{0,2},{1,3},{2,0},{3,1},{4,6},{5,7},{6,4},{7,5},{8,10},{9,11},{10,... | collective-permute-start | bytes 1179656 | tf_op jit(solution)/shard_map/ppermute | solution.py:24
  79.7 18.3 %collective-permute-start.9 = (bf16[16,3072]{1,0:T(8,128)(2,1)S(1)}, bf16[16,3072]{1,0:T(8,128)(2,1)S(1)}, u32[]{:S(2)}, u32[]{:S(2)}) collective-permute-start(bf16[16,3072]{1,0:T(8,128)(2,1)S(1)} %get-tuple-element.16), channel_id=1, source_target_pairs={{0,8},{1,9},{2,10},{3,11},{4,12},{5,13},{6,14},{7,15},{8,0},{9,1},... | collective-permute-start | bytes 294920 | tf_op jit(solution)/shard_map/ppermute | solution.py:24
  88.8 10.5 %collective-permute-start.10 = (bf16[16,3072]{1,0:T(8,128)(2,1)S(1)}, bf16[16,3072]{1,0:T(8,128)(2,1)S(1)}, u32[]{:S(2)}, u32[]{:S(2)}) collective-permute-start(bf16[16,3072]{1,0:T(8,128)(2,1)S(1)} %get-tuple-element.17), channel_id=1, source_target_pairs={{0,12},{1,13},{2,14},{3,15},{4,0},{5,1},{6,2},{7,3},{8,4},{9,5},{1... | collective-permute-start | bytes 294920 | tf_op jit(solution)/shard_map/ppermute | solution.py:24
  94.1 17.7 %collective-permute-start.11 = (bf16[16,3072]{1,0:T(8,128)(2,1)S(1)}, bf16[16,3072]{1,0:T(8,128)(2,1)S(1)}, u32[]{:S(2)}, u32[]{:S(2)}) collective-permute-start(bf16[16,3072]{1,0:T(8,128)(2,1)S(1)} %get-tuple-element.18), channel_id=1, source_target_pairs={{0,4},{1,5},{2,6},{3,7},{4,8},{5,9},{6,10},{7,11},{8,12},{9,13},{1... | collective-permute-start | bytes 294920 | tf_op jit(solution)/shard_map/ppermute | solution.py:24

commit v8 on v6

--- a/solution.py
+++ b/solution.py
@@ -39,12 +39,26 @@
     )(*args)
 
 
-def normalize_body(tokens, gain, out):
+def normalize_body(tokens_hbm, gain_hbm, out, tokens, gain, sems):
+    copies = [
+        pltpu.make_async_copy(tokens_hbm, tokens, sems.at[0]),
+        pltpu.make_async_copy(gain_hbm, gain, sems.at[1]),
+    ]
+    for copy in copies:
+        copy.start()
+    for copy in copies:
+        copy.wait()
     values = tokens[...].astype(jnp.float32)
     center = jnp.mean(values, axis=1, keepdims=True)
     centered = values - center
     spread = jnp.mean(centered * centered, axis=1, keepdims=True)
     out[...] = (centered * lax.rsqrt(spread + 1e-06) * gain[...]).astype(jnp.bfloat16)
+
+
+def normalize(tokens, gain):
+    outs = [jax.ShapeDtypeStruct(tokens.shape, jnp.bfloat16)]
+    scratch = [pltpu.VMEM(a.shape, a.dtype) for a in (tokens, gain)] + [pltpu.SemaphoreType.DMA((2,))]
+    return call(normalize_body, outs, (tokens, gain), specs=[AFTER, AFTER], scratch=scratch, limit=60)[0]
 
 
 def ready_body(w_in, w_out, after, out):
@@ -116,9 +130,7 @@
 def on_device(shape, tokens, ln_gain, w_in, w_out):
     along_z = functools.partial(shift, shape=shape, axis=0)
     along_x = functools.partial(shift, shape=shape, axis=1)
-    (own,) = call(
-        normalize_body, [jax.ShapeDtypeStruct(tokens.shape, jnp.bfloat16)], (tokens, ln_gain[None, :])
-    )
+    own = normalize(tokens, ln_gain[None, :])
     near, far = along_z(own, step=1), along_z(own, step=-1)
     opposite = along_z(near, step=1)
     held = ready(w_in, w_out, own)
@@ -130,9 +142,10 @@
     (opposite,) = feed([opposite], w_in, w_out, own)
     opposite = along_x(opposite, step=2)
     own, near, far, opposite = add([own, near, far, opposite], 4)
-    opposite = along_z(opposite, step=2)
-    near, far = along_z(near, step=-1), along_z(far, step=1)
-    return add([tokens, own, opposite, near, far])[0]
+    opposite = along_z(opposite, step=-1)
+    far = along_z(far, step=1)
+    (near,) = add([near, opposite])
+    return add([tokens, own, along_z(near, step=-1), far])[0]
 
 
 def solution(mesh):

time: 108 us -> 111 us (1.028)
  the two profiles are of different devices: /device:TPU:1 before, /device:TPU:40 now
where the time goes in v8:
time: 111 us
  starting transfers between devices  63.6 us (57%)
  waiting for transfers between devices  34.4 us (31%)
  Pallas kernels  7.19 us (6%)
  local copies, waits for them, and re-layouts  5.57 us (5%)
    ppermute x12, starting transfers between devices, shift(): return lax.ppermute(value, ('dp', 'mp'), pairs)  63.6 us
    ppermute x12, waiting for transfers between devices, shift(): return lax.ppermute(value, ('dp', 'mp'), pairs)  34.4 us
    pallas_call x8, Pallas kernels, call(): pl.pallas_call(body, out_shape=outs, in_specs=specs or [VMEM] * len(args)...  7.19 us
    unnamed x12, local copies, waits for them, and re-layouts  5.57 us
  transfers between devices with their start and end apart: 12, of which 7 were waited for; matrix products, arithmetic and copies ran while one was open for 0% of the time, Pallas kernels for 4%

profile of v8, /device:TPU:40, one launch (start us, length us, event | category | flops | bytes accessed | tf_op | source)
XLA Modules:
  0.0 110.9 jit_solution(11739678958392498680)
XLA Ops:
  0.0 1.8 %shard_map.46.after.refs_0_ = bf16[16,3072]{1,0:T(8,128)(2,1)} custom-call(bf16[16,3072]{1,0:T(8,128)(2,1)} %refs_0_.1, f32[1,3072]{1,0:T(1,128)} %bitcast.1), custom_call_target="tpu_custom_call" | custom-call | bytes 208896 | tf_op jit(solution)/shard_map/pallas_call | solution.py:31
  1.8 10.9 %collective-permute-start = (bf16[16,3072]{1,0:T(8,128)(2,1)}, bf16[16,3072]{1,0:T(8,128)(2,1)S(1)}, u32[]{:S(2)}, u32[]{:S(2)}) collective-permute-start(bf16[16,3072]{1,0:T(8,128)(2,1)} %shard_map.46.after.refs_0_), channel_id=1, source_target_pairs={{0,4},{1,5},{2,6},{3,7},{4,8},{5,9},{6,10},{7,11},{8,12},{9,13},{1... | collective-permute-start | bytes 294920 | tf_op jit(solution)/shard_map/ppermute | solution.py:24
  12.7 9.2 %collective-permute-start.1 = (bf16[16,3072]{1,0:T(8,128)(2,1)}, bf16[16,3072]{1,0:T(8,128)(2,1)S(1)}, u32[]{:S(2)}, u32[]{:S(2)}) collective-permute-start(bf16[16,3072]{1,0:T(8,128)(2,1)} %shard_map.46.after.refs_0_), channel_id=1, source_target_pairs={{0,12},{1,13},{2,14},{3,15},{4,0},{5,1},{6,2},{7,3},{8,4},{9,5},{1... | collective-permute-start | bytes 294920 | tf_op jit(solution)/shard_map/ppermute | solution.py:24
  21.9 1.2 %collective-permute-done.refs_1_ = bf16[16,3072]{1,0:T(8,128)(2,1)S(1)} collective-permute-done((bf16[16,3072]{1,0:T(8,128)(2,1)}, bf16[16,3072]{1,0:T(8,128)(2,1)S(1)}, u32[]{:S(2)}, u32[]{:S(2)}) %collective-permute-start) | collective-permute-done | bytes 98336 | tf_op jit(solution)/shard_map/ppermute | solution.py:24
  23.1 4.4 %collective-permute-start.2 = (bf16[16,3072]{1,0:T(8,128)(2,1)S(1)}, bf16[16,3072]{1,0:T(8,128)(2,1)S(1)}, u32[]{:S(2)}, u32[]{:S(2)}) collective-permute-start(bf16[16,3072]{1,0:T(8,128)(2,1)S(1)} %collective-permute-done.refs_1_), channel_id=1, source_target_pairs={{0,4},{1,5},{2,6},{3,7},{4,8},{5,9},{6,10},{7,11},{8,12},{9,13},{1... | collective-permute-start | bytes 294920 | tf_op jit(solution)/shard_map/ppermute | solution.py:24
  27.5 0.0 copy-start
  27.5 2.3 %copy-done = bf16[3072,768]{1,0:T(8,128)(2,1)S(1)} copy-done((bf16[3072,768]{1,0:T(8,128)(2,1)S(1)}, bf16[3072,768]{1,0:T(8,128)(2,1)}, u32[]{:S(2)}) %copy-start) | copy-done | bytes 4718616
  29.9 0.0 copy-start.2
  29.9 2.3 %copy-done.2 = bf16[768,3072]{1,0:T(8,128)(2,1)S(1)} copy-done((bf16[768,3072]{1,0:T(8,128)(2,1)S(1)}, bf16[768,3072]{1,0:T(8,128)(2,1)}, u32[]{:S(2)}) %copy-start.2) | copy-done | bytes 4718616
  32.2 0.0 copy-start.4
  32.2 0.9 copy-done.4
  33.1 0.0 copy-start.1
  33.1 0.0 copy-start.3
  33.1 0.0 collective-permute-done.1.refs_2_
  33.1 3.6 %collective-permute-done.2.refs_3_ = bf16[16,3072]{1,0:T(8,128)(2,1)S(1)} collective-permute-done((bf16[16,3072]{1,0:T(8,128)(2,1)S(1)}, bf16[16,3072]{1,0:T(8,128)(2,1)S(1)}, u32[]{:S(2)}, u32[]{:S(2)}) %collective-permute-start.2) | collective-permute-done | bytes 98336 | tf_op jit(solution)/shard_map/ppermute | solution.py:24
  36.7 3.4 %collective-permute-start.3 = (bf16[64,3072]{1,0:T(8,128)(2,1)S(1)}, bf16[64,3072]{1,0:T(8,128)(2,1)S(1)}, u32[]{:S(2)}, u32[]{:S(2)}) collective-permute-start(bf16[64,3072]{1,0:T(8,128)(2,1)S(1)} %shard_map.48.refs_0_), channel_id=1, source_target_pairs={{0,1},{1,2},{2,3},{3,0},{4,5},{5,6},{6,7},{7,4},{8,9},{9,10},{10,1... | collective-permute-start | bytes 1179656 | tf_op jit(solution)/shard_map/ppermute | solution.py:24
  40.1 3.7 %collective-permute-start.4 = (bf16[64,3072]{1,0:T(8,128)(2,1)S(1)}, bf16[64,3072]{1,0:T(8,128)(2,1)S(1)}, u32[]{:S(2)}, u32[]{:S(2)}) collective-permute-start(bf16[64,3072]{1,0:T(8,128)(2,1)S(1)} %shard_map.48.refs_0_), channel_id=1, source_target_pairs={{0,3},{1,0},{2,1},{3,2},{4,7},{5,4},{6,5},{7,6},{8,11},{9,8},{10,9... | collective-permute-start | bytes 1179656 | tf_op jit(solution)/shard_map/ppermute | solution.py:24
  43.8 3.8 %collective-permute-done.3.refs_1_ = bf16[64,3072]{1,0:T(8,128)(2,1)S(1)} collective-permute-done((bf16[64,3072]{1,0:T(8,128)(2,1)S(1)}, bf16[64,3072]{1,0:T(8,128)(2,1)S(1)}, u32[]{:S(2)}, u32[]{:S(2)}) %collective-permute-start.3) | collective-permute-done | bytes 393248 | tf_op jit(solution)/shard_map/ppermute | solution.py:24
  47.6 2.6 %collective-permute-start.7 = (bf16[64,3072]{1,0:T(8,128)(2,1)S(1)}, bf16[64,3072]{1,0:T(8,128)(2,1)S(1)}, u32[]{:S(2)}, u32[]{:S(2)}) collective-permute-start(bf16[64,3072]{1,0:T(8,128)(2,1)S(1)} %collective-permute-done.3.refs_1_), channel_id=1, source_target_pairs={{0,1},{1,2},{2,3},{3,0},{4,5},{5,6},{6,7},{7,4},{8,9},{9,10},{10,1... | collective-permute-start | bytes 1179656 | tf_op jit(solution)/shard_map/ppermute | solution.py:24
  50.2 1.2 %collective-permute-done.4.refs_2_ = bf16[64,3072]{1,0:T(8,128)(2,1)S(1)} collective-permute-done((bf16[64,3072]{1,0:T(8,128)(2,1)S(1)}, bf16[64,3072]{1,0:T(8,128)(2,1)S(1)}, u32[]{:S(2)}, u32[]{:S(2)}) %collective-permute-start.4) | collective-permute-done | bytes 393248 | tf_op jit(solution)/shard_map/ppermute | solution.py:24
  51.4 0.0 copy-done.1
  51.4 0.0 copy-done.3
  51.4 2.4 %shard_map.49 = (bf16[64,3072]{1,0:T(8,128)(2,1)S(1)}, bf16[64,3072]{1,0:T(8,128)(2,1)S(1)}, bf16[64,3072]{1,0:T(8,128)(2,1)S(1)}) custom-call(bf16[64,3072]{1,0:T(8,128)(2,1)S(1)} %shard_map.48.refs_0_, bf16[64,3072]{1,0:T(8,128)(2,1)S(1)} %collective-permute-done.3.refs_1_, bf16[64,3072]{1,0:T(8,128)(2,1)S(1)} %collective-permute-done.4.refs_2_, ...), custom_call_target="tpu_custom_call" | custom-call | flops 1811939328 | bytes 11798528 | tf_op jit(solution)/shard_map/pallas_call | solution.py:31
  53.8 5.6 %collective-permute-start.5 = (bf16[64,3072]{1,0:T(8,128)(2,1)S(1)}, bf16[64,3072]{1,0:T(8,128)(2,1)S(1)}, u32[]{:S(2)}, u32[]{:S(2)}) collective-permute-start(bf16[64,3072]{1,0:T(8,128)(2,1)S(1)} %get-tuple-element.13), channel_id=1, source_target_pairs={{0,3},{1,0},{2,1},{3,2},{4,7},{5,4},{6,5},{7,6},{8,11},{9,8},{10,9... | collective-permute-start | bytes 1179656 | tf_op jit(solution)/shard_map/ppermute | solution.py:24
  59.4 1.9 %collective-permute-start.6 = (bf16[64,3072]{1,0:T(8,128)(2,1)S(1)}, bf16[64,3072]{1,0:T(8,128)(2,1)S(1)}, u32[]{:S(2)}, u32[]{:S(2)}) collective-permute-start(bf16[64,3072]{1,0:T(8,128)(2,1)S(1)} %get-tuple-element.14), channel_id=1, source_target_pairs={{0,1},{1,2},{2,3},{3,0},{4,5},{5,6},{6,7},{7,4},{8,9},{9,10},{10,1... | collective-permute-start | bytes 1179656 | tf_op jit(solution)/shard_map/ppermute | solution.py:24
  61.4 0.0 collective-permute-done.7.refs_0_
  61.4 0.0 copy-start.5
  61.4 2.0 %shard_map.50 = bf16[64,3072]{1,0:T(8,128)(2,1)S(1)} custom-call(bf16[64,3072]{1,0:T(8,128)(2,1)S(1)} %collective-permute-done.7.refs_0_, bf16[3072,768]{1,0:T(8,128)(2,1)S(1)} %copy-done.1, bf16[768,3072]{1,0:T(8,128)(2,1)S(1)} %copy-done.3, bf16[64,3072]{1,0:T(8,128)(2,1)S(1)} %get-tuple-element.12.refs_3_.refs_0_), custom_call_target="tpu_custom_call" | custom-call | flops 603979776 | bytes 10616832 | tf_op jit(solution)/shard_map/pallas_call | solution.py:31
  63.4 3.4 %collective-permute-start.8 = (bf16[64,3072]{1,0:T(8,128)(2,1)S(1)}, bf16[64,3072]{1,0:T(8,128)(2,1)S(1)}, u32[]{:S(2)}, u32[]{:S(2)}) collective-permute-start(bf16[64,3072]{1,0:T(8,128)(2,1)S(1)} %shard_map.50), channel_id=1, source_target_pairs={{0,2},{1,3},{2,0},{3,1},{4,6},{5,7},{6,4},{7,5},{8,10},{9,11},{10,... | collective-permute-start | bytes 1179656 | tf_op jit(solution)/shard_map/ppermute | solution.py:24
  66.8 0.0 collective-permute-done.5.refs_1_
  66.8 13.1 %collective-permute-done.6.refs_2_ = bf16[64,3072]{1,0:T(8,128)(2,1)S(1)} collective-permute-done((bf16[64,3072]{1,0:T(8,128)(2,1)S(1)}, bf16[64,3072]{1,0:T(8,128)(2,1)S(1)}, u32[]{:S(2)}, u32[]{:S(2)}) %collective-permute-start.6) | collective-permute-done | bytes 393248 | tf_op jit(solution)/shard_map/ppermute | solution.py:24
  79.9 0.0 collective-permute-done.8.refs_3_
  79.9 0.2 shard_map.51
  80.1 8.1 %collective-permute-start.9 = (bf16[16,3072]{1,0:T(8,128)(2,1)S(1)}, bf16[16,3072]{1,0:T(8,128)(2,1)S(1)}, u32[]{:S(2)}, u32[]{:S(2)}) collective-permute-start(bf16[16,3072]{1,0:T(8,128)(2,1)S(1)} %get-tuple-element.17), channel_id=1, source_target_pairs={{0,12},{1,13},{2,14},{3,15},{4,0},{5,1},{6,2},{7,3},{8,4},{9,5},{1... | collective-permute-start | bytes 294920 | tf_op jit(solution)/shard_map/ppermute | solution.py:24
  88.3 1.9 %collective-permute-start.11 = (bf16[16,3072]{1,0:T(8,128)(2,1)S(1)}, bf16[16,3072]{1,0:T(8,128)(2,1)S(1)}, u32[]{:S(2)}, u32[]{:S(2)}) collective-permute-start(bf16[16,3072]{1,0:T(8,128)(2,1)S(1)} %get-tuple-element.18), channel_id=1, source_target_pairs={{0,4},{1,5},{2,6},{3,7},{4,8},{5,9},{6,10},{7,11},{8,12},{9,13},{1... | collective-permute-start | bytes 294920 | tf_op jit(solution)/shard_map/ppermute | solution.py:24
  90.2 6.7 %collective-permute-done.9.refs_1_ = bf16[16,3072]{1,0:T(8,128)(2,1)S(1)} collective-permute-done((bf16[16,3072]{1,0:T(8,128)(2,1)S(1)}, bf16[16,3072]{1,0:T(8,128)(2,1)S(1)}, u32[]{:S(2)}, u32[]{:S(2)}) %collective-permute-start.9) | collective-permute-done | bytes 98336 | tf_op jit(solution)/shard_map/ppermute | solution.py:24
  96.9 8.4 %collective-permute-start.10 = (bf16[16,3072]{1,0:T(8,128)(2,1)S(1)}, bf16[16,3072]{1,0:T(8,128)(2,1)S(1)}, u32[]{:S(2)}, u32[]{:S(2)}) collective-permute-start(bf16[16,3072]{1,0:T(8,128)(2,1)S(1)} %shard_map.52), channel_id=1, source_target_pairs={{0,12},{1,13},{2,14},{3,15},{4,0},{5,1},{6,2},{7,3},{8,4},{9,5},{1... | collective-permute-start | bytes 294920 | tf_op jit(solution)/shard_map/ppermute | solution.py:24
  105.3 0.0 collective-permute-done.11.refs_3_
  105.3 4.9 %collective-permute-done.10.refs_2_ = bf16[16,3072]{1,0:T(8,128)(2,1)S(1)} collective-permute-done((bf16[16,3072]{1,0:T(8,128)(2,1)S(1)}, bf16[16,3072]{1,0:T(8,128)(2,1)S(1)}, u32[]{:S(2)}, u32[]{:S(2)}) %collective-permute-start.10) | collective-permute-done | bytes 98336 | tf_op jit(solution)/shard_map/ppermute | solution.py:24
  110.2 0.0 copy-done.5
  110.2 0.7 shard_map.53
  (3 shorter events, 0.1 us)
Async XLA Ops:
  1.8 21.3 %collective-permute-start = (bf16[16,3072]{1,0:T(8,128)(2,1)}, bf16[16,3072]{1,0:T(8,128)(2,1)S(1)}, u32[]{:S(2)}, u32[]{:S(2)}) collective-permute-start(bf16[16,3072]{1,0:T(8,128)(2,1)} %shard_map.46.after.refs_0_), channel_id=1, source_target_pairs={{0,4},{1,5},{2,6},{3,7},{4,8},{5,9},{6,10},{7,11},{8,12},{9,13},{1... | collective-permute-start | bytes 294920 | tf_op jit(solution)/shard_map/ppermute | solution.py:24
  12.7 20.4 %collective-permute-start.1 = (bf16[16,3072]{1,0:T(8,128)(2,1)}, bf16[16,3072]{1,0:T(8,128)(2,1)S(1)}, u32[]{:S(2)}, u32[]{:S(2)}) collective-permute-start(bf16[16,3072]{1,0:T(8,128)(2,1)} %shard_map.46.after.refs_0_), channel_id=1, source_target_pairs={{0,12},{1,13},{2,14},{3,15},{4,0},{5,1},{6,2},{7,3},{8,4},{9,5},{1... | collective-permute-start | bytes 294920 | tf_op jit(solution)/shard_map/ppermute | solution.py:24
  23.1 13.6 %collective-permute-start.2 = (bf16[16,3072]{1,0:T(8,128)(2,1)S(1)}, bf16[16,3072]{1,0:T(8,128)(2,1)S(1)}, u32[]{:S(2)}, u32[]{:S(2)}) collective-permute-start(bf16[16,3072]{1,0:T(8,128)(2,1)S(1)} %collective-permute-done.refs_1_), channel_id=1, source_target_pairs={{0,4},{1,5},{2,6},{3,7},{4,8},{5,9},{6,10},{7,11},{8,12},{9,13},{1... | collective-permute-start | bytes 294920 | tf_op jit(solution)/shard_map/ppermute | solution.py:24
  27.5 2.3 %copy-start = (bf16[3072,768]{1,0:T(8,128)(2,1)S(1)}, bf16[3072,768]{1,0:T(8,128)(2,1)}, u32[]{:S(2)}) copy-start(bf16[3072,768]{1,0:T(8,128)(2,1)} %refs_1_.1) | copy-start | bytes 14155780
  29.9 2.3 %copy-start.2 = (bf16[768,3072]{1,0:T(8,128)(2,1)S(1)}, bf16[768,3072]{1,0:T(8,128)(2,1)}, u32[]{:S(2)}) copy-start(bf16[768,3072]{1,0:T(8,128)(2,1)} %refs_2_.1) | copy-start | bytes 14155780
  32.2 0.9 copy-start.4
  33.1 18.3 %copy-start.1 = (bf16[3072,768]{1,0:T(8,128)(2,1)S(1)}, bf16[3072,768]{1,0:T(8,128)(2,1)}, u32[]{:S(2)}) copy-start(bf16[3072,768]{1,0:T(8,128)(2,1)} %refs_1_.1) | copy-start | bytes 14155780
  33.1 18.3 %copy-start.3 = (bf16[768,3072]{1,0:T(8,128)(2,1)S(1)}, bf16[768,3072]{1,0:T(8,128)(2,1)}, u32[]{:S(2)}) copy-start(bf16[768,3072]{1,0:T(8,128)(2,1)} %refs_2_.1) | copy-start | bytes 14155780
  36.7 10.9 %collective-permute-start.3 = (bf16[64,3072]{1,0:T(8,128)(2,1)S(1)}, bf16[64,3072]{1,0:T(8,128)(2,1)S(1)}, u32[]{:S(2)}, u32[]{:S(2)}) collective-permute-start(bf16[64,3072]{1,0:T(8,128)(2,1)S(1)} %shard_map.48.refs_0_), channel_id=1, source_target_pairs={{0,1},{1,2},{2,3},{3,0},{4,5},{5,6},{6,7},{7,4},{8,9},{9,10},{10,1... | collective-permute-start | bytes 1179656 | tf_op jit(solution)/shard_map/ppermute | solution.py:24
  40.1 11.3 %collective-permute-start.4 = (bf16[64,3072]{1,0:T(8,128)(2,1)S(1)}, bf16[64,3072]{1,0:T(8,128)(2,1)S(1)}, u32[]{:S(2)}, u32[]{:S(2)}) collective-permute-start(bf16[64,3072]{1,0:T(8,128)(2,1)S(1)} %shard_map.48.refs_0_), channel_id=1, source_target_pairs={{0,3},{1,0},{2,1},{3,2},{4,7},{5,4},{6,5},{7,6},{8,11},{9,8},{10,9... | collective-permute-start | bytes 1179656 | tf_op jit(solution)/shard_map/ppermute | solution.py:24
  47.6 13.8 %collective-permute-start.7 = (bf16[64,3072]{1,0:T(8,128)(2,1)S(1)}, bf16[64,3072]{1,0:T(8,128)(2,1)S(1)}, u32[]{:S(2)}, u32[]{:S(2)}) collective-permute-start(bf16[64,3072]{1,0:T(8,128)(2,1)S(1)} %collective-permute-done.3.refs_1_), channel_id=1, source_target_pairs={{0,1},{1,2},{2,3},{3,0},{4,5},{5,6},{6,7},{7,4},{8,9},{9,10},{10,1... | collective-permute-start | bytes 1179656 | tf_op jit(solution)/shard_map/ppermute | solution.py:24
  53.8 13.0 %collective-permute-start.5 = (bf16[64,3072]{1,0:T(8,128)(2,1)S(1)}, bf16[64,3072]{1,0:T(8,128)(2,1)S(1)}, u32[]{:S(2)}, u32[]{:S(2)}) collective-permute-start(bf16[64,3072]{1,0:T(8,128)(2,1)S(1)} %get-tuple-element.13), channel_id=1, source_target_pairs={{0,3},{1,0},{2,1},{3,2},{4,7},{5,4},{6,5},{7,6},{8,11},{9,8},{10,9... | collective-permute-start | bytes 1179656 | tf_op jit(solution)/shard_map/ppermute | solution.py:24
  59.4 20.5 %collective-permute-start.6 = (bf16[64,3072]{1,0:T(8,128)(2,1)S(1)}, bf16[64,3072]{1,0:T(8,128)(2,1)S(1)}, u32[]{:S(2)}, u32[]{:S(2)}) collective-permute-start(bf16[64,3072]{1,0:T(8,128)(2,1)S(1)} %get-tuple-element.14), channel_id=1, source_target_pairs={{0,1},{1,2},{2,3},{3,0},{4,5},{5,6},{6,7},{7,4},{8,9},{9,10},{10,1... | collective-permute-start | bytes 1179656 | tf_op jit(solution)/shard_map/ppermute | solution.py:24
  61.4 48.8 %copy-start.5 = (bf16[16,3072]{1,0:T(8,128)(2,1)S(1)}, bf16[16,3072]{1,0:T(8,128)(2,1)}, u32[]{:S(2)}) copy-start(bf16[16,3072]{1,0:T(8,128)(2,1)} %refs_0_.1) | copy-start | bytes 294916
  63.4 16.5 %collective-permute-start.8 = (bf16[64,3072]{1,0:T(8,128)(2,1)S(1)}, bf16[64,3072]{1,0:T(8,128)(2,1)S(1)}, u32[]{:S(2)}, u32[]{:S(2)}) collective-permute-start(bf16[64,3072]{1,0:T(8,128)(2,1)S(1)} %shard_map.50), channel_id=1, source_target_pairs={{0,2},{1,3},{2,0},{3,1},{4,6},{5,7},{6,4},{7,5},{8,10},{9,11},{10,... | collective-permute-start | bytes 1179656 | tf_op jit(solution)/shard_map/ppermute | solution.py:24
  80.1 16.7 %collective-permute-start.9 = (bf16[16,3072]{1,0:T(8,128)(2,1)S(1)}, bf16[16,3072]{1,0:T(8,128)(2,1)S(1)}, u32[]{:S(2)}, u32[]{:S(2)}) collective-permute-start(bf16[16,3072]{1,0:T(8,128)(2,1)S(1)} %get-tuple-element.17), channel_id=1, source_target_pairs={{0,12},{1,13},{2,14},{3,15},{4,0},{5,1},{6,2},{7,3},{8,4},{9,5},{1... | collective-permute-start | bytes 294920 | tf_op jit(solution)/shard_map/ppermute | solution.py:24
  88.3 17.1 %collective-permute-start.11 = (bf16[16,3072]{1,0:T(8,128)(2,1)S(1)}, bf16[16,3072]{1,0:T(8,128)(2,1)S(1)}, u32[]{:S(2)}, u32[]{:S(2)}) collective-permute-start(bf16[16,3072]{1,0:T(8,128)(2,1)S(1)} %get-tuple-element.18), channel_id=1, source_target_pairs={{0,4},{1,5},{2,6},{3,7},{4,8},{5,9},{6,10},{7,11},{8,12},{9,13},{1... | collective-permute-start | bytes 294920 | tf_op jit(solution)/shard_map/ppermute | solution.py:24
  96.9 13.3 %collective-permute-start.10 = (bf16[16,3072]{1,0:T(8,128)(2,1)S(1)}, bf16[16,3072]{1,0:T(8,128)(2,1)S(1)}, u32[]{:S(2)}, u32[]{:S(2)}) collective-permute-start(bf16[16,3072]{1,0:T(8,128)(2,1)S(1)} %shard_map.52), channel_id=1, source_target_pairs={{0,12},{1,13},{2,14},{3,15},{4,0},{5,1},{6,2},{7,3},{8,4},{9,5},{1... | collective-permute-start | bytes 294920 | tf_op jit(solution)/shard_map/ppermute | solution.py:24

commit v9 on v8

--- a/solution.py
+++ b/solution.py
@@ -142,10 +142,9 @@
     (opposite,) = feed([opposite], w_in, w_out, own)
     opposite = along_x(opposite, step=2)
     own, near, far, opposite = add([own, near, far, opposite], 4)
-    opposite = along_z(opposite, step=-1)
-    far = along_z(far, step=1)
-    (near,) = add([near, opposite])
-    return add([tokens, own, along_z(near, step=-1), far])[0]
+    opposite = along_z(opposite, step=2)
+    near, far = along_z(near, step=-1), along_z(far, step=1)
+    return add([tokens, own, opposite, near, far])[0]
 
 
 def solution(mesh):

time: 111 us -> 108 us (0.973)
  the two profiles are of different devices: /device:TPU:40 before, /device:TPU:1 now
where the time goes in v9:
time: 108 us
  starting transfers between devices  68.7 us (64%)
  waiting for transfers between devices  26.2 us (24%)
  Pallas kernels  7.18 us (7%)
  local copies, waits for them, and re-layouts  5.57 us (5%)
    ppermute x12, starting transfers between devices, shift(): return lax.ppermute(value, ('dp', 'mp'), pairs)  68.7 us
    ppermute x12, waiting for transfers between devices, shift(): return lax.ppermute(value, ('dp', 'mp'), pairs)  26.2 us
    pallas_call x7, Pallas kernels, call(): pl.pallas_call(body, out_shape=outs, in_specs=specs or [VMEM] * len(args)...  7.18 us
    unnamed x12, local copies, waits for them, and re-layouts  5.57 us
  transfers between devices with their start and end apart: 12, of which 6 were waited for; matrix products, arithmetic and copies ran while one was open for 0% of the time, Pallas kernels for 4%

profile of v9, /device:TPU:1, one launch (start us, length us, event | category | flops | bytes accessed | tf_op | source)
XLA Modules:
  0.0 107.9 jit_solution(3777680826615726110)
XLA Ops:
  0.0 1.8 %shard_map.46.after.refs_0_ = bf16[16,3072]{1,0:T(8,128)(2,1)} custom-call(bf16[16,3072]{1,0:T(8,128)(2,1)} %refs_0_.1, f32[1,3072]{1,0:T(1,128)} %bitcast.1), custom_call_target="tpu_custom_call" | custom-call | bytes 208896 | tf_op jit(solution)/shard_map/pallas_call | solution.py:31
  1.8 18.7 %collective-permute-start = (bf16[16,3072]{1,0:T(8,128)(2,1)}, bf16[16,3072]{1,0:T(8,128)(2,1)S(1)}, u32[]{:S(2)}, u32[]{:S(2)}) collective-permute-start(bf16[16,3072]{1,0:T(8,128)(2,1)} %shard_map.46.after.refs_0_), channel_id=1, source_target_pairs={{0,4},{1,5},{2,6},{3,7},{4,8},{5,9},{6,10},{7,11},{8,12},{9,13},{1... | collective-permute-start | bytes 294920 | tf_op jit(solution)/shard_map/ppermute | solution.py:24
  20.5 1.9 %collective-permute-start.1 = (bf16[16,3072]{1,0:T(8,128)(2,1)}, bf16[16,3072]{1,0:T(8,128)(2,1)S(1)}, u32[]{:S(2)}, u32[]{:S(2)}) collective-permute-start(bf16[16,3072]{1,0:T(8,128)(2,1)} %shard_map.46.after.refs_0_), channel_id=1, source_target_pairs={{0,12},{1,13},{2,14},{3,15},{4,0},{5,1},{6,2},{7,3},{8,4},{9,5},{1... | collective-permute-start | bytes 294920 | tf_op jit(solution)/shard_map/ppermute | solution.py:24
  22.5 0.0 collective-permute-done.refs_1_
  22.5 11.6 %collective-permute-start.2 = (bf16[16,3072]{1,0:T(8,128)(2,1)S(1)}, bf16[16,3072]{1,0:T(8,128)(2,1)S(1)}, u32[]{:S(2)}, u32[]{:S(2)}) collective-permute-start(bf16[16,3072]{1,0:T(8,128)(2,1)S(1)} %collective-permute-done.refs_1_), channel_id=1, source_target_pairs={{0,4},{1,5},{2,6},{3,7},{4,8},{5,9},{6,10},{7,11},{8,12},{9,13},{1... | collective-permute-start | bytes 294920 | tf_op jit(solution)/shard_map/ppermute | solution.py:24
  34.1 0.0 copy-start
  34.1 2.3 %copy-done = bf16[3072,768]{1,0:T(8,128)(2,1)S(1)} copy-done((bf16[3072,768]{1,0:T(8,128)(2,1)S(1)}, bf16[3072,768]{1,0:T(8,128)(2,1)}, u32[]{:S(2)}) %copy-start) | copy-done | bytes 4718616
  36.4 0.0 copy-start.2
  36.4 2.3 %copy-done.2 = bf16[768,3072]{1,0:T(8,128)(2,1)S(1)} copy-done((bf16[768,3072]{1,0:T(8,128)(2,1)S(1)}, bf16[768,3072]{1,0:T(8,128)(2,1)}, u32[]{:S(2)}) %copy-start.2) | copy-done | bytes 4718616
  38.7 0.0 copy-start.4
  38.7 0.9 copy-done.4
  39.6 0.0 copy-start.1
  39.6 0.0 copy-start.3
  39.6 0.0 collective-permute-done.1.refs_2_
  39.6 0.0 collective-permute-done.2.refs_3_
  39.7 3.9 %collective-permute-start.3 = (bf16[64,3072]{1,0:T(8,128)(2,1)S(1)}, bf16[64,3072]{1,0:T(8,128)(2,1)S(1)}, u32[]{:S(2)}, u32[]{:S(2)}) collective-permute-start(bf16[64,3072]{1,0:T(8,128)(2,1)S(1)} %shard_map.48.refs_0_), channel_id=1, source_target_pairs={{0,1},{1,2},{2,3},{3,0},{4,5},{5,6},{6,7},{7,4},{8,9},{9,10},{10,1... | collective-permute-start | bytes 1179656 | tf_op jit(solution)/shard_map/ppermute | solution.py:24
  43.6 1.9 %collective-permute-start.4 = (bf16[64,3072]{1,0:T(8,128)(2,1)S(1)}, bf16[64,3072]{1,0:T(8,128)(2,1)S(1)}, u32[]{:S(2)}, u32[]{:S(2)}) collective-permute-start(bf16[64,3072]{1,0:T(8,128)(2,1)S(1)} %shard_map.48.refs_0_), channel_id=1, source_target_pairs={{0,3},{1,0},{2,1},{3,2},{4,7},{5,4},{6,5},{7,6},{8,11},{9,8},{10,9... | collective-permute-start | bytes 1179656 | tf_op jit(solution)/shard_map/ppermute | solution.py:24
  45.5 5.5 %collective-permute-done.3.refs_1_ = bf16[64,3072]{1,0:T(8,128)(2,1)S(1)} collective-permute-done((bf16[64,3072]{1,0:T(8,128)(2,1)S(1)}, bf16[64,3072]{1,0:T(8,128)(2,1)S(1)}, u32[]{:S(2)}, u32[]{:S(2)}) %collective-permute-start.3) | collective-permute-done | bytes 393248 | tf_op jit(solution)/shard_map/ppermute | solution.py:24
  51.0 4.8 %collective-permute-start.7 = (bf16[64,3072]{1,0:T(8,128)(2,1)S(1)}, bf16[64,3072]{1,0:T(8,128)(2,1)S(1)}, u32[]{:S(2)}, u32[]{:S(2)}) collective-permute-start(bf16[64,3072]{1,0:T(8,128)(2,1)S(1)} %collective-permute-done.3.refs_1_), channel_id=1, source_target_pairs={{0,1},{1,2},{2,3},{3,0},{4,5},{5,6},{6,7},{7,4},{8,9},{9,10},{10,1... | collective-permute-start | bytes 1179656 | tf_op jit(solution)/shard_map/ppermute | solution.py:24
  55.9 0.0 collective-permute-done.4.refs_2_
  55.9 0.0 copy-done.1
  55.9 0.0 copy-done.3
  55.9 2.4 %shard_map.49 = (bf16[64,3072]{1,0:T(8,128)(2,1)S(1)}, bf16[64,3072]{1,0:T(8,128)(2,1)S(1)}, bf16[64,3072]{1,0:T(8,128)(2,1)S(1)}) custom-call(bf16[64,3072]{1,0:T(8,128)(2,1)S(1)} %shard_map.48.refs_0_, bf16[64,3072]{1,0:T(8,128)(2,1)S(1)} %collective-permute-done.3.refs_1_, bf16[64,3072]{1,0:T(8,128)(2,1)S(1)} %collective-permute-done.4.refs_2_, ...), custom_call_target="tpu_custom_call" | custom-call | flops 1811939328 | bytes 11798528 | tf_op jit(solution)/shard_map/pallas_call | solution.py:31
  58.4 1.9 %collective-permute-start.5 = (bf16[64,3072]{1,0:T(8,128)(2,1)S(1)}, bf16[64,3072]{1,0:T(8,128)(2,1)S(1)}, u32[]{:S(2)}, u32[]{:S(2)}) collective-permute-start(bf16[64,3072]{1,0:T(8,128)(2,1)S(1)} %get-tuple-element.13), channel_id=1, source_target_pairs={{0,3},{1,0},{2,1},{3,2},{4,7},{5,4},{6,5},{7,6},{8,11},{9,8},{10,9... | collective-permute-start | bytes 1179656 | tf_op jit(solution)/shard_map/ppermute | solution.py:24
  60.3 4.6 %collective-permute-start.6 = (bf16[64,3072]{1,0:T(8,128)(2,1)S(1)}, bf16[64,3072]{1,0:T(8,128)(2,1)S(1)}, u32[]{:S(2)}, u32[]{:S(2)}) collective-permute-start(bf16[64,3072]{1,0:T(8,128)(2,1)S(1)} %get-tuple-element.14), channel_id=1, source_target_pairs={{0,1},{1,2},{2,3},{3,0},{4,5},{5,6},{6,7},{7,4},{8,9},{9,10},{10,1... | collective-permute-start | bytes 1179656 | tf_op jit(solution)/shard_map/ppermute | solution.py:24
  64.9 0.0 collective-permute-done.7.refs_0_
  64.9 0.0 copy-start.5
  64.9 2.0 %shard_map.50 = bf16[64,3072]{1,0:T(8,128)(2,1)S(1)} custom-call(bf16[64,3072]{1,0:T(8,128)(2,1)S(1)} %collective-permute-done.7.refs_0_, bf16[3072,768]{1,0:T(8,128)(2,1)S(1)} %copy-done.1, bf16[768,3072]{1,0:T(8,128)(2,1)S(1)} %copy-done.3, bf16[64,3072]{1,0:T(8,128)(2,1)S(1)} %get-tuple-element.12.refs_3_.refs_0_), custom_call_target="tpu_custom_call" | custom-call | flops 603979776 | bytes 10616832 | tf_op jit(solution)/shard_map/pallas_call | solution.py:31
  66.9 1.9 %collective-permute-start.8 = (bf16[64,3072]{1,0:T(8,128)(2,1)S(1)}, bf16[64,3072]{1,0:T(8,128)(2,1)S(1)}, u32[]{:S(2)}, u32[]{:S(2)}) collective-permute-start(bf16[64,3072]{1,0:T(8,128)(2,1)S(1)} %shard_map.50), channel_id=1, source_target_pairs={{0,2},{1,3},{2,0},{3,1},{4,6},{5,7},{6,4},{7,5},{8,10},{9,11},{10,... | collective-permute-start | bytes 1179656 | tf_op jit(solution)/shard_map/ppermute | solution.py:24
  68.8 0.6 collective-permute-done.5.refs_1_
  69.5 9.0 %collective-permute-done.6.refs_2_ = bf16[64,3072]{1,0:T(8,128)(2,1)S(1)} collective-permute-done((bf16[64,3072]{1,0:T(8,128)(2,1)S(1)}, bf16[64,3072]{1,0:T(8,128)(2,1)S(1)}, u32[]{:S(2)}, u32[]{:S(2)}) %collective-permute-start.6) | collective-permute-done | bytes 393248 | tf_op jit(solution)/shard_map/ppermute | solution.py:24
  78.5 1.3 %collective-permute-done.8.refs_3_ = bf16[64,3072]{1,0:T(8,128)(2,1)S(1)} collective-permute-done((bf16[64,3072]{1,0:T(8,128)(2,1)S(1)}, bf16[64,3072]{1,0:T(8,128)(2,1)S(1)}, u32[]{:S(2)}, u32[]{:S(2)}) %collective-permute-start.8) | collective-permute-done | bytes 393248 | tf_op jit(solution)/shard_map/ppermute | solution.py:24
  79.7 0.2 shard_map.51
  79.9 5.7 %collective-permute-start.9 = (bf16[16,3072]{1,0:T(8,128)(2,1)S(1)}, bf16[16,3072]{1,0:T(8,128)(2,1)S(1)}, u32[]{:S(2)}, u32[]{:S(2)}) collective-permute-start(bf16[16,3072]{1,0:T(8,128)(2,1)S(1)} %get-tuple-element.16), channel_id=1, source_target_pairs={{0,8},{1,9},{2,10},{3,11},{4,12},{5,13},{6,14},{7,15},{8,0},{9,1},... | collective-permute-start | bytes 294920 | tf_op jit(solution)/shard_map/ppermute | solution.py:24
  85.6 9.8 %collective-permute-start.10 = (bf16[16,3072]{1,0:T(8,128)(2,1)S(1)}, bf16[16,3072]{1,0:T(8,128)(2,1)S(1)}, u32[]{:S(2)}, u32[]{:S(2)}) collective-permute-start(bf16[16,3072]{1,0:T(8,128)(2,1)S(1)} %get-tuple-element.17), channel_id=1, source_target_pairs={{0,12},{1,13},{2,14},{3,15},{4,0},{5,1},{6,2},{7,3},{8,4},{9,5},{1... | collective-permute-start | bytes 294920 | tf_op jit(solution)/shard_map/ppermute | solution.py:24
  95.5 1.9 %collective-permute-start.11 = (bf16[16,3072]{1,0:T(8,128)(2,1)S(1)}, bf16[16,3072]{1,0:T(8,128)(2,1)S(1)}, u32[]{:S(2)}, u32[]{:S(2)}) collective-permute-start(bf16[16,3072]{1,0:T(8,128)(2,1)S(1)} %get-tuple-element.18), channel_id=1, source_target_pairs={{0,4},{1,5},{2,6},{3,7},{4,8},{5,9},{6,10},{7,11},{8,12},{9,13},{1... | collective-permute-start | bytes 294920 | tf_op jit(solution)/shard_map/ppermute | solution.py:24
  97.4 0.0 collective-permute-done.9.refs_2_
  97.4 2.4 %collective-permute-done.10.refs_3_ = bf16[16,3072]{1,0:T(8,128)(2,1)S(1)} collective-permute-done((bf16[16,3072]{1,0:T(8,128)(2,1)S(1)}, bf16[16,3072]{1,0:T(8,128)(2,1)S(1)}, u32[]{:S(2)}, u32[]{:S(2)}) %collective-permute-start.10) | collective-permute-done | bytes 98336 | tf_op jit(solution)/shard_map/ppermute | solution.py:24
  99.8 7.4 %collective-permute-done.11.refs_4_ = bf16[16,3072]{1,0:T(8,128)(2,1)S(1)} collective-permute-done((bf16[16,3072]{1,0:T(8,128)(2,1)S(1)}, bf16[16,3072]{1,0:T(8,128)(2,1)S(1)}, u32[]{:S(2)}, u32[]{:S(2)}) %collective-permute-start.11) | collective-permute-done | bytes 98336 | tf_op jit(solution)/shard_map/ppermute | solution.py:24
  107.2 0.0 copy-done.5
  107.2 0.7 shard_map.52
  (2 shorter events, 0.0 us)
Async XLA Ops:
  1.8 20.7 %collective-permute-start = (bf16[16,3072]{1,0:T(8,128)(2,1)}, bf16[16,3072]{1,0:T(8,128)(2,1)S(1)}, u32[]{:S(2)}, u32[]{:S(2)}) collective-permute-start(bf16[16,3072]{1,0:T(8,128)(2,1)} %shard_map.46.after.refs_0_), channel_id=1, source_target_pairs={{0,4},{1,5},{2,6},{3,7},{4,8},{5,9},{6,10},{7,11},{8,12},{9,13},{1... | collective-permute-start | bytes 294920 | tf_op jit(solution)/shard_map/ppermute | solution.py:24
  20.5 19.1 %collective-permute-start.1 = (bf16[16,3072]{1,0:T(8,128)(2,1)}, bf16[16,3072]{1,0:T(8,128)(2,1)S(1)}, u32[]{:S(2)}, u32[]{:S(2)}) collective-permute-start(bf16[16,3072]{1,0:T(8,128)(2,1)} %shard_map.46.after.refs_0_), channel_id=1, source_target_pairs={{0,12},{1,13},{2,14},{3,15},{4,0},{5,1},{6,2},{7,3},{8,4},{9,5},{1... | collective-permute-start | bytes 294920 | tf_op jit(solution)/shard_map/ppermute | solution.py:24
  22.5 17.2 %collective-permute-start.2 = (bf16[16,3072]{1,0:T(8,128)(2,1)S(1)}, bf16[16,3072]{1,0:T(8,128)(2,1)S(1)}, u32[]{:S(2)}, u32[]{:S(2)}) collective-permute-start(bf16[16,3072]{1,0:T(8,128)(2,1)S(1)} %collective-permute-done.refs_1_), channel_id=1, source_target_pairs={{0,4},{1,5},{2,6},{3,7},{4,8},{5,9},{6,10},{7,11},{8,12},{9,13},{1... | collective-permute-start | bytes 294920 | tf_op jit(solution)/shard_map/ppermute | solution.py:24
  34.1 2.3 %copy-start = (bf16[3072,768]{1,0:T(8,128)(2,1)S(1)}, bf16[3072,768]{1,0:T(8,128)(2,1)}, u32[]{:S(2)}) copy-start(bf16[3072,768]{1,0:T(8,128)(2,1)} %refs_1_.1) | copy-start | bytes 14155780
  36.4 2.3 %copy-start.2 = (bf16[768,3072]{1,0:T(8,128)(2,1)S(1)}, bf16[768,3072]{1,0:T(8,128)(2,1)}, u32[]{:S(2)}) copy-start(bf16[768,3072]{1,0:T(8,128)(2,1)} %refs_2_.1) | copy-start | bytes 14155780
  38.7 0.9 copy-start.4
  39.6 16.3 %copy-start.1 = (bf16[3072,768]{1,0:T(8,128)(2,1)S(1)}, bf16[3072,768]{1,0:T(8,128)(2,1)}, u32[]{:S(2)}) copy-start(bf16[3072,768]{1,0:T(8,128)(2,1)} %refs_1_.1) | copy-start | bytes 14155780
  39.6 16.3 %copy-start.3 = (bf16[768,3072]{1,0:T(8,128)(2,1)S(1)}, bf16[768,3072]{1,0:T(8,128)(2,1)}, u32[]{:S(2)}) copy-start(bf16[768,3072]{1,0:T(8,128)(2,1)} %refs_2_.1) | copy-start | bytes 14155780
  39.7 11.4 %collective-permute-start.3 = (bf16[64,3072]{1,0:T(8,128)(2,1)S(1)}, bf16[64,3072]{1,0:T(8,128)(2,1)S(1)}, u32[]{:S(2)}, u32[]{:S(2)}) collective-permute-start(bf16[64,3072]{1,0:T(8,128)(2,1)S(1)} %shard_map.48.refs_0_), channel_id=1, source_target_pairs={{0,1},{1,2},{2,3},{3,0},{4,5},{5,6},{6,7},{7,4},{8,9},{9,10},{10,1... | collective-permute-start | bytes 1179656 | tf_op jit(solution)/shard_map/ppermute | solution.py:24
  43.6 12.3 %collective-permute-start.4 = (bf16[64,3072]{1,0:T(8,128)(2,1)S(1)}, bf16[64,3072]{1,0:T(8,128)(2,1)S(1)}, u32[]{:S(2)}, u32[]{:S(2)}) collective-permute-start(bf16[64,3072]{1,0:T(8,128)(2,1)S(1)} %shard_map.48.refs_0_), channel_id=1, source_target_pairs={{0,3},{1,0},{2,1},{3,2},{4,7},{5,4},{6,5},{7,6},{8,11},{9,8},{10,9... | collective-permute-start | bytes 1179656 | tf_op jit(solution)/shard_map/ppermute | solution.py:24
  51.0 13.8 %collective-permute-start.7 = (bf16[64,3072]{1,0:T(8,128)(2,1)S(1)}, bf16[64,3072]{1,0:T(8,128)(2,1)S(1)}, u32[]{:S(2)}, u32[]{:S(2)}) collective-permute-start(bf16[64,3072]{1,0:T(8,128)(2,1)S(1)} %collective-permute-done.3.refs_1_), channel_id=1, source_target_pairs={{0,1},{1,2},{2,3},{3,0},{4,5},{5,6},{6,7},{7,4},{8,9},{9,10},{10,1... | collective-permute-start | bytes 1179656 | tf_op jit(solution)/shard_map/ppermute | solution.py:24
  58.4 11.1 %collective-permute-start.5 = (bf16[64,3072]{1,0:T(8,128)(2,1)S(1)}, bf16[64,3072]{1,0:T(8,128)(2,1)S(1)}, u32[]{:S(2)}, u32[]{:S(2)}) collective-permute-start(bf16[64,3072]{1,0:T(8,128)(2,1)S(1)} %get-tuple-element.13), channel_id=1, source_target_pairs={{0,3},{1,0},{2,1},{3,2},{4,7},{5,4},{6,5},{7,6},{8,11},{9,8},{10,9... | collective-permute-start | bytes 1179656 | tf_op jit(solution)/shard_map/ppermute | solution.py:24
  60.3 18.2 %collective-permute-start.6 = (bf16[64,3072]{1,0:T(8,128)(2,1)S(1)}, bf16[64,3072]{1,0:T(8,128)(2,1)S(1)}, u32[]{:S(2)}, u32[]{:S(2)}) collective-permute-start(bf16[64,3072]{1,0:T(8,128)(2,1)S(1)} %get-tuple-element.14), channel_id=1, source_target_pairs={{0,1},{1,2},{2,3},{3,0},{4,5},{5,6},{6,7},{7,4},{8,9},{9,10},{10,1... | collective-permute-start | bytes 1179656 | tf_op jit(solution)/shard_map/ppermute | solution.py:24
  64.9 42.3 %copy-start.5 = (bf16[16,3072]{1,0:T(8,128)(2,1)S(1)}, bf16[16,3072]{1,0:T(8,128)(2,1)}, u32[]{:S(2)}) copy-start(bf16[16,3072]{1,0:T(8,128)(2,1)} %refs_0_.1) | copy-start | bytes 294916
  66.9 12.8 %collective-permute-start.8 = (bf16[64,3072]{1,0:T(8,128)(2,1)S(1)}, bf16[64,3072]{1,0:T(8,128)(2,1)S(1)}, u32[]{:S(2)}, u32[]{:S(2)}) collective-permute-start(bf16[64,3072]{1,0:T(8,128)(2,1)S(1)} %shard_map.50), channel_id=1, source_target_pairs={{0,2},{1,3},{2,0},{3,1},{4,6},{5,7},{6,4},{7,5},{8,10},{9,11},{10,... | collective-permute-start | bytes 1179656 | tf_op jit(solution)/shard_map/ppermute | solution.py:24
  79.9 17.5 %collective-permute-start.9 = (bf16[16,3072]{1,0:T(8,128)(2,1)S(1)}, bf16[16,3072]{1,0:T(8,128)(2,1)S(1)}, u32[]{:S(2)}, u32[]{:S(2)}) collective-permute-start(bf16[16,3072]{1,0:T(8,128)(2,1)S(1)} %get-tuple-element.16), channel_id=1, source_target_pairs={{0,8},{1,9},{2,10},{3,11},{4,12},{5,13},{6,14},{7,15},{8,0},{9,1},... | collective-permute-start | bytes 294920 | tf_op jit(solution)/shard_map/ppermute | solution.py:24
  85.6 14.2 %collective-permute-start.10 = (bf16[16,3072]{1,0:T(8,128)(2,1)S(1)}, bf16[16,3072]{1,0:T(8,128)(2,1)S(1)}, u32[]{:S(2)}, u32[]{:S(2)}) collective-permute-start(bf16[16,3072]{1,0:T(8,128)(2,1)S(1)} %get-tuple-element.17), channel_id=1, source_target_pairs={{0,12},{1,13},{2,14},{3,15},{4,0},{5,1},{6,2},{7,3},{8,4},{9,5},{1... | collective-permute-start | bytes 294920 | tf_op jit(solution)/shard_map/ppermute | solution.py:24
  95.5 11.7 %collective-permute-start.11 = (bf16[16,3072]{1,0:T(8,128)(2,1)S(1)}, bf16[16,3072]{1,0:T(8,128)(2,1)S(1)}, u32[]{:S(2)}, u32[]{:S(2)}) collective-permute-start(bf16[16,3072]{1,0:T(8,128)(2,1)S(1)} %get-tuple-element.18), channel_id=1, source_target_pairs={{0,4},{1,5},{2,6},{3,7},{4,8},{5,9},{6,10},{7,11},{8,12},{9,13},{1... | collective-permute-start | bytes 294920 | tf_op jit(solution)/shard_map/ppermute | solution.py:24
